TPU v7x, 32 devices: a whole 2x2x4 slice. The times are simulated.
32 devices in a mesh: section: 2 (over core), dp: 4 (over y, x), tensor: 4 (over z).
Axes of the slice: x: 2, y: 2, z: 4, core: 2. Of those that a mesh axis runs over, the one named last changes fastest.
Arguments:
- tokens_in: bfloat16 [2, 1024, 1536], P(None, ('dp', 'tensor')), may hold values from -6 to 6
- out_cotangent: bfloat16 [2, 1024, 1536], P(None, ('dp', 'tensor')), may hold values from -6 to 6
- attn_gain: float32 [2, 1536], P('section'), may hold values from 0.25 to 1.75
- query_weight: bfloat16 [2, 1536, 1536], P('section', None, 'tensor'), may hold values from -0.15625 to 0.15625
- key_weight: bfloat16 [2, 1536, 512], P('section', None, 'tensor'), may hold values from -0.15625 to 0.15625
- value_weight: bfloat16 [2, 1536, 512], P('section', None, 'tensor'), may hold values from -0.15625 to 0.15625
- output_weight: bfloat16 [2, 1536, 1536], P('section', 'tensor'), may hold values from -1.25 to 1.25
- expert_gain: float32 [2, 1536], P('section'), may hold values from 0.25 to 1.75
- router_weight: bfloat16 [2, 1536, 16], P('section'), may hold values from -0.078125 to 0.078125
- gate_weight: bfloat16 [2, 16, 1536, 512], P('section', None, None, 'tensor'), may hold values from -0.15625 to 0.15625
- up_weight: bfloat16 [2, 16, 1536, 512], P('section', None, None, 'tensor'), may hold values from -0.15625 to 0.15625
- down_weight: bfloat16 [2, 16, 512, 1536], P('section', None, 'tensor'), may hold values from -1.5 to 1.5
- lengths: int32 [2, 4, 3], P(None, 'dp'), may hold values from 1 to 192, 256 in all within a row
- dealing: int32 [2, 4, 3], P(None, 'dp'), may hold values from 0 to 2, each once within a row
- slot_order: int32 [2, 2, 4, 256], P('section', None, 'dp'), may hold values from 0 to 255, each once within a row
- routes: int32 [2, 2, 1024, 8], P('section', None, 'dp'), may hold values from 0 to 15, all different within a row
Outputs:
- layer_outputs: float32 [2, 2, 1024, 1536], P('section', None, ('dp', 'tensor'))
- input_grads: float32 [2, 2, 1024, 1536], P('section', None, ('dp', 'tensor'))
- attn_gain_grad: float32 [2, 1536], P('section')
- query_weight_grad: float32 [2, 1536, 1536], P('section', None, 'tensor')
- key_weight_grad: float32 [2, 1536, 512], P('section', None, 'tensor')
- value_weight_grad: float32 [2, 1536, 512], P('section', None, 'tensor')
- output_weight_grad: float32 [2, 1536, 1536], P('section', 'tensor')
- expert_gain_grad: float32 [2, 1536], P('section')
- router_weight_grad: float32 [2, 1536, 16], P('section')
- gate_weight_grad: float32 [2, 16, 1536, 512], P('section', 'dp', None, 'tensor')
- up_weight_grad: float32 [2, 16, 1536, 512], P('section', 'dp', None, 'tensor')
- down_weight_grad: float32 [2, 16, 512, 1536], P('section', 'dp', 'tensor')
Inputs may be any that keep to these rules, and one draw needn't show every extreme that they name: `lengths`: each row sums to 256; its largest entry is 192. `dealing`: each row is a permutation. `slot_order`: each row is a permutation. `routes`: the 8 entries of a row are different.
All inputs are finite; a program needn't handle non-finite values.
Results may differ from a plain program's by a relative error of at most 0.03.
Values may be sent and summed in bfloat16 or wider, within the bound.
A program may use at most 320 MiB of HBM per device.

v0:
```python
import jax
import jax.numpy as jnp
from jax import lax
from jax.sharding import PartitionSpec as P

H = 24
KV = 8
HD = 64
E = 16
CAP = 160


epsilon = 1e-05
rope_base = 10000.0
masked_score = -1e30
highest = lax.Precision.HIGHEST


def shifted(value, axis, steps):
    count = lax.axis_size(axis)
    initial, last = (max(0, -steps), min(count, count - steps))
    return lax.ppermute(value, axis, [(source, source + steps) for source in range(initial, last)])


def rms_scale(stream, gain):
    return stream * lax.rsqrt(jnp.mean(stream * stream, axis=-1, keepdims=True) + epsilon) * gain


def rotate_half(rows_in):
    half_width = rows_in.shape[-1] // 2
    return jnp.concatenate([-rows_in[..., half_width:], rows_in[..., :half_width]], axis=-1)


def rope_tables(position, head_dim):
    half_width = head_dim // 2
    freqs = rope_base ** (-2.0 * jnp.arange(half_width, dtype=jnp.float32) / head_dim)
    angles = position.astype(jnp.float32)[:, None] * freqs[None, :]
    return (
        jnp.concatenate([jnp.cos(angles)] * 2, axis=1),
        jnp.concatenate([jnp.sin(angles)] * 2, axis=1),
    )


def rope_apply(rows_in, cosine_table, sine_table):
    return rows_in * cosine_table[:, None, :] + rotate_half(rows_in) * sine_table[:, None, :]


def rope_reverse(rows_in, cosine_table, sine_table):
    return rows_in * cosine_table[:, None, :] - rotate_half(rows_in) * sine_table[:, None, :]


def pack_layout(lengths, dealing, order, routes, experts, capacity):
    tokens_pack = order.shape[0]
    seq_count = lengths.shape[0]
    top_count = routes.shape[1]
    token_index = jnp.arange(tokens_pack, dtype=jnp.int32)
    seq_index = jnp.arange(seq_count, dtype=jnp.int32)
    seq_ends = jnp.cumsum(lengths)
    seq_starts = seq_ends - lengths
    segment = jnp.sum((token_index[:, None] >= seq_ends[None, :]).astype(jnp.int32), axis=1)
    seg_onehot = (segment[:, None] == seq_index[None, :]).astype(jnp.int32)
    position = token_index - jnp.sum(seg_onehot * seq_starts[None, :], axis=1)
    dealt_rank = jnp.sum(
        jnp.where(dealing[:, None] == seq_index[None, :], seq_index[:, None], 0), axis=0
    )
    dealt_start = jnp.sum(
        jnp.where(dealt_rank[:, None] < dealt_rank[None, :], lengths[:, None], 0), axis=0
    )
    dealt_place = jnp.sum(seg_onehot * dealt_start[None, :], axis=1) + position
    priority = order[dealt_place]
    served = jnp.zeros((tokens_pack,), jnp.int32).at[priority].set(token_index)
    expert_index = jnp.arange(experts, dtype=jnp.int32)
    picked = jnp.sum((routes[:, :, None] == expert_index[None, None, :]).astype(jnp.int32), axis=1)
    ordered = picked[served]
    earlier = jnp.cumsum(ordered, axis=0) - ordered
    slot_rank = jnp.take_along_axis(earlier[priority], routes, axis=1)
    slot_id = jnp.where(slot_rank < capacity, routes * capacity + slot_rank, experts * capacity)
    slot_token = (
        jnp.full((experts * capacity + 1,), tokens_pack, jnp.int32)
        .at[slot_id.reshape(-1)]
        .set(jnp.repeat(token_index, top_count))
    )
    return (segment, position, slot_id, slot_token[: experts * capacity])


def select_layout(lengths, dealing, slot_order, routes, micro_index):
    length_row = lax.dynamic_index_in_dim(lengths, micro_index, 0, keepdims=False)[0]
    deal_row = lax.dynamic_index_in_dim(dealing, micro_index, 0, keepdims=False)[0]
    order_row = lax.dynamic_index_in_dim(slot_order[0], micro_index, 0, keepdims=False)[0]
    route_rows = lax.dynamic_index_in_dim(routes[0], micro_index, 0, keepdims=False)
    segment, position, slot_id, slot_token = pack_layout(
        length_row, deal_row, order_row, route_rows, E, CAP
    )
    return (segment, position, slot_id, slot_token, route_rows)


def attention_mask(segment):
    token_index = jnp.arange(segment.shape[0], dtype=jnp.int32)
    return (segment[:, None] == segment[None, :]) & (token_index[None, :] <= token_index[:, None])


def gate_softmax(logits, route_rows):
    return jax.nn.softmax(jnp.take_along_axis(logits, route_rows, axis=1), axis=-1)


def swiglu(gate_pre, up_pre):
    return jax.nn.silu(gate_pre) * up_pre


def slot_rows(expert_input, slot_token):
    padded = jnp.concatenate(
        [expert_input, jnp.zeros((1, expert_input.shape[1]), expert_input.dtype)], axis=0
    )
    return padded[slot_token].reshape(E, CAP, expert_input.shape[1])


def layer_forward(weights, stream, layout):
    (
        attn_gain,
        joint_weight,
        output_weight,
        expert_gain,
        router_weight,
        gate_weight,
        up_weight,
        down_weight,
    ) = weights
    segment, position, slot_id, slot_token, route_rows = layout
    tokens_pack = segment.shape[0]
    tensor_size = lax.axis_size("tensor")
    heads_local = H // tensor_size
    key_heads = KV // tensor_size
    group_size = H // KV
    query_width = heads_local * HD
    key_width = key_heads * HD
    attn_in = rms_scale(stream, attn_gain).astype(jnp.bfloat16)
    projected = jnp.dot(
        lax.all_gather(attn_in, "tensor", axis=0, tiled=True),
        joint_weight,
        preferred_element_type=jnp.float32,
    )
    cosine_table, sine_table = rope_tables(position, HD)
    queries = rope_apply(
        projected[:, :query_width].reshape(tokens_pack, heads_local, HD), cosine_table, sine_table
    ).astype(jnp.bfloat16)
    keys_rot = rope_apply(
        projected[:, query_width : query_width + key_width].reshape(tokens_pack, key_heads, HD),
        cosine_table,
        sine_table,
    ).astype(jnp.bfloat16)
    value_rows = (
        projected[:, query_width + key_width :]
        .reshape(tokens_pack, key_heads, HD)
        .astype(jnp.bfloat16)
    )
    query_groups = queries.reshape(tokens_pack, key_heads, group_size, HD)
    allowed = attention_mask(segment)
    scores = (
        jnp.einsum("qgnd,kgd->gnqk", query_groups, keys_rot, preferred_element_type=jnp.float32)
        * 0.125
    )
    scores = jnp.where(allowed, scores, masked_score)
    row_max = jnp.max(scores, axis=-1, keepdims=True)
    exp_scores = jnp.exp(scores - row_max)
    row_total = jnp.sum(exp_scores, axis=-1, keepdims=True)
    soft_scores = exp_scores / row_total
    log_total = row_max + jnp.log(row_total)
    attended = jnp.einsum(
        "gnqk,kgd->qgnd",
        soft_scores.astype(jnp.bfloat16),
        value_rows,
        preferred_element_type=jnp.float32,
    )
    attended = attended.reshape(tokens_pack, query_width).astype(jnp.bfloat16)
    mid_stream = stream + lax.psum_scatter(
        jnp.dot(attended, output_weight, preferred_element_type=jnp.float32),
        "tensor",
        scatter_dimension=0,
        tiled=True,
    )
    expert_rows_in = rms_scale(mid_stream, expert_gain).astype(jnp.bfloat16)
    expert_input = lax.all_gather(expert_rows_in, "tensor", axis=0, tiled=True)
    logits = jnp.dot(expert_input, router_weight, preferred_element_type=jnp.float32)
    gate_weights = gate_softmax(logits, route_rows)
    slot_in = slot_rows(expert_input, slot_token)
    gate_pre = jnp.einsum("ecd,edf->ecf", slot_in, gate_weight, preferred_element_type=jnp.float32)
    up_pre = jnp.einsum("ecd,edf->ecf", slot_in, up_weight, preferred_element_type=jnp.float32)
    hidden = swiglu(gate_pre, up_pre).astype(jnp.bfloat16)
    expert_out = jnp.einsum(
        "ecf,efd->ecd", hidden, down_weight, preferred_element_type=jnp.float32
    ).reshape(E * CAP, -1)
    expert_pad = jnp.concatenate(
        [expert_out, jnp.zeros((1, expert_out.shape[1]), jnp.float32)], axis=0
    )
    out_stream = mid_stream + lax.psum_scatter(
        jnp.einsum("tk,tkd->td", gate_weights, expert_pad[slot_id], precision=highest),
        "tensor",
        scatter_dimension=0,
        tiled=True,
    )
    kept_state = (
        stream,
        attn_in,
        mid_stream,
        queries,
        keys_rot,
        value_rows,
        log_total,
        attended,
        expert_input,
        gate_pre,
        up_pre,
        gate_weights,
    )
    return (out_stream, kept_state)


def layer_backward(weights, kept_state, layout, out_grad):
    (
        attn_gain,
        joint_weight,
        output_weight,
        expert_gain,
        router_weight,
        gate_weight,
        up_weight,
        down_weight,
    ) = weights
    segment, position, slot_id, slot_token, route_rows = layout
    (
        stream,
        attn_in,
        mid_stream,
        queries,
        keys_rot,
        value_rows,
        log_total,
        attended,
        expert_input,
        gate_pre,
        up_pre,
        gate_weights,
    ) = kept_state
    tokens_pack = segment.shape[0]
    rows_local = stream.shape[0]
    width = stream.shape[1]
    tensor_size = lax.axis_size("tensor")
    heads_local = H // tensor_size
    key_heads = KV // tensor_size
    group_size = H // KV
    query_width = heads_local * HD
    key_width = key_heads * HD
    grad_full = lax.all_gather(out_grad, "tensor", axis=0, tiled=True)
    hidden = swiglu(gate_pre, up_pre).astype(jnp.bfloat16)
    expert_out = jnp.einsum(
        "ecf,efd->ecd", hidden, down_weight, preferred_element_type=jnp.float32
    ).reshape(E * CAP, width)
    expert_pad = jnp.concatenate([expert_out, jnp.zeros((1, width), jnp.float32)], axis=0)
    slot_gate = (
        jnp.zeros((E * CAP + 1,), jnp.float32)
        .at[slot_id.reshape(-1)]
        .set(gate_weights.reshape(-1))[: E * CAP]
    )
    grad_pad = jnp.concatenate([grad_full, jnp.zeros((1, width), jnp.float32)], axis=0)
    slot_grad = (
        (slot_gate[:, None] * grad_pad[slot_token]).astype(jnp.bfloat16).reshape(E, CAP, width)
    )
    gate_grad_part = jnp.einsum("td,tkd->tk", grad_full, expert_pad[slot_id], precision=highest)
    down_grad = jnp.einsum("ecf,ecd->efd", hidden, slot_grad, preferred_element_type=jnp.float32)
    hidden_grad = jnp.einsum(
        "ecd,efd->ecf", slot_grad, down_weight, preferred_element_type=jnp.float32
    )
    swiglu_value, swiglu_pull = jax.vjp(swiglu, gate_pre, up_pre)
    gate_pre_grad, up_pre_grad = swiglu_pull(hidden_grad)
    gate_pre_grad = gate_pre_grad.astype(jnp.bfloat16)
    up_pre_grad = up_pre_grad.astype(jnp.bfloat16)
    slot_in = slot_rows(expert_input, slot_token)
    gate_grad = jnp.einsum(
        "ecd,ecf->edf", slot_in, gate_pre_grad, preferred_element_type=jnp.float32
    )
    up_grad = jnp.einsum("ecd,ecf->edf", slot_in, up_pre_grad, preferred_element_type=jnp.float32)
    slots_back = jnp.einsum(
        "ecf,edf->ecd", gate_pre_grad, gate_weight, preferred_element_type=jnp.float32
    )
    slots_back = slots_back + jnp.einsum(
        "ecf,edf->ecd", up_pre_grad, up_weight, preferred_element_type=jnp.float32
    )
    slots_back = jnp.concatenate(
        [slots_back.reshape(E * CAP, width), jnp.zeros((1, width), jnp.float32)], axis=0
    )
    expert_in_part = jnp.sum(slots_back[slot_id], axis=1)
    expert_in_grad, gate_grad_rows = (
        lax.psum_scatter(expert_in_part, "tensor", scatter_dimension=0, tiled=True),
        lax.psum_scatter(gate_grad_part, "tensor", scatter_dimension=0, tiled=True),
    )
    row_start = lax.axis_index("tensor") * rows_local
    expert_rows = lax.dynamic_slice_in_dim(expert_input, row_start, rows_local, 0)
    route_local = lax.dynamic_slice_in_dim(route_rows, row_start, rows_local, 0)
    logits_rows = jnp.dot(expert_rows, router_weight, preferred_element_type=jnp.float32)

    def gate_of(logit_rows):
        return gate_softmax(logit_rows, route_local)

    gate_value, gate_pull = jax.vjp(gate_of, logits_rows)
    logits_grad = gate_pull(gate_grad_rows)[0].astype(jnp.bfloat16)
    router_grad = jnp.einsum(
        "td,te->de", expert_rows, logits_grad, preferred_element_type=jnp.float32
    )
    expert_in_grad = expert_in_grad + jnp.einsum(
        "te,de->td", logits_grad, router_weight, preferred_element_type=jnp.float32
    )
    norm_value, norm_pull = jax.vjp(rms_scale, mid_stream, expert_gain)
    mid_part, expert_gain_grad = norm_pull(expert_in_grad)
    mid_grad = out_grad + mid_part
    attn_out_grad = lax.all_gather(mid_grad.astype(jnp.bfloat16), "tensor", axis=0, tiled=True)
    output_grad = jnp.einsum(
        "tq,td->qd", attended, attn_out_grad, preferred_element_type=jnp.float32
    )
    attended_grad = jnp.einsum(
        "td,qd->tq", attn_out_grad, output_weight, preferred_element_type=jnp.float32
    )
    attended_grad = attended_grad.astype(jnp.bfloat16).reshape(
        tokens_pack, key_heads, group_size, HD
    )
    query_groups = queries.reshape(tokens_pack, key_heads, group_size, HD)
    allowed = attention_mask(segment)
    scores = (
        jnp.einsum("qgnd,kgd->gnqk", query_groups, keys_rot, preferred_element_type=jnp.float32)
        * 0.125
    )
    soft_scores = jnp.exp(jnp.where(allowed, scores, masked_score) - log_total)
    soft_grad = jnp.einsum(
        "qgnd,kgd->gnqk", attended_grad, value_rows, preferred_element_type=jnp.float32
    )
    row_inner = jnp.sum(soft_scores * soft_grad, axis=-1, keepdims=True)
    score_grad = (soft_scores * (soft_grad - row_inner)).astype(jnp.bfloat16)
    value_grad = jnp.einsum(
        "gnqk,qgnd->kgd",
        soft_scores.astype(jnp.bfloat16),
        attended_grad,
        preferred_element_type=jnp.float32,
    )
    value_grad = value_grad.astype(jnp.bfloat16).reshape(tokens_pack, key_width)
    query_grad = (
        jnp.einsum("gnqk,kgd->qgnd", score_grad, keys_rot, preferred_element_type=jnp.float32)
        * 0.125
    )
    key_grad = (
        jnp.einsum("gnqk,qgnd->kgd", score_grad, query_groups, preferred_element_type=jnp.float32)
        * 0.125
    )
    cosine_table, sine_table = rope_tables(position, HD)
    query_grad = rope_reverse(
        query_grad.reshape(tokens_pack, heads_local, HD), cosine_table, sine_table
    )
    query_grad = query_grad.astype(jnp.bfloat16).reshape(tokens_pack, query_width)
    key_grad = (
        rope_reverse(key_grad, cosine_table, sine_table)
        .astype(jnp.bfloat16)
        .reshape(tokens_pack, key_width)
    )
    joint_rows = jnp.concatenate([query_grad, key_grad, value_grad], axis=1)
    attn_in_grad = lax.psum_scatter(
        jnp.einsum("tc,dc->td", joint_rows, joint_weight, preferred_element_type=jnp.float32),
        "tensor",
        scatter_dimension=0,
        tiled=True,
    )
    joint_grad = jnp.einsum(
        "td,tc->dc",
        lax.all_gather(attn_in, "tensor", axis=0, tiled=True),
        joint_rows,
        preferred_element_type=jnp.float32,
    )
    norm_again, attn_pull = jax.vjp(rms_scale, stream, attn_gain)
    stream_part, attn_gain_grad = attn_pull(attn_in_grad)
    stream_grad = mid_grad + stream_part
    return (
        stream_grad,
        (
            attn_gain_grad,
            joint_grad,
            output_grad,
            expert_gain_grad,
            router_grad,
            gate_grad,
            up_grad,
            down_grad,
        ),
    )


def reduce_experts(expert_parts):
    return (
        lax.psum_scatter(expert_parts[0], "dp", scatter_dimension=0, tiled=True),
        lax.psum_scatter(expert_parts[1], "dp", scatter_dimension=0, tiled=True),
        lax.psum_scatter(expert_parts[2], "dp", scatter_dimension=0, tiled=True),
    )


def shards(
    tokens_in,
    out_cotangent,
    attn_gain,
    query_weight,
    key_weight,
    value_weight,
    output_weight,
    expert_gain,
    router_weight,
    gate_weight,
    up_weight,
    down_weight,
    lengths,
    dealing,
    slot_order,
    routes,
):
    micro_count = tokens_in.shape[0]
    rows_local = tokens_in.shape[1]
    width = tokens_in.shape[2]
    section_index = lax.axis_index("section")
    on_first = section_index == 0
    query_width = query_weight.shape[2]
    key_width = key_weight.shape[2]
    joint_weight = jnp.concatenate([query_weight[0], key_weight[0], value_weight[0]], axis=1)
    weights = (
        attn_gain[0],
        joint_weight,
        output_weight[0],
        expert_gain[0],
        router_weight[0],
        gate_weight[0],
        up_weight[0],
        down_weight[0],
    )
    empty_rows = jnp.zeros((rows_local, width), jnp.bfloat16)
    received = empty_rows
    out_list = []
    kept_list = []
    layouts = []
    for micro_step in range(micro_count + 1):
        micro_index = jnp.clip(micro_step - section_index, 0, micro_count - 1)
        layout = select_layout(lengths, dealing, slot_order, routes, micro_index)
        if micro_step < micro_count:
            own_rows = tokens_in[micro_step]
        else:
            own_rows = empty_rows
        stream = jnp.where(on_first, own_rows, received).astype(jnp.float32)
        out_stream, kept_state = layer_forward(weights, stream, layout)
        out_list.append(out_stream)
        kept_list.append(kept_state)
        layouts.append(layout)
        if micro_step < micro_count:
            received = shifted(out_stream.astype(jnp.bfloat16), "section", 1)
    layer_outputs = jnp.stack(
        [
            jnp.where(on_first, out_list[micro_pos], out_list[micro_pos + 1])
            for micro_pos in range(micro_count)
        ]
    )[None]
    back_received = empty_rows
    dense_sums = None
    expert_sums = None
    returned_list = []
    for back_step in range(micro_count + 1):
        fwd_step = micro_count - back_step
        if back_step < micro_count:
            given_grad = out_cotangent[micro_count - 1 - back_step]
        else:
            given_grad = empty_rows
        incoming = jnp.where(on_first, back_received, given_grad).astype(jnp.float32)
        stream_grad, layer_grads = layer_backward(
            weights, kept_list[fwd_step], layouts[fwd_step], incoming
        )
        returned_list.append(stream_grad)
        if back_step < micro_count:
            back_received = shifted(stream_grad.astype(jnp.bfloat16), "section", -1)
        dense_part = layer_grads[:5]
        if dense_sums is None:
            dense_sums = dense_part
        else:
            dense_sums = tuple((running + added for running, added in zip(dense_sums, dense_part)))
        expert_part = layer_grads[5:]
        if expert_sums is None:
            expert_sums = expert_part
        else:
            expert_sums = tuple(
                (running + added for running, added in zip(expert_sums, expert_part))
            )
    expert_final = reduce_experts(expert_sums)
    input_grads = jnp.stack(
        [
            jnp.where(
                on_first,
                returned_list[micro_count - micro_pos],
                returned_list[micro_count - 1 - micro_pos],
            )
            for micro_pos in range(micro_count)
        ]
    )[None]
    attn_gain_sum, joint_sum, output_sum, expert_gain_sum, router_sum = dense_sums
    query_grad = joint_sum[:, :query_width]
    key_grad = joint_sum[:, query_width : query_width + key_width]
    value_grad = joint_sum[:, query_width + key_width :]
    query_grad, key_grad, value_grad, output_grad = lax.psum(
        (query_grad, key_grad, value_grad, output_sum), "dp"
    )
    attn_gain_total, expert_gain_total, router_total = lax.psum(
        (attn_gain_sum, expert_gain_sum, router_sum), ("dp", "tensor")
    )
    return (
        layer_outputs,
        input_grads,
        attn_gain_total[None],
        query_grad[None],
        key_grad[None],
        value_grad[None],
        output_grad[None],
        expert_gain_total[None],
        router_total[None],
        expert_final[0][None],
        expert_final[1][None],
        expert_final[2][None],
    )


def solution(mesh):
    return jax.shard_map(
        shards,
        mesh=mesh,
        in_specs=(
            P(None, ("dp", "tensor"), None),
            P(None, ("dp", "tensor"), None),
            P("section", None),
            P("section", None, "tensor"),
            P("section", None, "tensor"),
            P("section", None, "tensor"),
            P("section", "tensor", None),
            P("section", None),
            P("section", None, None),
            P("section", None, None, "tensor"),
            P("section", None, None, "tensor"),
            P("section", None, "tensor", None),
            P(None, "dp", None),
            P(None, "dp", None),
            P("section", None, "dp", None),
            P("section", None, "dp", None),
        ),
        out_specs=(
            P("section", None, ("dp", "tensor"), None),
            P("section", None, ("dp", "tensor"), None),
            P("section", None),
            P("section", None, "tensor"),
            P("section", None, "tensor"),
            P("section", None, "tensor"),
            P("section", "tensor", None),
            P("section", None),
            P("section", None, None),
            P("section", "dp", None, "tensor"),
            P("section", "dp", None, "tensor"),
            P("section", "dp", "tensor", None),
        ),
        check_vma=False,
    )
```

profile of v0, /device:TPU:0, one launch (start us, length us, event | category | flops | bytes accessed | tf_op | source)
XLA Modules:
  0.0 2018.2 jit_solution(8383258869526624983)
XLA Ops:
  10.8 21.3 %all_gather.39 = bf16[256,1536]{1,0:T(8,128)(2,1)S(1)} all-gather(bf16[64,1536]{1,0:T(8,128)(2,1)S(1)} %fusion.115), channel_id=1, replica_groups=mesh['section'=2,'dp'=4,'tensor'=4] {'tensor'}, dimensions={0}, use_global_device_ids=true | all-gather | bytes 983040 | tf_op jit(solution)/shard_map/all_gather | solution.py:138
  53.5 13.6 gather_fusion.22
  82.5 18.6 all_gather.40
  102.3 16.8 gather_fusion.21
  151.9 19.7 gather_fusion.4
  171.6 14.5 fusion.8
  194.0 13.6 gather_fusion.24
  226.9 18.4 all_gather.41
  258.6 13.6 gather_fusion.26
  288.7 18.4 all_gather.42
  339.7 16.8 gather_fusion.23
  368.4 19.7 gather_fusion.9
  388.1 14.5 fusion.4
  404.9 33.9 %reduce-scatter.25.cloned.1.call-done = f32[64,1536]{1,0:T(8,128)} async-done(((f32[256,1536]{1,0:T(8,128)}), f32[64,1536]{1,0:T(8,128)}) %reduce-scatter.25.cloned.1.call-update) | async-done | bytes 393232 | tf_op jit(solution)/shard_map/reduce_scatter | solution.py:195
  443.5 28.0 %all_gather.43 = bf16[256,1536]{1,0:T(8,128)(2,1)S(1)} all-gather(bf16[64,1536]{1,0:T(8,128)(2,1)S(1)} %fusion.117), channel_id=1, replica_groups=mesh['section'=2,'dp'=4,'tensor'=4] {'tensor'}, dimensions={0}, use_global_device_ids=true | all-gather | bytes 983040 | tf_op jit(solution)/shard_map/all_gather | solution.py:138
  499.0 24.8 %reduce-scatter.27.cloned.1.call-done = f32[64,1536]{1,0:T(8,128)} async-done(((f32[256,1536]{1,0:T(8,128)}), f32[64,1536]{1,0:T(8,128)}) %reduce-scatter.27.cloned.1.call-update) | async-done | bytes 393232 | tf_op jit(solution)/shard_map/reduce_scatter | solution.py:175
  525.1 18.2 all_gather.44
  567.0 16.8 gather_fusion.25
  615.5 19.9 gather_fusion.14
  635.4 29.1 %fusion.2 = f32[256,1,8]{2,1,0:T(1,128)} fusion(f32[2048,1536]{1,0:T(8,128)} %gather_fusion.14, f32[256,1536,1]{1,0,2:T(8,128)S(1)} %bitcast.681), kind=kOutput, calls=%fused_computation.50 | convolution fusion | flops 37748736 | bytes 14163968 | tf_op jit(solution)/shard_map/td,tkd->tk/dot_general | solution.py:268
  675.3 15.1 convolution_add_fusion.2
  701.6 19.8 gather_fusion.16
  738.7 25.2 %scatter_fusion = f32[64,16]{0,1:T(8,128)S(1)} fusion(f32[64,16]{0,1:T(8,128)S(1)} %broadcast_in_dim.180.clone, s32[512]{0:T(512)S(1)} %reshape.1200, f32[512]{0:T(512)S(1)} %reshape.1202), kind=kCustom, calls=%fused_computation.39 | custom fusion | flops 512 | bytes 10240 | tf_op jit(solution)/shard_map/transpose(jvp(jit(take_along_axis)))/scatter-add | solution.py:103
  768.8 18.6 all_gather.46
  796.3 14.3 fusion
  812.1 18.7 reduce-scatter.35.cloned.1.call-done
  832.5 35.4 %reduce-scatter.29.cloned.1.call-done = f32[64,1536]{1,0:T(8,128)} async-done(((f32[256,1536]{1,0:T(8,128)}), f32[64,1536]{1,0:T(8,128)}) %reduce-scatter.29.cloned.1.call-update) | async-done | bytes 393232 | tf_op jit(solution)/shard_map/reduce_scatter | solution.py:195
  883.0 27.6 %all-gather.5.cloned.1.call-done = f32[256,1536]{1,0:T(8,128)} async-done(((f32[64,1536]{1,0:T(8,128)}), f32[256,1536]{1,0:T(8,128)}) %all-gather.5.cloned.1.call-update) | async-done | bytes 1572880 | tf_op jit(solution)/shard_map/all_gather | solution.py:253
  922.4 25.3 %fusion.6 = f32[256,1,8]{2,1,0:T(1,128)} fusion(f32[2048,1536]{1,0:T(8,128)} %gather_fusion.9, f32[256,1536,1]{1,0,2:T(8,128)} %bitcast.683), kind=kOutput, calls=%fused_computation.54 | convolution fusion | flops 37748736 | bytes 14163968 | tf_op jit(solution)/shard_map/td,tkd->tk/dot_general | solution.py:268
  966.9 15.2 convolution_add_fusion.1
  993.4 19.7 gather_fusion.18
  1030.0 25.2 %scatter_fusion.1 = f32[64,16]{0,1:T(8,128)S(1)} fusion(f32[64,16]{0,1:T(8,128)S(1)} %broadcast_in_dim.180.clone.1, s32[512]{0:T(512)S(1)} %reshape.1206, f32[512]{0:T(512)S(1)} %reshape.1208), kind=kCustom, calls=%fused_computation.40 | custom fusion | flops 512 | bytes 10240 | tf_op jit(solution)/shard_map/transpose(jvp(jit(take_along_axis)))/scatter-add | solution.py:103
  1060.1 18.1 all_gather.48
  1085.5 34.7 %reduce-scatter.41.cloned.1.call-done = f32[64,1536]{1,0:T(8,128)} async-done(((f32[256,1536]{1,0:T(8,128)}), f32[64,1536]{1,0:T(8,128)}) %reduce-scatter.41.cloned.1.call-update) | async-done | bytes 393232 | tf_op jit(solution)/shard_map/reduce_scatter | solution.py:363
  1136.5 27.8 %all-gather.7.cloned.1.call-done = f32[256,1536]{1,0:T(8,128)} async-done(((f32[64,1536]{1,0:T(8,128)}), f32[256,1536]{1,0:T(8,128)}) %all-gather.7.cloned.1.call-update) | async-done | bytes 1572880 | tf_op jit(solution)/shard_map/all_gather | solution.py:253
  1176.2 25.3 %fusion.10 = f32[256,1,8]{2,1,0:T(1,128)} fusion(f32[2048,1536]{1,0:T(8,128)} %gather_fusion.4, f32[256,1536,1]{1,0,2:T(8,128)} %bitcast.682), kind=kOutput, calls=%fused_computation.58 | convolution fusion | flops 37748736 | bytes 14163968 | tf_op jit(solution)/shard_map/td,tkd->tk/dot_general | solution.py:268
  1220.7 15.1 convolution_add_fusion
  1247.1 19.7 gather_fusion.20
  1283.5 25.2 %scatter_fusion.2 = f32[64,16]{0,1:T(8,128)S(1)} fusion(f32[64,16]{0,1:T(8,128)S(1)} %broadcast_in_dim.180, s32[512]{0:T(512)S(1)} %reshape.1212, f32[512]{0:T(512)S(1)} %reshape.1214), kind=kCustom, calls=%fused_computation.41 | custom fusion | flops 512 | bytes 10240 | tf_op jit(solution)/shard_map/transpose(jvp(jit(take_along_axis)))/scatter-add | solution.py:103
  1312.1 18.3 all_gather.50
  1390.6 19.9 add_add_fusion
  1434.9 17.6 add_add_fusion.1
  1476.9 17.5 add_add_fusion.2
  1498.8 76.5 %all-reduce.12 = (f32[1,1536]{1,0:T(1,128)}, f32[1,1536]{1,0:T(1,128)}) all-reduce(f32[1,1536]{1,0:T(1,128)S(1)} %broadcast_in_dim.191, f32[1,1536]{1,0:T(1,128)S(1)} %broadcast_in_dim.196), channel_id=1, replica_groups=mesh['section'=2,'dp'=4,'tensor'=4] {'dp','tensor'}, use_global_device_ids=true, to_apply=%region_96.100 | all-reduce | flops 3072 | bytes 24576 | tf_op jit(solution)/shard_map/psum | solution.py:509
  1577.6 52.0 %all-reduce.19.cloned.1.call-done = (f32[1,1536,384]{2,1,0:T(8,128)}, f32[1,1536,128]{2,1,0:T(8,128)}, f32[1,1536,128]{2,1,0:T(8,128)}, f32[1,384,1536]{2,1,0:T(8,128)}) async-done(((f32[1,1536,384]{2,1,0:T(8,128)}, f32[1,1536,128]{2,1,0:T(8,128)}, f32[1,1536,128]{2,1,0:T(8,128)}, f32[1,384,1536]{2,1,0:T(8,128)}), (f32[1,1536,384]{2,1,0:T(8,128)}, f32[1,1536,128]{2,1,0:T(8,128)}, f32[1,1536,128]{2,1,0:T(8,128)}, ...) | async-done | bytes 6291472 | tf_op jit(solution)/shard_map/psum | solution.py:506
  1629.6 124.8 %reduce-scatter.53.cloned.1.call-done = f32[4,128,1536]{2,1,0:T(8,128)} async-done(((f32[16,128,1536]{2,1,0:T(8,128)}), f32[4,128,1536]{2,1,0:T(8,128)}) %reduce-scatter.53.cloned.1.call-update) | async-done | bytes 3145744 | tf_op jit(solution)/shard_map/reduce_scatter | solution.py:397
  1754.4 124.7 %reduce-scatter.51.cloned.1.call-done = f32[4,1536,128]{2,1,0:T(8,128)} async-done(((f32[16,1536,128]{2,1,0:T(8,128)}), f32[4,1536,128]{2,1,0:T(8,128)}) %reduce-scatter.51.cloned.1.call-update) | async-done | bytes 3145744 | tf_op jit(solution)/shard_map/reduce_scatter | solution.py:396
  1879.1 124.8 %reduce-scatter.49.cloned.1.call-done = f32[4,1536,128]{2,1,0:T(8,128)} async-done(((f32[16,1536,128]{2,1,0:T(8,128)}), f32[4,1536,128]{2,1,0:T(8,128)}) %reduce-scatter.49.cloned.1.call-update) | async-done | bytes 3145744 | tf_op jit(solution)/shard_map/reduce_scatter | solution.py:395
  (991 shorter events, 607.7 us)
Async XLA Ops:
  7.2 73.4 %reduce-scatter.19.cloned.1.call-start = ((), (), s32[]{:S(2)}) async-start(), calls=%async_computation.18 | async-start | bytes 1966080 | tf_op jit(solution)/shard_map/reduce_scatter | solution.py:175
  45.8 176.4 %reduce-scatter.21.cloned.1.call-start = ((), (), s32[]{:S(2)}) async-start(), calls=%async_computation.19 | async-start | bytes 1966080 | tf_op jit(solution)/shard_map/reduce_scatter | solution.py:195
  75.8 43.9 %copy-start.165 = (s32[3072]{0:T(1024)}, s32[3072]{0:T(1024)S(1)}, u32[]{:S(2)}) copy-start(s32[3072]{0:T(1024)S(1)} %pad_clamp_fusion.2) | copy-start | bytes 36868
  75.8 76.1 %copy-start.30 = (s32[2048]{0:T(1024)}, s32[2048]{0:T(1024)S(1)}, u32[]{:S(2)}) copy-start(s32[2048]{0:T(1024)S(1)} %broadcast_clamp_fusion.2) | copy-start | bytes 24580
  119.7 52.0 %copy-start.103 = (f32[256,8]{1,0:T(8,128)}, f32[256,8]{1,0:T(8,128)S(1)}, u32[]{:S(2)}) copy-start(f32[256,8]{1,0:T(8,128)S(1)} %fusion.182) | copy-start | bytes 24580
  187.4 99.5 %reduce-scatter.23.cloned.1.call-start = ((), (), s32[]{:S(2)}) async-start(), calls=%async_computation.20 | async-start | bytes 1966080 | tf_op jit(solution)/shard_map/reduce_scatter | solution.py:175
  208.6 43.8 %copy-start.137 = (s32[256,8]{0,1:T(8,128)}, s32[256,8]{0,1:T(8,128)S(1)}, u32[]{:S(2)}) copy-start(s32[256,8]{0,1:T(8,128)S(1)} %get-tuple-element.67) | copy-start | bytes 24580
  224.0 2.6 collective-permute-start
  226.8 60.2 %copy-start.50 = (bf16[64,1536]{1,0:T(8,128)(2,1)}, bf16[64,1536]{1,0:T(8,128)(2,1)S(1)}, u32[]{:S(2)}) copy-start(bf16[64,1536]{1,0:T(8,128)(2,1)S(1)} %get-tuple-element.80) | copy-start | bytes 589828
  252.3 186.5 %reduce-scatter.25.cloned.1.call-start = ((), (), s32[]{:S(2)}) async-start(), calls=%async_computation.21 | async-start | bytes 1966080 | tf_op jit(solution)/shard_map/reduce_scatter | solution.py:195
  281.0 87.4 %copy-start.32 = (s32[2048]{0:T(1024)}, s32[2048]{0:T(1024)S(1)}, u32[]{:S(2)}) copy-start(s32[2048]{0:T(1024)S(1)} %broadcast_clamp_fusion.1) | copy-start | bytes 24580
  288.1 150.7 %copy-start.20 = (f32[64,1536]{1,0:T(8,128)}, f32[64,1536]{1,0:T(8,128)S(1)}, u32[]{:S(2)}) copy-start(f32[64,1536]{1,0:T(8,128)S(1)} %get-tuple-element.76) | copy-start | bytes 1179652
  403.9 83.1 %all-gather.9.cloned.1.call-start = ((), (), s32[]{:S(2)}) async-start(), calls=%async_computation.39 | async-start | bytes 1966080 | tf_op jit(solution)/shard_map/all_gather | solution.py:253
  404.8 66.7 %copy-start.242 = (bf16[1,1536,128]{2,1,0:T(8,128)(2,1)S(1)}, bf16[1,1536,128]{2,1,0:T(8,128)(2,1)}, u32[]{:S(2)}) copy-start(bf16[1,1536,128]{2,1,0:T(8,128)(2,1)} %param.27) | copy-start | bytes 1179652
  404.8 66.7 %copy-start.246 = (bf16[1,1536,128]{2,1,0:T(8,128)(2,1)S(1)}, bf16[1,1536,128]{2,1,0:T(8,128)(2,1)}, u32[]{:S(2)}) copy-start(bf16[1,1536,128]{2,1,0:T(8,128)(2,1)} %param.26) | copy-start | bytes 1179652
  404.8 118.9 %reduce-scatter.27.cloned.1.call-start = ((), (), s32[]{:S(2)}) async-start(), calls=%async_computation.22 | async-start | bytes 1966080 | tf_op jit(solution)/shard_map/reduce_scatter | solution.py:175
  440.6 2.6 collective-permute-start.1
  443.2 80.5 %copy-start.52 = (bf16[64,1536]{1,0:T(8,128)(2,1)}, bf16[64,1536]{1,0:T(8,128)(2,1)S(1)}, u32[]{:S(2)}) copy-start(bf16[64,1536]{1,0:T(8,128)(2,1)S(1)} %collective-permute-done.1) | copy-start | bytes 589828
  478.3 258.4 %reduce-scatter.33.cloned.1.call-start = ((), (), s32[]{:S(2)}) async-start(), calls=%async_computation.25 | async-start | bytes 163840 | tf_op jit(solution)/shard_map/reduce_scatter | solution.py:294
  499.0 44.2 %copy-start.60 = (bf16[1,1536,16]{1,2,0:T(8,128)(2,1)S(1)}, bf16[1,1536,16]{1,2,0:T(8,128)(2,1)}, u32[]{:S(2)}) copy-start(bf16[1,1536,16]{1,2,0:T(8,128)(2,1)} %param.30) | copy-start | bytes 147460
  603.7 61.1 %copy-start.40 = (bf16[16,160,128]{2,1,0:T(8,128)(2,1)}, bf16[16,160,128]{2,1,0:T(8,128)(2,1)S(1)}, u32[]{:S(2)}) copy-start(bf16[16,160,128]{2,1,0:T(8,128)(2,1)S(1)} %get-tuple-element.97) | copy-start | bytes 1966084
  664.5 100.4 %reduce-scatter.31.cloned.1.call-start = ((), (), s32[]{:S(2)}) async-start(), calls=%async_computation.24 | async-start | bytes 1966080 | tf_op jit(solution)/shard_map/reduce_scatter | solution.py:293
  730.2 100.6 %reduce-scatter.35.cloned.1.call-start = ((), (), s32[]{:S(2)}) async-start(), calls=%async_computation.26 | async-start | bytes 1966080 | tf_op jit(solution)/shard_map/reduce_scatter | solution.py:363
  796.1 71.8 %reduce-scatter.29.cloned.1.call-start = ((), (), s32[]{:S(2)}) async-start(), calls=%async_computation.23 | async-start | bytes 1966080 | tf_op jit(solution)/shard_map/reduce_scatter | solution.py:195
  810.7 57.2 %copy-start.68 = (f32[64,1536]{1,0:T(8,128)S(1)}, f32[64,1536]{1,0:T(8,128)}, u32[]{:S(2)}) copy-start(f32[64,1536]{1,0:T(8,128)} %copy-done.67) | copy-start | bytes 1179652
  810.7 57.2 %copy-start.70 = (f32[64,1536]{1,0:T(8,128)S(1)}, f32[64,1536]{1,0:T(8,128)}, u32[]{:S(2)}) copy-start(f32[64,1536]{1,0:T(8,128)} %copy-done.69) | copy-start | bytes 1179652
  810.7 57.2 %copy-start.97 = (bf16[2,64,1536]{2,1,0:T(8,128)(2,1)S(1)}, bf16[2,64,1536]{2,1,0:T(8,128)(2,1)}, u32[]{:S(2)}) copy-start(bf16[2,64,1536]{2,1,0:T(8,128)(2,1)} %param.23) | copy-start | bytes 1179652
  812.0 98.6 %all-gather.5.cloned.1.call-start = ((), (), s32[]{:S(2)}) async-start(), calls=%async_computation.27 | async-start | bytes 1966080 | tf_op jit(solution)/shard_map/all_gather | solution.py:253
  870.1 3.5 collective-permute-start.2
  874.4 153.6 %reduce-scatter.39.cloned.1.call-start = ((), (), s32[]{:S(2)}) async-start(), calls=%async_computation.29 | async-start | bytes 163840 | tf_op jit(solution)/shard_map/reduce_scatter | solution.py:294
  883.0 64.8 %copy-start.161 = (f32[16,160]{1,0:T(8,128)}, f32[16,160]{1,0:T(8,128)S(1)}, u32[]{:S(2)}) copy-start(f32[16,160]{1,0:T(8,128)S(1)} %mul.1075) | copy-start | bytes 30724
  947.8 108.4 %reduce-scatter.37.cloned.1.call-start = ((), (), s32[]{:S(2)}) async-start(), calls=%async_computation.28 | async-start | bytes 1966080 | tf_op jit(solution)/shard_map/reduce_scatter | solution.py:293
  1021.8 98.3 %reduce-scatter.41.cloned.1.call-start = ((), (), s32[]{:S(2)}) async-start(), calls=%async_computation.30 | async-start | bytes 1966080 | tf_op jit(solution)/shard_map/reduce_scatter | solution.py:363
  1085.4 78.9 %all-gather.7.cloned.1.call-start = ((), (), s32[]{:S(2)}) async-start(), calls=%async_computation.31 | async-start | bytes 1966080 | tf_op jit(solution)/shard_map/all_gather | solution.py:253
  1123.8 3.5 collective-permute-start.3
  1128.1 153.4 %reduce-scatter.45.cloned.1.call-start = ((), (), s32[]{:S(2)}) async-start(), calls=%async_computation.33 | async-start | bytes 163840 | tf_op jit(solution)/shard_map/reduce_scatter | solution.py:294
  1201.5 108.3 %reduce-scatter.43.cloned.1.call-start = ((), (), s32[]{:S(2)}) async-start(), calls=%async_computation.32 | async-start | bytes 1966080 | tf_op jit(solution)/shard_map/reduce_scatter | solution.py:293
  1275.5 222.0 %reduce-scatter.47.cloned.1.call-start = ((), (), s32[]{:S(2)}) async-start(), calls=%async_computation.34 | async-start | bytes 1966080 | tf_op jit(solution)/shard_map/reduce_scatter | solution.py:363
  1340.8 236.8 %all-reduce.17.cloned.1.call-start = ((), (), s32[]{:S(2)}) async-start(), calls=%async_computation.35 | async-start | bytes 196608 | tf_op jit(solution)/shard_map/psum | solution.py:509
  1354.9 274.7 %all-reduce.19.cloned.1.call-start = ((), (), s32[]{:S(2)}) async-start(), calls=%async_computation.40 | async-start | bytes 12582912 | tf_op jit(solution)/shard_map/psum | solution.py:506
  1365.3 389.1 %reduce-scatter.53.cloned.1.call-start = ((), (), s32[]{:S(2)}) async-start(), calls=%async_computation.38 | async-start | bytes 15728640 | tf_op jit(solution)/shard_map/reduce_scatter | solution.py:397
  1410.6 468.5 %reduce-scatter.51.cloned.1.call-start = ((), (), s32[]{:S(2)}) async-start(), calls=%async_computation.37 | async-start | bytes 15728640 | tf_op jit(solution)/shard_map/reduce_scatter | solution.py:396
  1452.5 551.3 %reduce-scatter.49.cloned.1.call-start = ((), (), s32[]{:S(2)}) async-start(), calls=%async_computation.36 | async-start | bytes 15728640 | tf_op jit(solution)/shard_map/reduce_scatter | solution.py:395
  1494.5 80.8 %copy-start.230 = (f32[64]{0:T(128)S(1)}, f32[64]{0:T(128)}, u32[]{:S(2)}) copy-start(f32[64]{0:T(128)} %copy-done.229) | copy-start | bytes 772
  1494.5 80.8 %copy-start.206 = (f32[64]{0:T(128)S(1)}, f32[64]{0:T(128)}, u32[]{:S(2)}) copy-start(f32[64]{0:T(128)} %copy-done.204) | copy-start | bytes 772
  1494.5 80.8 %copy-start.226 = (f32[64]{0:T(128)S(1)}, f32[64]{0:T(128)}, u32[]{:S(2)}) copy-start(f32[64]{0:T(128)} %copy-done.225) | copy-start | bytes 772
  1494.5 80.8 %copy-start.63 = (f32[64,1536]{1,0:T(8,128)S(1)}, f32[64,1536]{1,0:T(8,128)}, u32[]{:S(2)}) copy-start(f32[64,1536]{1,0:T(8,128)} %copy-done.62) | copy-start | bytes 1179652
  1494.5 80.8 %copy-start.92 = (f32[64,1536]{1,0:T(8,128)S(1)}, f32[64,1536]{1,0:T(8,128)}, u32[]{:S(2)}) copy-start(f32[64,1536]{1,0:T(8,128)} %get-tuple-element.53) | copy-start | bytes 1179652
  (237 other events, 2547.0 us)
Sparse Core Ops, SparseCore 0:
  45.9 34.6 reduce-scatter.18
  187.6 34.5 reduce-scatter.20
  252.4 34.4 reduce-scatter.22
  404.0 34.6 reduce-scatter.24
  440.2 45.3 all-gather.8
  488.3 35.3 reduce-scatter.26
  664.6 18.4 reduce-scatter.32
  730.3 34.5 reduce-scatter.30
  796.3 34.4 reduce-scatter.34
  833.6 34.2 reduce-scatter.28
  874.5 36.0 all-gather.4
  947.9 18.0 reduce-scatter.38
  1021.9 34.1 reduce-scatter.36
  1085.6 34.5 reduce-scatter.40
  1128.2 36.0 all-gather.6
  1201.7 17.9 reduce-scatter.44
  1275.6 34.1 reduce-scatter.42
  1340.9 34.5 reduce-scatter.46
  1382.4 102.0 all-reduce.16
  1489.1 140.3 all-reduce.18
  1633.6 120.7 reduce-scatter.52
  1758.3 120.7 reduce-scatter.50
  1883.1 120.7 reduce-scatter.48
where the time goes:
time: 2030 us; the launch traced here: 2020 us
  waiting for transfers between devices  662 us (33%)
  matrix products  470 us (23%)
  local copies, waits for them, and re-layouts  454 us (22%)
  blocking collectives  254 us (13%)
  other arithmetic  151 us (7%)
    reduce_scatter x1, waiting for transfers between devices, reduce_experts(): lax.psum_scatter(expert_parts[2], 'dp', scatter_dimension=0, tiled=True)  125 us
    reduce_scatter x1, waiting for transfers between devices, reduce_experts(): lax.psum_scatter(expert_parts[0], 'dp', scatter_dimension=0, tiled=True)  125 us
    reduce_scatter x1, waiting for transfers between devices, reduce_experts(): lax.psum_scatter(expert_parts[1], 'dp', scatter_dimension=0, tiled=True)  125 us
    reduce_scatter x3, waiting for transfers between devices, layer_forward(): lax.psum_scatter(jnp.einsum('tk,tkd->td', gate_weights, expert_pad[slot_i...  82.1 us
    dot_general x3, matrix products, layer_backward(): jnp.einsum('td,tkd->tk', grad_full, expert_pad[slot_id], precision=highest)  79.8 us
    psum x1, blocking collectives, shards(): lax.psum((attn_gain_sum, expert_gain_sum, router_sum), ('dp', 'tensor'))  76.5 us
    scatter-add x6, other arithmetic, gate_softmax(): jnp.take_along_axis(logits, route_rows, axis=1)  75.6 us
    all_gather x3, blocking collectives, layer_forward(): lax.all_gather(attn_in, 'tensor', axis=0, tiled=True)  67.6 us
  transfers between devices with their start and end apart: 27, of which 21 were waited for; matrix products, arithmetic and copies ran while one was open for 30% of the time, Pallas kernels for 0%

commit v1 on v0

v1 whole, which is shorter than its diff:
```python
import jax
import jax.numpy as jnp
from jax import lax
from jax.sharding import PartitionSpec as P

H = 24
KV = 8
HD = 64
E = 16
CAP = 160

epsilon = 1e-05
rope_base = 10000.0
masked_score = -1e30
bf16 = jnp.bfloat16
f32 = jnp.float32


def dot(a, b, dims):
    return lax.dot_general(a, b, (dims, ((), ())), preferred_element_type=f32)


NN = ((1,), (0,))
NT = ((1,), (1,))
TN = ((0,), (0,))


def swapped(value):
    return lax.ppermute(value, "section", [(0, 1), (1, 0)])


def rotate_half(rows_in):
    half_width = rows_in.shape[-1] // 2
    return jnp.concatenate([-rows_in[..., half_width:], rows_in[..., :half_width]], axis=-1)


def rope_tables(position, head_dim):
    half_width = head_dim // 2
    freqs = rope_base ** (-2.0 * jnp.arange(half_width, dtype=f32) / head_dim)
    angles = position.astype(f32)[:, None] * freqs[None, :]
    return (
        jnp.concatenate([jnp.cos(angles)] * 2, axis=1),
        jnp.concatenate([jnp.sin(angles)] * 2, axis=1),
    )


def token_places(lengths, dealing, tokens_pack):
    seq_count = lengths.shape[0]
    token_index = jnp.arange(tokens_pack, dtype=jnp.int32)
    seq_index = jnp.arange(seq_count, dtype=jnp.int32)
    before = seq_index[None, :] <= seq_index[:, None]
    seq_ends = jnp.sum(jnp.where(before, lengths[None, :], 0), axis=1)
    seq_starts = seq_ends - lengths
    segment = jnp.sum((token_index[:, None] >= seq_ends[None, :]).astype(jnp.int32), axis=1)
    seg_onehot = (segment[:, None] == seq_index[None, :]).astype(jnp.int32)
    position = token_index - jnp.sum(seg_onehot * seq_starts[None, :], axis=1)
    dealt_rank = jnp.sum(
        jnp.where(dealing[:, None] == seq_index[None, :], seq_index[:, None], 0), axis=0
    )
    dealt_start = jnp.sum(
        jnp.where(dealt_rank[:, None] < dealt_rank[None, :], lengths[:, None], 0), axis=0
    )
    dealt_place = jnp.sum(seg_onehot * dealt_start[None, :], axis=1) + position
    return segment, position, dealt_place


def expert_masks(dealt_place, order, routes):
    tokens_pack = order.shape[0]
    token_index = jnp.arange(tokens_pack, dtype=jnp.int32)
    priority = jnp.sum(
        jnp.where(dealt_place[:, None] == token_index[None, :], order[None, :], 0), axis=1
    )
    expert_index = jnp.arange(E, dtype=jnp.int32)
    picked = jnp.any(routes[:, :, None] == expert_index[None, None, :], axis=1)
    earlier = (priority[None, :] < priority[:, None]).astype(bf16)
    rank = dot(earlier, picked.astype(bf16), NN)
    kept = picked & (rank < CAP)
    return picked.astype(f32), kept.astype(f32)


def norm_scale(rows_in):
    return lax.rsqrt(jnp.mean(rows_in * rows_in, axis=-1, keepdims=True) + epsilon)


def norm_back(rows_in, gain, out_grad):
    scaled = rows_in * norm_scale(rows_in)
    gain_grad = jnp.sum(out_grad * scaled, axis=0)
    inner = out_grad * gain
    value_grad = norm_scale(rows_in) * (
        inner - scaled * jnp.mean(inner * scaled, axis=-1, keepdims=True)
    )
    return value_grad, gain_grad


def gathered(rows_in):
    return lax.all_gather(rows_in, "tensor", axis=0, tiled=True)


def scattered(partial):
    return lax.psum_scatter(
        partial.astype(bf16), "tensor", scatter_dimension=0, tiled=True
    ).astype(f32)


def layer_forward(weights, stream, tables, masks, allowed):
    attn_gain, joint_weight, output_weight, expert_gain, router_weight, gw, uw, dw = weights
    cosine, sine = tables
    picked, kept = masks
    tokens_pack = allowed.shape[0]
    tensor_size = lax.axis_size("tensor")
    key_heads = KV // tensor_size
    group = H // KV
    qw = H // tensor_size * HD
    kw = key_heads * HD
    attn_in = gathered((stream * norm_scale(stream) * attn_gain).astype(bf16))
    proj = dot(attn_in, joint_weight, NN)

    def rope(block):
        block = block.reshape(tokens_pack, -1, HD)
        return (
            (block * cosine[:, None, :] + rotate_half(block) * sine[:, None, :])
            .astype(bf16)
            .reshape(tokens_pack, -1)
        )

    queries = rope(proj[:, :qw])
    keys = rope(proj[:, qw : qw + kw])
    values = proj[:, qw + kw :].astype(bf16)
    q4 = queries.reshape(tokens_pack, key_heads, group, HD)
    k3 = keys.reshape(tokens_pack, key_heads, HD)
    v3 = values.reshape(tokens_pack, key_heads, HD)
    scores = jnp.einsum("qgnd,kgd->gnqk", q4, k3, preferred_element_type=f32) * 0.125
    scores = jnp.where(allowed, scores, masked_score)
    row_max = jnp.max(scores, axis=-1, keepdims=True)
    weighed = jnp.exp(scores - row_max)
    row_total = jnp.sum(weighed, axis=-1, keepdims=True)
    probs = weighed / row_total
    log_total = row_max + jnp.log(row_total)
    attended = jnp.einsum("gnqk,kgd->qgnd", probs.astype(bf16), v3, preferred_element_type=f32)
    attended = attended.reshape(tokens_pack, qw).astype(bf16)
    mid = stream + scattered(dot(attended, output_weight, NN))
    expert_in = gathered((mid * norm_scale(mid) * expert_gain).astype(bf16))
    logits = dot(expert_in, router_weight, NN)
    top = jnp.max(jnp.where(picked > 0, logits, masked_score), axis=1, keepdims=True)
    weighed = jnp.where(picked > 0, jnp.exp(logits - top), 0.0)
    gate = weighed / jnp.sum(weighed, axis=1, keepdims=True)
    gate_kept = gate * kept
    gate_pre = jnp.einsum("td,edf->tef", expert_in, gw, preferred_element_type=f32)
    up_pre = jnp.einsum("td,edf->tef", expert_in, uw, preferred_element_type=f32)
    hidden = (jax.nn.silu(gate_pre) * up_pre).astype(bf16).astype(f32)
    gated = (hidden * gate_kept[:, :, None]).astype(bf16).reshape(tokens_pack, -1)
    out = mid + scattered(dot(gated, dw.reshape(-1, dw.shape[2]), NN))
    state = (stream, attn_in, mid, queries, keys, values, log_total, attended, expert_in,
             gate_pre, up_pre, gate, gated)
    return out, state


def layer_backward(weights, state, tables, masks, allowed, out_grad):
    attn_gain, joint_weight, output_weight, expert_gain, router_weight, gw, uw, dw = weights
    (stream, attn_in, mid, queries, keys, values, log_total, attended, expert_in,
     gate_pre, up_pre, gate, gated) = state
    cosine, sine = tables
    picked, kept = masks
    tokens_pack = allowed.shape[0]
    rows = stream.shape[0]
    tensor_size = lax.axis_size("tensor")
    key_heads = KV // tensor_size
    group = H // KV
    qw = H // tensor_size * HD
    kw = key_heads * HD
    own = lax.axis_index("tensor") * rows
    grad_full = gathered(out_grad)
    plain = jnp.einsum("td,efd->tef", grad_full, dw, preferred_element_type=f32)
    sig = 1.0 / (1.0 + jnp.exp(-gate_pre))
    act = gate_pre * sig
    hidden = (act * up_pre).astype(bf16).astype(f32)
    gate_part = jnp.sum(hidden * plain, axis=2) * kept
    hidden_grad = plain * (gate * kept)[:, :, None]
    gpg = (hidden_grad * up_pre * (sig * (1.0 + gate_pre * (1.0 - sig)))).astype(bf16)
    upg = (hidden_grad * act).astype(bf16)
    in_part = jnp.einsum("tef,edf->td", gpg, gw, preferred_element_type=f32) + jnp.einsum(
        "tef,edf->td", upg, uw, preferred_element_type=f32
    )
    in_grad = scattered(in_part)
    gate_grad = lax.psum_scatter(gate_part, "tensor", scatter_dimension=0, tiled=True)
    gate_rows = lax.dynamic_slice_in_dim(gate, own, rows, 0)
    expert_rows = lax.dynamic_slice_in_dim(expert_in, own, rows, 0)
    logits_grad = (
        gate_rows * (gate_grad - jnp.sum(gate_rows * gate_grad, axis=1, keepdims=True))
    ).astype(bf16)
    router_grad = dot(expert_rows, logits_grad, TN)
    in_grad = in_grad + dot(logits_grad, router_weight, NT)
    mid_part, expert_gain_grad = norm_back(mid, expert_gain, in_grad)
    mid_grad = out_grad.astype(f32) + mid_part
    attn_out_grad = gathered(mid_grad.astype(bf16))
    attended_grad = dot(attn_out_grad, output_weight, NT).astype(bf16)
    q4 = queries.reshape(tokens_pack, key_heads, group, HD)
    k3 = keys.reshape(tokens_pack, key_heads, HD)
    v3 = values.reshape(tokens_pack, key_heads, HD)
    ag4 = attended_grad.reshape(tokens_pack, key_heads, group, HD)
    scores = jnp.einsum("qgnd,kgd->gnqk", q4, k3, preferred_element_type=f32) * 0.125
    probs = jnp.exp(jnp.where(allowed, scores, masked_score) - log_total)
    probs_grad = jnp.einsum("qgnd,kgd->gnqk", ag4, v3, preferred_element_type=f32)
    inner = jnp.sum(probs * probs_grad, axis=-1, keepdims=True)
    score_grad = (probs * (probs_grad - inner)).astype(bf16)
    value_grad = jnp.einsum("gnqk,qgnd->kgd", probs.astype(bf16), ag4, preferred_element_type=f32)
    value_grad = value_grad.astype(bf16).reshape(tokens_pack, kw)
    query_grad = jnp.einsum("gnqk,kgd->qgnd", score_grad, k3, preferred_element_type=f32) * 0.125
    key_grad = jnp.einsum("gnqk,qgnd->kgd", score_grad, q4, preferred_element_type=f32) * 0.125

    def unrope(block):
        block = block.reshape(tokens_pack, -1, HD)
        return (
            (block * cosine[:, None, :] - rotate_half(block) * sine[:, None, :])
            .astype(bf16)
            .reshape(tokens_pack, -1)
        )

    joint_rows = jnp.concatenate([unrope(query_grad), unrope(key_grad), value_grad], axis=1)
    attn_in_grad = scattered(dot(joint_rows, joint_weight, NT))
    stream_part, attn_gain_grad = norm_back(stream, attn_gain, attn_in_grad)
    stream_grad = mid_grad + stream_part
    small = (attn_gain_grad, expert_gain_grad, router_grad)
    acts = (expert_in, grad_full, attn_in, attn_out_grad,
            gpg.reshape(tokens_pack, -1), upg.reshape(tokens_pack, -1), gated, joint_rows, attended)
    return stream_grad, small, acts


def weight_grads(acts, section):
    expert_in, grad_full, attn_in, attn_out_grad, gpg, upg, gated, joint_rows, attended = acts
    half = expert_in.shape[1] // 2
    wide = (expert_in, grad_full, attn_in, attn_out_grad)
    mine = [lax.dynamic_slice_in_dim(v, section * half, half, 1) for v in wide]
    sent = [lax.dynamic_slice_in_dim(v, (1 - section) * half, half, 1) for v in wide]
    theirs = [swapped(v) for v in sent]
    x, og, ai, ao = [jnp.concatenate([a, b], axis=0) for a, b in zip(mine, theirs)]
    gpg, upg, gated, joint_rows, attended = [
        jnp.concatenate([v, swapped(v)], axis=0) for v in (gpg, upg, gated, joint_rows, attended)
    ]
    tokens = x.shape[0]
    gpg3, upg3, gated3 = [v.reshape(tokens, E, -1) for v in (gpg, upg, gated)]
    gate = jnp.einsum("td,tef->edf", x, gpg3, preferred_element_type=f32).astype(bf16)
    up = jnp.einsum("td,tef->edf", x, upg3, preferred_element_type=f32).astype(bf16)
    down = jnp.einsum("tef,td->efd", gated3, og, preferred_element_type=f32).astype(bf16)
    joint = dot(ai, joint_rows, TN).astype(bf16)
    output = dot(attended, ao, TN).astype(bf16)
    return gate, up, down, joint, output


def shards(
    tokens_in, out_cotangent, attn_gain, query_weight, key_weight, value_weight, output_weight,
    expert_gain, router_weight, gate_weight, up_weight, down_weight, lengths, dealing,
    slot_order, routes,
):
    section = lax.axis_index("section")
    first = section == 0

    def pick(pair):
        return lax.dynamic_index_in_dim(pair, section, 0, keepdims=False)

    qw = query_weight.shape[2]
    kw = key_weight.shape[2]
    joint_weight = jnp.concatenate([query_weight[0], key_weight[0], value_weight[0]], axis=1)
    held = (attn_gain[0], joint_weight, output_weight[0], expert_gain[0], router_weight[0],
            gate_weight[0], up_weight[0], down_weight[0])
    other = [swapped(v) for v in held]
    weights = (
        [jnp.where(first, a, b) for a, b in zip(held, other)],
        [jnp.where(first, b, a) for a, b in zip(held, other)],
    )
    tokens_pack = slot_order.shape[3]
    segment, position, dealt = token_places(pick(lengths)[0], pick(dealing)[0], tokens_pack)
    tables = rope_tables(position, HD)
    token_index = jnp.arange(tokens_pack, dtype=jnp.int32)
    allowed = (segment[:, None] == segment[None, :]) & (token_index[None, :] <= token_index[:, None])
    orders = slot_order[0, :, 0]
    order_own, order_sent = pick(orders), pick(orders[::-1])
    routes_own, routes_sent = pick(routes[0]), pick(routes[0][::-1])
    order_other, routes_other = swapped(order_sent), swapped(routes_sent)
    masks = (
        expert_masks(dealt, jnp.where(first, order_own, order_other),
                     jnp.where(first, routes_own, routes_other)),
        expert_masks(dealt, jnp.where(first, order_other, order_own),
                     jnp.where(first, routes_other, routes_own)),
    )
    stream = pick(tokens_in).astype(f32)
    out0, state0 = layer_forward(weights[0], stream, tables, masks[0], allowed)
    out1, state1 = layer_forward(weights[1], out0.astype(bf16).astype(f32), tables, masks[1], allowed)
    grad1, small1, acts1 = layer_backward(weights[1], state1, tables, masks[1], allowed,
                                          pick(out_cotangent))
    sums1 = weight_grads(acts1, section)
    grad0, small0, acts0 = layer_backward(weights[0], state0, tables, masks[0], allowed,
                                          grad1.astype(bf16))
    sums0 = weight_grads(acts0, section)

    def by_layer(zero, one):
        mine = jnp.where(first, zero, one)
        theirs = swapped(jnp.where(first, one, zero))
        return jnp.where(first, jnp.stack([mine, theirs]), jnp.stack([theirs, mine]))[None]

    layer_outputs = by_layer(out0, out1)
    input_grads = by_layer(grad0, grad1)

    def reduced(sums):
        gate, up, down, joint, output = sums
        gate, up, down = [
            lax.psum_scatter(v, "dp", scatter_dimension=0, tiled=True) for v in (gate, up, down)
        ]
        joint, output = lax.psum((joint, output), "dp")
        return gate, up, down, joint, output

    red1 = reduced(sums1)
    red0 = reduced(sums0)

    def joined(zero, one, axis):
        mine = jnp.where(first, zero, one)
        theirs = swapped(jnp.where(first, one, zero))
        return jnp.where(
            first,
            jnp.concatenate([mine, theirs], axis=axis),
            jnp.concatenate([theirs, mine], axis=axis),
        ).astype(f32)

    gate, up, down, joint, output = [
        joined(a, b, axis) for a, b, axis in zip(red0, red1, (1, 1, 2, 0, 1))
    ]
    gains = [lax.psum((a, b), ("section", "dp", "tensor")) for a, b in zip(small0, small1)]
    attn_gain_grad, expert_gain_grad, router_grad = [jnp.where(first, a, b) for a, b in gains]
    return (
        layer_outputs,
        input_grads,
        attn_gain_grad[None],
        joint[:, :qw][None],
        joint[:, qw : qw + kw][None],
        joint[:, qw + kw :][None],
        output[None],
        expert_gain_grad[None],
        router_grad[None],
        gate[None],
        up[None],
        down[None],
    )


def solution(mesh):
    return jax.shard_map(
        shards,
        mesh=mesh,
        in_specs=(
            P(None, ("dp", "tensor"), None),
            P(None, ("dp", "tensor"), None),
            P("section", None),
            P("section", None, "tensor"),
            P("section", None, "tensor"),
            P("section", None, "tensor"),
            P("section", "tensor", None),
            P("section", None),
            P("section", None, None),
            P("section", None, None, "tensor"),
            P("section", None, None, "tensor"),
            P("section", None, "tensor", None),
            P(None, "dp", None),
            P(None, "dp", None),
            P("section", None, "dp", None),
            P("section", None, "dp", None),
        ),
        out_specs=(
            P("section", None, ("dp", "tensor"), None),
            P("section", None, ("dp", "tensor"), None),
            P("section", None),
            P("section", None, "tensor"),
            P("section", None, "tensor"),
            P("section", None, "tensor"),
            P("section", "tensor", None),
            P("section", None),
            P("section", None, None),
            P("section", "dp", None, "tensor"),
            P("section", "dp", None, "tensor"),
            P("section", "dp", "tensor", None),
        ),
        check_vma=False,
    )
```

time: 2030 us -> 1040 us (0.51)
  local copies, waits for them, and re-layouts: 454 us -> 73 us
  matrix products: 470 us -> 128 us
  waiting for transfers between devices: 662 us -> 534 us
  other arithmetic: 151 us -> 78.8 us
  blocking collectives: 254 us -> 194 us
    dot_general x81 -> x46, matrix products: 470 us -> 114 us  [the longest x22 47.5 us: dot(): return lax.dot_general(a, b, (dims, ((), ())), preferred_element_type=f32)]
    gather x48 -> x0, local copies, waits for them, and re-layouts: 293 us -> none  [the longest x20 63.4 us: gate_softmax(): jnp.take_along_axis(logits, route_rows, axis=1)]
    reduce_scatter x18 -> x14, waiting for transfers between devices: 548 us -> 378 us  [the longest x6 224 us: reduced(): lax.psum_scatter(v, 'dp', scatter_dimension=0, tiled=True)]
    scatter-add x6 -> x0, other arithmetic: 75.6 us -> none  [gate_softmax(): jnp.take_along_axis(logits, route_rows, axis=1)]
    psum x2, waiting for transfers between devices: 52 us -> 127 us  [the longest x1 87.4 us: reduced(): joint, output = lax.psum((joint, output), 'dp')]
    concatenate x12 -> x0, local copies, waits for them, and re-layouts: 62.7 us -> none  [the longest x3 33.8 us: layer_backward(): jnp.concatenate([slots_back.reshape(E * CAP, width), jnp.zeros((1, width)...]
    all_gather x3 -> x0, waiting for transfers between devices: 55.4 us -> none  [layer_backward(): grad_full = lax.all_gather(out_grad, 'tensor', axis=0, tiled=True)]
    scatter x9 -> x0, local copies, waits for them, and re-layouts: 53.3 us -> none  [the longest x3 24.6 us: layer_backward(): slot_gate = jnp.zeros((E * CAP + 1,), jnp.float32).at[slot_id.reshape(-1)...]
  transfers between devices with their start and end apart: 27 -> 53, of which waited for: 21 -> 25; matrix products, arithmetic and copies ran while one was open for 30% -> 18% of each run, Pallas kernels for 0% -> 0%
where the time goes in v1:
time: 1040 us; the launch traced here: 1030 us
  waiting for transfers between devices  534 us (51%)
  blocking collectives  194 us (19%)
  matrix products  128 us (12%)
  other arithmetic  78.8 us (8%)
  local copies, waits for them, and re-layouts  73 us (7%)
  between operations  16.2 us (2%)
  starting transfers between devices  10.6 us (1%)
    reduce_scatter x6, waiting for transfers between devices, reduced(): lax.psum_scatter(v, 'dp', scatter_dimension=0, tiled=True)  224 us
    reduce_scatter x8, waiting for transfers between devices, scattered(): lax.psum_scatter(partial.astype(bf16), 'tensor', scatter_dimension=0, til...  155 us
    all_gather x8, blocking collectives, gathered(): return lax.all_gather(rows_in, 'tensor', axis=0, tiled=True)  153 us
    psum x1, waiting for transfers between devices, reduced(): joint, output = lax.psum((joint, output), 'dp')  87.4 us
    dot_general x22, matrix products, dot(): return lax.dot_general(a, b, (dims, ((), ())), preferred_element_type=f32)  47.5 us
    psum x1, blocking collectives, shards(): lax.psum((a, b), ('section', 'dp', 'tensor'))  41.1 us
    psum x1, waiting for transfers between devices, shards(): lax.psum((a, b), ('section', 'dp', 'tensor'))  40 us
    unnamed x271, local copies, waits for them, and re-layouts  27.3 us
  transfers between devices with their start and end apart: 53, of which 25 were waited for; matrix products, arithmetic and copies ran while one was open for 18% of the time, Pallas kernels for 0%

profile of v1, /device:TPU:0, one launch (start us, length us, event | category | flops | bytes accessed | tf_op | source)
XLA Modules:
  0.0 1034.3 jit_solution(17009948585308136289)
XLA Ops:
  13.1 20.9 %all_gather.24 = bf16[256,1536]{1,0:T(8,128)(2,1)S(1)} all-gather(bf16[64,1536]{1,0:T(8,128)(2,1)S(1)} %fusion.107), channel_id=1, replica_groups=mesh['section'=2,'dp'=4,'tensor'=4] {'tensor'}, dimensions={0}, use_global_device_ids=true | all-gather | bytes 983040 | tf_op jit(solution)/shard_map/all_gather | solution.py:96
  45.3 19.3 %reduce-scatter.21.cloned.1.call-done = bf16[64,1536]{1,0:T(8,128)(2,1)} async-done(((bf16[256,1536]{1,0:T(8,128)(2,1)}), bf16[64,1536]{1,0:T(8,128)(2,1)}) %reduce-scatter.21.cloned.1.call-update) | async-done | bytes 196624 | tf_op jit(solution)/shard_map/reduce_scatter | solution.py:100
  66.7 18.3 %all_gather.25 = bf16[256,1536]{1,0:T(8,128)(2,1)S(1)} all-gather(bf16[64,1536]{1,0:T(8,128)(2,1)S(1)} %multiply_convert_fusion.7), channel_id=1, replica_groups=mesh['section'=2,'dp'=4,'tensor'=4] {'tensor'}, dimensions={0}, use_global_device_ids=true | all-gather | bytes 983040 | tf_op jit(solution)/shard_map/all_gather | solution.py:96
  86.3 10.1 broadcast_select_fusion.3
  96.4 8.7 copy.137
  105.0 10.1 broadcast_select_fusion.2
  115.2 8.6 copy.138
  123.8 4.9 fusion.197
  136.5 22.8 %reduce-scatter.23.cloned.1.call-done = bf16[64,1536]{1,0:T(8,128)(2,1)} async-done(((bf16[256,1536]{1,0:T(8,128)(2,1)}), bf16[64,1536]{1,0:T(8,128)(2,1)}) %reduce-scatter.23.cloned.1.call-update) | async-done | bytes 196624 | tf_op jit(solution)/shard_map/reduce_scatter | solution.py:100
  160.6 18.0 %all_gather.26 = bf16[256,1536]{1,0:T(8,128)(2,1)S(1)} all-gather(bf16[64,1536]{1,0:T(8,128)(2,1)S(1)} %fusion.103), channel_id=1, replica_groups=mesh['section'=2,'dp'=4,'tensor'=4] {'tensor'}, dimensions={0}, use_global_device_ids=true | all-gather | bytes 983040 | tf_op jit(solution)/shard_map/all_gather | solution.py:96
  178.6 3.2 fusion.74
  185.8 3.1 convolution_convert_fusion.2
  189.9 25.1 %all-gather = bf16[1,256,1536]{2,1,0:T(8,128)(2,1)} all-gather(bf16[1,64,1536]{2,1,0:T(8,128)(2,1)S(1)} %constant_dynamic-slice_fusion.14), channel_id=2, replica_groups=mesh['section'=2,'dp'=4,'tensor'=4] {'tensor'}, dimensions={1}, use_global_device_ids=true | all-gather | bytes 983040 | tf_op jit(solution)/shard_map/all_gather | solution.py:96
  215.0 8.6 copy.146
  223.7 8.6 copy.145
  234.5 16.2 %all_gather.27 = bf16[256,1536]{1,0:T(8,128)(2,1)S(1)} all-gather(bf16[64,1536]{1,0:T(8,128)(2,1)S(1)} %multiply_convert_fusion.6), channel_id=1, replica_groups=mesh['section'=2,'dp'=4,'tensor'=4] {'tensor'}, dimensions={0}, use_global_device_ids=true | all-gather | bytes 983040 | tf_op jit(solution)/shard_map/all_gather | solution.py:96
  250.7 5.1 fusion.200
  258.9 9.3 fusion.11
  268.3 3.0 convolution_bitcast_fusion.2
  272.1 6.3 fusion.3
  279.8 11.3 %reduce-scatter.49.cloned.1.call-done = f32[64,16]{1,0:T(8,128)} async-done(((f32[256,16]{1,0:T(8,128)}), f32[64,16]{1,0:T(8,128)}) %reduce-scatter.49.cloned.1.call-update) | async-done | bytes 4112
  294.1 21.4 %reduce-scatter.29.cloned.1.call-done = bf16[64,1536]{1,0:T(8,128)(2,1)} async-done(((bf16[256,1536]{1,0:T(8,128)(2,1)}), bf16[64,1536]{1,0:T(8,128)(2,1)}) %reduce-scatter.29.cloned.1.call-update) | async-done | bytes 196624 | tf_op jit(solution)/shard_map/reduce_scatter | solution.py:100
  319.4 18.1 %all_gather.29 = bf16[256,1536]{1,0:T(8,128)(2,1)S(1)} all-gather(bf16[64,1536]{1,0:T(8,128)(2,1)S(1)} %fusion.188), channel_id=1, replica_groups=mesh['section'=2,'dp'=4,'tensor'=4] {'tensor'}, dimensions={0}, use_global_device_ids=true | all-gather | bytes 983040 | tf_op jit(solution)/shard_map/all_gather | solution.py:96
  348.7 3.4 convolution_convert_fusion.1
  352.2 22.7 %reduce-scatter.31.cloned.1.call-done = bf16[64,1536]{1,0:T(8,128)(2,1)} async-done(((bf16[256,1536]{1,0:T(8,128)(2,1)}), bf16[64,1536]{1,0:T(8,128)(2,1)}) %reduce-scatter.31.cloned.1.call-update) | async-done | bytes 196624 | tf_op jit(solution)/shard_map/reduce_scatter | solution.py:100
  378.9 18.0 %all_gather.30 = bf16[256,1536]{1,0:T(8,128)(2,1)S(1)} all-gather(bf16[64,1536]{1,0:T(8,128)(2,1)S(1)} %get-tuple-element.86), channel_id=1, replica_groups=mesh['section'=2,'dp'=4,'tensor'=4] {'tensor'}, dimensions={0}, use_global_device_ids=true | all-gather | bytes 983040 | tf_op jit(solution)/shard_map/all_gather | solution.py:96
  396.9 7.9 multiply_convert_fusion.1
  408.7 6.3 fusion.2
  416.5 7.5 fusion.5
  431.1 20.5 %reduce-scatter.33.cloned.1.call-done = bf16[64,1536]{1,0:T(8,128)(2,1)} async-done(((bf16[256,1536]{1,0:T(8,128)(2,1)}), bf16[64,1536]{1,0:T(8,128)(2,1)}) %reduce-scatter.33.cloned.1.call-update) | async-done | bytes 196624 | tf_op jit(solution)/shard_map/reduce_scatter | solution.py:100
  454.3 22.8 %reduce-scatter.27.cloned.1.call-done = bf16[64,1536]{1,0:T(8,128)(2,1)} async-done(((bf16[256,1536]{1,0:T(8,128)(2,1)}), bf16[64,1536]{1,0:T(8,128)(2,1)}) %reduce-scatter.27.cloned.1.call-update) | async-done | bytes 196624 | tf_op jit(solution)/shard_map/reduce_scatter | solution.py:100
  479.7 18.1 %all_gather.31 = bf16[256,1536]{1,0:T(8,128)(2,1)S(1)} all-gather(bf16[64,1536]{1,0:T(8,128)(2,1)S(1)} %get-tuple-element.84), channel_id=1, replica_groups=mesh['section'=2,'dp'=4,'tensor'=4] {'tensor'}, dimensions={0}, use_global_device_ids=true | all-gather | bytes 983040 | tf_op jit(solution)/shard_map/all_gather | solution.py:96
  521.5 4.7 convolution_convert_fusion.4
  530.1 4.7 convolution_convert_fusion.5
  538.1 4.8 convert_bitcast_fusion.2
  548.1 3.5 convert_bitcast_fusion.3
  555.5 3.5 convert_bitcast_fusion
  562.9 3.5 convert_bitcast_fusion.1
  566.4 40.0 %all-reduce.6.cloned.1.call-done = (f32[1536,16]{0,1:T(8,128)}, f32[1536,16]{0,1:T(8,128)}) async-done(((f32[1536,16]{0,1:T(8,128)}, f32[1536,16]{0,1:T(8,128)}), (f32[1536,16]{0,1:T(8,128)}, f32[1536,16]{0,1:T(8,128)})) %all-reduce.6.cloned.1.call-update) | async-done | bytes 196624 | tf_op jit(solution)/shard_map/psum | solution.py:327
  607.9 25.6 %reduce-scatter.35.cloned.1.call-done = bf16[64,1536]{1,0:T(8,128)(2,1)} async-done(((bf16[256,1536]{1,0:T(8,128)(2,1)}), bf16[64,1536]{1,0:T(8,128)(2,1)}) %reduce-scatter.35.cloned.1.call-update) | async-done | bytes 196624 | tf_op jit(solution)/shard_map/reduce_scatter | solution.py:100
  637.1 87.4 %all-reduce.8.cloned.1.call-done = (bf16[768,640]{1,0:T(8,128)(2,1)}, bf16[768,640]{1,0:T(8,128)(2,1)}, bf16[384,768]{1,0:T(8,128)(2,1)}, bf16[384,768]{1,0:T(8,128)(2,1)}) async-done(((bf16[768,640]{1,0:T(8,128)(2,1)}, bf16[768,640]{1,0:T(8,128)(2,1)}, bf16[384,768]{1,0:T(8,128)(2,1)}, bf16[384,768]{1,0:T(8,128)(2,1)}), (bf16[768,640]{1,0:T(8,128)(2,1)}, bf16[768,640]{1,0:T(8,128)(2,1)}, ...) | async-done | bytes 3145744 | tf_op jit(solution)/shard_map/psum | solution.py:309
  730.3 41.1 %all-reduce = (f32[1536]{0:T(1024)}, f32[1536]{0:T(1024)}, f32[1536]{0:T(1024)}, f32[1536]{0:T(1024)}) all-reduce(f32[1536]{0:T(1024)} %get-tuple-element.64, f32[1536]{0:T(1024)} %get-tuple-element.66, f32[1536]{0:T(1024)} %get-tuple-element.60, ...), channel_id=1, replica_groups=mesh['section'=2,'dp'=4,'tensor'=4] {'section','dp','tensor'}, use_global_device_ids=true, to_apply=%region_43.44 | all-reduce | flops 6144 | bytes 49152 | tf_op jit(solution)/shard_map/psum | solution.py:327
  775.3 3.0 fusion.46
  782.2 37.7 %reduce-scatter.45.cloned.1.call-done = bf16[4,128,768]{2,1,0:T(8,128)(2,1)} async-done(((bf16[16,128,768]{2,1,0:T(8,128)(2,1)}), bf16[4,128,768]{2,1,0:T(8,128)(2,1)}) %reduce-scatter.45.cloned.1.call-update) | async-done | bytes 786448 | tf_op jit(solution)/shard_map/reduce_scatter | solution.py:307
  821.5 46.1 %reduce-scatter.39.cloned.1.call-done = bf16[4,768,128]{1,2,0:T(8,128)(2,1)} async-done(((bf16[16,768,128]{1,2,0:T(8,128)(2,1)}), bf16[4,768,128]{1,2,0:T(8,128)(2,1)}) %reduce-scatter.39.cloned.1.call-update) | async-done | bytes 786448 | tf_op jit(solution)/shard_map/reduce_scatter | solution.py:307
  867.6 47.7 %reduce-scatter.37.cloned.1.call-done = bf16[4,768,128]{1,2,0:T(8,128)(2,1)} async-done(((bf16[16,768,128]{1,2,0:T(8,128)(2,1)}), bf16[4,768,128]{1,2,0:T(8,128)(2,1)}) %reduce-scatter.37.cloned.1.call-update) | async-done | bytes 786448 | tf_op jit(solution)/shard_map/reduce_scatter | solution.py:307
  917.9 44.4 %reduce-scatter.43.cloned.1.call-done = bf16[4,768,128]{1,2,0:T(8,128)(2,1)} async-done(((bf16[16,768,128]{1,2,0:T(8,128)(2,1)}), bf16[4,768,128]{1,2,0:T(8,128)(2,1)}) %reduce-scatter.43.cloned.1.call-update) | async-done | bytes 786448 | tf_op jit(solution)/shard_map/reduce_scatter | solution.py:307
  962.3 47.7 %reduce-scatter.41.cloned.1.call-done = bf16[4,768,128]{1,2,0:T(8,128)(2,1)} async-done(((bf16[16,768,128]{1,2,0:T(8,128)(2,1)}), bf16[4,768,128]{1,2,0:T(8,128)(2,1)}) %reduce-scatter.41.cloned.1.call-update) | async-done | bytes 786448 | tf_op jit(solution)/shard_map/reduce_scatter | solution.py:307
  (543 shorter events, 164.8 us)
Async XLA Ops:
  7.2 57.4 %reduce-scatter.21.cloned.1.call-start = ((), (), s32[]{:S(2)}) async-start(), calls=%async_computation.16 | async-start | bytes 983040 | tf_op jit(solution)/shard_map/reduce_scatter | solution.py:100
  8.0 5.0 collective-permute-start
  10.3 23.7 %collective-permute-start.1 = (bf16[1536,640]{1,0:T(8,128)(2,1)S(1)}, bf16[1536,640]{1,0:T(8,128)(2,1)}, u32[]{:S(2)}, u32[]{:S(2)}) collective-permute-start(bf16[1536,640]{1,0:T(8,128)(2,1)S(1)} %pad_maximum_fusion), channel_id=1, source_target_pairs={{0,16},{16,0},{1,17},{17,1},{2,18},{18,2},{3,19},{19,3},{4,20},{20... | collective-permute-start | bytes 5898248 | tf_op jit(solution)/shard_map/ppermute | solution.py:29
  10.4 28.1 %collective-permute-start.2 = (bf16[384,1536]{1,0:T(8,128)(2,1)}, bf16[384,1536]{1,0:T(8,128)(2,1)}, u32[]{:S(2)}, u32[]{:S(2)}) collective-permute-start(bf16[384,1536]{1,0:T(8,128)(2,1)} %bitcast.19), channel_id=1, source_target_pairs={{0,16},{16,0},{1,17},{17,1},{2,18},{18,2},{3,19},{19,3},{4,20},{20... | collective-permute-start | bytes 3538952 | tf_op jit(solution)/shard_map/ppermute | solution.py:29
  10.9 75.4 %collective-permute-start.4 = (bf16[16,1536,128]{2,1,0:T(8,128)(2,1)}, bf16[16,1536,128]{2,1,0:T(8,128)(2,1)}, u32[]{:S(2)}, u32[]{:S(2)}) collective-permute-start(bf16[16,1536,128]{2,1,0:T(8,128)(2,1)} %bitcast.416), channel_id=1, source_target_pairs={{0,16},{16,0},{1,17},{17,1},{2,18},{18,2},{3,19},{19,3},{4,20},{20... | collective-permute-start | bytes 18874376 | tf_op jit(solution)/shard_map/ppermute | solution.py:29
  11.0 94.1 %collective-permute-start.5 = (bf16[16,1536,128]{2,1,0:T(8,128)(2,1)}, bf16[16,1536,128]{2,1,0:T(8,128)(2,1)}, u32[]{:S(2)}, u32[]{:S(2)}) collective-permute-start(bf16[16,1536,128]{2,1,0:T(8,128)(2,1)} %bitcast.417), channel_id=1, source_target_pairs={{0,16},{16,0},{1,17},{17,1},{2,18},{18,2},{3,19},{19,3},{4,20},{20... | collective-permute-start | bytes 18874376 | tf_op jit(solution)/shard_map/ppermute | solution.py:29
  41.4 117.9 %reduce-scatter.23.cloned.1.call-start = ((), (), s32[]{:S(2)}) async-start(), calls=%async_computation.17 | async-start | bytes 983040 | tf_op jit(solution)/shard_map/reduce_scatter | solution.py:100
  41.5 2.8 collective-permute-start.3
  41.6 3.0 collective-permute-start.6
  43.4 41.6 %collective-permute-start.8 = (bf16[1536,16]{0,1:T(8,128)(2,1)S(1)}, bf16[1536,16]{0,1:T(8,128)(2,1)S(1)}, u32[]{:S(2)}, u32[]{:S(2)}) collective-permute-start(bf16[1536,16]{0,1:T(8,128)(2,1)S(1)} %bitcast.443), channel_id=1, source_target_pairs={{0,16},{16,0},{1,17},{17,1},{2,18},{18,2},{3,19},{19,3},{4,20},{20... | collective-permute-start | bytes 147464 | tf_op jit(solution)/shard_map/ppermute | solution.py:29
  44.4 88.2 %collective-permute-start.9 = (bf16[16,128,1536]{2,1,0:T(8,128)(2,1)}, bf16[16,128,1536]{2,1,0:T(8,128)(2,1)}, u32[]{:S(2)}, u32[]{:S(2)}) collective-permute-start(bf16[16,128,1536]{2,1,0:T(8,128)(2,1)} %bitcast.478), channel_id=1, source_target_pairs={{0,16},{16,0},{1,17},{17,1},{2,18},{18,2},{3,19},{19,3},{4,20},{20... | collective-permute-start | bytes 18874376 | tf_op jit(solution)/shard_map/ppermute | solution.py:29
  136.5 95.8 %reduce-scatter.25.cloned.1.call-start = ((), (), s32[]{:S(2)}) async-start(), calls=%async_computation.18 | async-start | bytes 983040 | tf_op jit(solution)/shard_map/reduce_scatter | solution.py:100
  188.9 102.2 %reduce-scatter.49.cloned.1.call-start = ((), (), s32[]{:S(2)}) async-start(), calls=%async_computation.30 | async-start | bytes 163840
  272.1 43.5 %reduce-scatter.29.cloned.1.call-start = ((), (), s32[]{:S(2)}) async-start(), calls=%async_computation.20 | async-start | bytes 983040 | tf_op jit(solution)/shard_map/reduce_scatter | solution.py:100
  278.4 96.4 %reduce-scatter.31.cloned.1.call-start = ((), (), s32[]{:S(2)}) async-start(), calls=%async_computation.21 | async-start | bytes 983040 | tf_op jit(solution)/shard_map/reduce_scatter | solution.py:100
  352.1 75.1 %reduce-scatter.51.cloned.1.call-start = ((), (), s32[]{:S(2)}) async-start(), calls=%async_computation.31 | async-start | bytes 163840
  408.6 43.0 %reduce-scatter.33.cloned.1.call-start = ((), (), s32[]{:S(2)}) async-start(), calls=%async_computation.22 | async-start | bytes 983040 | tf_op jit(solution)/shard_map/reduce_scatter | solution.py:100
  415.0 62.1 %reduce-scatter.27.cloned.1.call-start = ((), (), s32[]{:S(2)}) async-start(), calls=%async_computation.19 | async-start | bytes 983040 | tf_op jit(solution)/shard_map/reduce_scatter | solution.py:100
  424.1 182.2 %all-reduce.6.cloned.1.call-start = ((), (), s32[]{:S(2)}) async-start(), calls=%async_computation.32 | async-start | bytes 393216 | tf_op jit(solution)/shard_map/psum | solution.py:327
  431.1 202.4 %reduce-scatter.35.cloned.1.call-start = ((), (), s32[]{:S(2)}) async-start(), calls=%async_computation.23 | async-start | bytes 983040 | tf_op jit(solution)/shard_map/reduce_scatter | solution.py:100
  507.9 216.5 %all-reduce.8.cloned.1.call-start = ((), (), s32[]{:S(2)}) async-start(), calls=%async_computation.33 | async-start | bytes 6291456 | tf_op jit(solution)/shard_map/psum | solution.py:309
  508.1 3.0 collective-permute-start.14
  509.9 3.8 collective-permute-start.20
  510.5 4.5 collective-permute-start.12
  510.6 3.0 collective-permute-start.19
  511.1 3.9 collective-permute-start.13
  511.4 5.4 collective-permute-start.18
  513.6 3.2 collective-permute-start.17
  518.2 264.1 %reduce-scatter.47.cloned.1.call-start = ((), (), s32[]{:S(2)}) async-start(), calls=%async_computation.29 | async-start | bytes 3932160 | tf_op jit(solution)/shard_map/reduce_scatter | solution.py:307
  518.2 3.3 collective-permute-start.32
  526.3 293.6 %reduce-scatter.45.cloned.1.call-start = ((), (), s32[]{:S(2)}) async-start(), calls=%async_computation.28 | async-start | bytes 3932160 | tf_op jit(solution)/shard_map/reduce_scatter | solution.py:307
  526.8 2.9 collective-permute-start.30
  534.7 332.8 %reduce-scatter.39.cloned.1.call-start = ((), (), s32[]{:S(2)}) async-start(), calls=%async_computation.25 | async-start | bytes 3932160 | tf_op jit(solution)/shard_map/reduce_scatter | solution.py:307
  534.8 3.3 collective-permute-start.24
  535.3 2.8 collective-permute-start.25
  542.9 372.3 %reduce-scatter.37.cloned.1.call-start = ((), (), s32[]{:S(2)}) async-start(), calls=%async_computation.24 | async-start | bytes 3932160 | tf_op jit(solution)/shard_map/reduce_scatter | solution.py:307
  544.2 3.2 collective-permute-start.22
  544.6 2.8 collective-permute-start.23
  551.6 410.7 %reduce-scatter.43.cloned.1.call-start = ((), (), s32[]{:S(2)}) async-start(), calls=%async_computation.27 | async-start | bytes 3932160 | tf_op jit(solution)/shard_map/reduce_scatter | solution.py:307
  559.0 451.0 %reduce-scatter.41.cloned.1.call-start = ((), (), s32[]{:S(2)}) async-start(), calls=%async_computation.26 | async-start | bytes 3932160 | tf_op jit(solution)/shard_map/reduce_scatter | solution.py:307
  560.2 2.7 collective-permute-start.27
  607.9 119.9 %collective-permute-start.10 = (f32[64,1536]{1,0:T(8,128)}, f32[64,1536]{1,0:T(8,128)}, u32[]{:S(2)}, u32[]{:S(2)}) collective-permute-start(f32[64,1536]{1,0:T(8,128)} %get-tuple-element.139), channel_id=1, source_target_pairs={{0,16},{16,0},{1,17},{17,1},{2,18},{18,2},{3,19},{19,3},{4,20},{20... | collective-permute-start | bytes 1179656 | tf_op jit(solution)/shard_map/ppermute | solution.py:29
  637.1 136.2 %collective-permute-start.11 = (f32[64,1536]{1,0:T(8,128)}, f32[64,1536]{1,0:T(8,128)}, u32[]{:S(2)}, u32[]{:S(2)}) collective-permute-start(f32[64,1536]{1,0:T(8,128)} %get-tuple-element.118), channel_id=1, source_target_pairs={{0,16},{16,0},{1,17},{17,1},{2,18},{18,2},{3,19},{19,3},{4,20},{20... | collective-permute-start | bytes 1179656 | tf_op jit(solution)/shard_map/ppermute | solution.py:29
  727.1 51.2 %collective-permute-start.16 = (bf16[768,640]{1,0:T(8,128)(2,1)}, bf16[768,640]{1,0:T(8,128)(2,1)S(1)}, u32[]{:S(2)}, u32[]{:S(2)}) collective-permute-start(bf16[768,640]{1,0:T(8,128)(2,1)} %get-tuple-element.110), channel_id=1, source_target_pairs={{0,16},{16,0},{1,17},{17,1},{2,18},{18,2},{3,19},{19,3},{4,20},{20... | collective-permute-start | bytes 2949128 | tf_op jit(solution)/shard_map/ppermute | solution.py:29
  727.3 48.1 %collective-permute-start.21 = (bf16[384,768]{1,0:T(8,128)(2,1)S(1)}, bf16[384,768]{1,0:T(8,128)(2,1)}, u32[]{:S(2)}, u32[]{:S(2)}) collective-permute-start(bf16[384,768]{1,0:T(8,128)(2,1)S(1)} %get-tuple-element.122), channel_id=1, source_target_pairs={{0,16},{16,0},{1,17},{17,1},{2,18},{18,2},{3,19},{19,3},{4,20},{20... | collective-permute-start | bytes 1769480 | tf_op jit(solution)/shard_map/ppermute | solution.py:29
  821.4 193.8 %collective-permute-start.34 = (bf16[4,128,768]{2,1,0:T(8,128)(2,1)S(1)}, bf16[4,128,768]{2,1,0:T(8,128)(2,1)S(1)}, u32[]{:S(2)}, u32[]{:S(2)}) collective-permute-start(bf16[4,128,768]{2,1,0:T(8,128)(2,1)S(1)} %get-tuple-element.112), channel_id=1, source_target_pairs={{0,16},{16,0},{1,17},{17,1},{2,18},{18,2},{3,19},{19,3},{4,20},{20... | collective-permute-start | bytes 2359304 | tf_op jit(solution)/shard_map/ppermute | solution.py:29
  917.9 99.5 %collective-permute-start.26 = (bf16[4,768,128]{1,2,0:T(8,128)(2,1)}, bf16[4,768,128]{1,2,0:T(8,128)(2,1)S(1)}, u32[]{:S(2)}, u32[]{:S(2)}) collective-permute-start(bf16[4,768,128]{1,2,0:T(8,128)(2,1)} %get-tuple-element.116), channel_id=1, source_target_pairs={{0,16},{16,0},{1,17},{17,1},{2,18},{18,2},{3,19},{19,3},{4,20},{20... | collective-permute-start | bytes 2359304 | tf_op jit(solution)/shard_map/ppermute | solution.py:29
  1012.6 10.0 collective-permute-start.29
  (137 other events, 2010.5 us)
Sparse Core Ops, SparseCore 0:
  41.6 22.9 reduce-scatter.20
  136.6 22.6 reduce-scatter.22
  189.0 29.3 reduce-scatter.24
  272.2 18.8 reduce-scatter.48
  293.9 21.5 reduce-scatter.28
  352.2 22.5 reduce-scatter.30
  408.7 18.4 reduce-scatter.50
  430.1 21.4 reduce-scatter.32
  454.5 22.5 reduce-scatter.26
  483.2 123.1 all-reduce.5
  609.2 24.2 reduce-scatter.34
  637.3 87.0 all-reduce.7
  727.7 45.0 reduce-scatter.46
  775.9 43.9 reduce-scatter.44
  823.6 43.9 reduce-scatter.38
  871.3 43.9 reduce-scatter.36
  918.3 43.9 reduce-scatter.42
  966.0 43.9 reduce-scatter.40

commit v2 on v1

v2 whole, which is shorter than its diff:
```python
import functools
import math

import jax
import jax.numpy as jnp
from jax import lax
from jax.experimental import pallas as pl
from jax.experimental.pallas import tpu as pltpu
from jax.sharding import PartitionSpec as P

H = 24
KV = 8
HD = 64
E = 16
CAP = 160

epsilon = 1e-05
rope_base = 10000.0
masked_score = -1e30
bf16 = jnp.bfloat16
f32 = jnp.float32
MESH = pl.DeviceIdType.MESH


def dot(a, b, dims):
    return lax.dot_general(a, b, (dims, ((), ())), preferred_element_type=f32)


NN = ((1,), (0,))
NT = ((1,), (1,))
TN = ((0,), (0,))


def swapped(value):
    return lax.ppermute(value, "section", [(0, 1), (1, 0)])


def rotate_half(rows_in):
    half_width = rows_in.shape[-1] // 2
    return jnp.concatenate([-rows_in[..., half_width:], rows_in[..., :half_width]], axis=-1)


def rope_tables(position, head_dim):
    half_width = head_dim // 2
    freqs = rope_base ** (-2.0 * jnp.arange(half_width, dtype=f32) / head_dim)
    angles = position.astype(f32)[:, None] * freqs[None, :]
    return (
        jnp.concatenate([jnp.cos(angles)] * 2, axis=1),
        jnp.concatenate([jnp.sin(angles)] * 2, axis=1),
    )


def token_places(lengths, dealing, tokens_pack):
    seq_count = lengths.shape[0]
    token_index = jnp.arange(tokens_pack, dtype=jnp.int32)
    seq_index = jnp.arange(seq_count, dtype=jnp.int32)
    before = seq_index[None, :] <= seq_index[:, None]
    seq_ends = jnp.sum(jnp.where(before, lengths[None, :], 0), axis=1)
    seq_starts = seq_ends - lengths
    segment = jnp.sum((token_index[:, None] >= seq_ends[None, :]).astype(jnp.int32), axis=1)
    seg_onehot = (segment[:, None] == seq_index[None, :]).astype(jnp.int32)
    position = token_index - jnp.sum(seg_onehot * seq_starts[None, :], axis=1)
    dealt_rank = jnp.sum(
        jnp.where(dealing[:, None] == seq_index[None, :], seq_index[:, None], 0), axis=0
    )
    dealt_start = jnp.sum(
        jnp.where(dealt_rank[:, None] < dealt_rank[None, :], lengths[:, None], 0), axis=0
    )
    dealt_place = jnp.sum(seg_onehot * dealt_start[None, :], axis=1) + position
    return segment, position, dealt_place


def expert_masks(dealt_place, order, routes):
    tokens_pack = order.shape[0]
    token_index = jnp.arange(tokens_pack, dtype=jnp.int32)
    priority = jnp.sum(
        jnp.where(dealt_place[:, None] == token_index[None, :], order[None, :], 0), axis=1
    )
    expert_index = jnp.arange(E, dtype=jnp.int32)
    picked = jnp.any(routes[:, :, None] == expert_index[None, None, :], axis=1)
    earlier = (priority[None, :] < priority[:, None]).astype(bf16)
    rank = dot(earlier, picked.astype(bf16), NN)
    kept = picked & (rank < CAP)
    return picked.astype(f32), kept.astype(f32)


def norm_scale(rows_in):
    return lax.rsqrt(jnp.mean(rows_in * rows_in, axis=-1, keepdims=True) + epsilon)


def params(collective_id):
    return pltpu.CompilerParams(
        collective_id=collective_id, has_side_effects=True, vmem_limit_bytes=56 * 2**20
    )


def tensor_peers(count):
    me = lax.axis_index("tensor")
    return [{"tensor": lax.rem(me + step, count)} for step in range(1, count)]


def greet(peers):
    barrier = pltpu.get_barrier_semaphore()
    for peer in peers:
        pl.semaphore_signal(barrier, inc=1, device_id=peer, device_id_type=MESH)
    pl.semaphore_wait(barrier, len(peers))


def factors(count):
    inner = math.isqrt(count)
    while count % inner:
        inner -= 1
    return count // inner, inner


def group_place(count):
    outer, inner = factors(count)
    me = lax.axis_index("dp")
    return outer, inner, me // inner, lax.rem(me, inner)


def near_groups(count):
    outer, inner, mo, mi = group_place(count)
    across = [lax.rem(mi + step, inner) for step in range(1, inner)]
    along = [lax.rem(mo + step, outer) for step in range(1, outer)]
    return (
        [(place, {"dp": mo * inner + place}) for place in across],
        [(place, {"dp": place * inner + mi}) for place in along],
    )


class FirstStage:
    def __init__(self, value, axis):
        self.count = lax.axis_size("dp")
        outer, inner = factors(self.count)
        self.inputs = [value.reshape((outer, inner, value.shape[0] // self.count) + value.shape[1:])]
        self.axis = axis
        shape = list(self.inputs[0].shape[2:])
        shape[axis] //= 2
        self.half = shape[axis]
        self.outputs = [
            jax.ShapeDtypeStruct((inner - 1, outer, *shape), value.dtype),
            jax.ShapeDtypeStruct((outer - 1, inner, *shape), value.dtype),
        ]
        self.copies = inner + outer - 2

    def pairs(self, inputs, outputs):
        across, along = near_groups(self.count)
        value = inputs[0]
        cut = [slice(None)] * 3
        first, second = list(cut), list(cut)
        first[self.axis], second[self.axis] = pl.ds(0, self.half), pl.ds(self.half, self.half)
        found = []
        for slot, (place, device) in enumerate(across):
            found.append((value.at[(slice(None), place, *first)], outputs[0].at[slot], device))
        for slot, (place, device) in enumerate(along):
            found.append((value.at[(place, slice(None), *second)], outputs[1].at[slot], device))
        return found

    def peers(self):
        across, along = near_groups(self.count)
        return [device for _, device in across + along]

    def sums(self, outputs):
        outer, inner, mo, mi = group_place(self.count)
        value = self.inputs[0]
        first, second = jnp.split(value, 2, axis=2 + self.axis)
        row = lax.dynamic_index_in_dim(first, mi, 1, keepdims=False).astype(f32)
        col = lax.dynamic_index_in_dim(second, mo, 0, keepdims=False).astype(f32)
        for slot in range(inner - 1):
            row = row + outputs[0][slot].astype(f32)
        for slot in range(outer - 1):
            col = col + outputs[1][slot].astype(f32)
        return row.astype(bf16), col.astype(bf16)


class SecondStage:
    def __init__(self, row, col, axis):
        self.count = lax.axis_size("dp")
        outer, inner = factors(self.count)
        self.inputs = [row, col]
        self.axis = axis
        self.outputs = [
            jax.ShapeDtypeStruct((outer - 1, *row.shape[1:]), row.dtype),
            jax.ShapeDtypeStruct((inner - 1, *col.shape[1:]), col.dtype),
        ]
        self.copies = inner + outer - 2

    def pairs(self, inputs, outputs):
        across, along = near_groups(self.count)
        found = []
        for slot, (place, device) in enumerate(along):
            found.append((inputs[0].at[place], outputs[0].at[slot], device))
        for slot, (place, device) in enumerate(across):
            found.append((inputs[1].at[place], outputs[1].at[slot], device))
        return found

    def peers(self):
        across, along = near_groups(self.count)
        return [device for _, device in across + along]

    def sums(self, outputs):
        outer, inner, mo, mi = group_place(self.count)
        row = lax.dynamic_index_in_dim(self.inputs[0], mo, 0, keepdims=False).astype(f32)
        col = lax.dynamic_index_in_dim(self.inputs[1], mi, 0, keepdims=False).astype(f32)
        for slot in range(outer - 1):
            row = row + outputs[0][slot].astype(f32)
        for slot in range(inner - 1):
            col = col + outputs[1][slot].astype(f32)
        return jnp.concatenate([row, col], axis=self.axis)


class Scatter:
    def __init__(self, value):
        self.count = lax.axis_size("dp")
        block = (value.shape[0] // self.count,) + value.shape[1:]
        self.inputs = [value.reshape((self.count, *block))]
        self.outputs = [jax.ShapeDtypeStruct((self.count - 1, *block), value.dtype)]
        self.copies = self.count - 1

    def pairs(self, inputs, outputs):
        me = lax.axis_index("dp")
        found = []
        for step in range(1, self.count):
            place = lax.rem(me + step, self.count)
            found.append((inputs[0].at[place], outputs[0].at[step - 1], {"dp": place}))
        return found

    def peers(self):
        me = lax.axis_index("dp")
        return [{"dp": lax.rem(me + step, self.count)} for step in range(1, self.count)]

    def sums(self, outputs):
        me = lax.axis_index("dp")
        total = lax.dynamic_index_in_dim(self.inputs[0], me, 0, keepdims=False).astype(f32)
        for slot in range(self.count - 1):
            total = total + outputs[0][slot].astype(f32)
        return total.astype(bf16)


class Gather:
    def __init__(self, block):
        self.count = lax.axis_size("dp")
        self.inputs = [block]
        self.outputs = [jax.ShapeDtypeStruct((self.count, *block.shape), block.dtype)]
        self.copies = self.count - 1

    def pairs(self, inputs, outputs):
        me = lax.axis_index("dp")
        return [
            (inputs[0], outputs[0].at[me], {"dp": lax.rem(me + step, self.count)})
            for step in range(1, self.count)
        ]

    def peers(self):
        me = lax.axis_index("dp")
        return [{"dp": lax.rem(me + step, self.count)} for step in range(1, self.count)]

    def sums(self, outputs):
        me = lax.axis_index("dp")
        whole = lax.dynamic_update_index_in_dim(outputs[0], self.inputs[0], me, 0)
        return whole.reshape((-1, *self.inputs[0].shape[1:]))


class Beside:
    def __init__(self, jobs):
        self.jobs = jobs
        self.inputs = [v for job in jobs for v in job.inputs]
        self.outputs = [v for job in jobs for v in job.outputs]
        self.total = sum(job.copies for job in jobs)
        self.sems = [pltpu.SemaphoreType.DMA((max(1, self.total),)) for _ in range(2)]

    def peers(self):
        if any(isinstance(job, (Scatter, Gather)) for job in self.jobs):
            count = lax.axis_size("dp")
            me = lax.axis_index("dp")
            return [{"dp": lax.rem(me + step, count)} for step in range(1, count)]
        return self.jobs[0].peers() if self.jobs else []

    def make(self, inputs, outputs, sends, recvs):
        copies = []
        for job in self.jobs:
            mine, inputs = inputs[: len(job.inputs)], inputs[len(job.inputs) :]
            theirs, outputs = outputs[: len(job.outputs)], outputs[len(job.outputs) :]
            for src, dst, device in job.pairs(mine, theirs):
                index = len(copies)
                copies.append(
                    pltpu.make_async_remote_copy(
                        src_ref=src, dst_ref=dst, send_sem=sends.at[index], recv_sem=recvs.at[index],
                        device_id=device, device_id_type=MESH,
                    )
                )
        return copies

    def results(self, outputs):
        found = []
        for job in self.jobs:
            found.append(job.sums(outputs[: len(job.outputs)]))
            outputs = outputs[len(job.outputs) :]
        return found


def spread(count, buf, rows, sends, recvs):
    me = lax.axis_index("tensor")
    own = buf.at[pl.ds(pl.multiple_of(me * rows, rows), rows)]
    copies = []
    for step in range(1, count):
        copies.append(
            pltpu.make_async_remote_copy(
                src_ref=own,
                dst_ref=own,
                send_sem=sends.at[step - 1],
                recv_sem=recvs.at[step - 1],
                device_id={"tensor": lax.rem(me + step, count)},
                device_id_type=MESH,
            )
        )
    for copy in copies:
        copy.start()
    return copies


def deal_out(count, part, rows, columns, landing, sends, recvs):
    me = lax.axis_index("tensor")
    copies = []
    for step in range(1, count):
        peer = lax.rem(me + step, count)
        copies.append(
            pltpu.make_async_remote_copy(
                src_ref=part.at[pl.ds(pl.multiple_of(peer * rows, rows), rows), columns],
                dst_ref=landing.at[step - 1, :, columns],
                send_sem=sends.at[step - 1],
                recv_sem=recvs.at[step - 1],
                device_id={"tensor": peer},
                device_id_type=MESH,
            )
        )
    for copy in copies:
        copy.start()
    return copies


def core_peer():
    return {"section": 1 - lax.axis_index("section")}


def hand_over(own, sent, kept, received, sems, index):
    copies = [
        pltpu.make_async_copy(own, kept, sems[0].at[index]),
        pltpu.make_async_remote_copy(
            src_ref=sent, dst_ref=received, send_sem=sems[1].at[index], recv_sem=sems[2].at[index],
            device_id=core_peer(), device_id_type=MESH,
        ),
    ]
    for copy in copies:
        copy.start()
    return copies


def hand_rows(value, pair, sems, index):
    tokens = value.shape[0]
    return hand_over(value, value, pair.at[pl.ds(0, tokens)], pair.at[pl.ds(tokens, tokens)], sems, index)


def hand_halves(value, pair, sems, index):
    section = lax.axis_index("section")
    tokens, half = value.shape[0], value.shape[1] // 2
    mine = value.at[:, pl.ds(pl.multiple_of(section * half, half), half)]
    other = value.at[:, pl.ds(pl.multiple_of((1 - section) * half, half), half)]
    return hand_over(mine, other, pair.at[pl.ds(0, tokens)], pair.at[pl.ds(tokens, tokens)], sems, index)


def wait_all(copies):
    for copy in copies:
        copy.wait()


def either(use_own, own, other, run):
    @pl.when(use_own)
    def _():
        run(own)

    @pl.when(jnp.logical_not(use_own))
    def _():
        run(other)


def weight_copies(refs, scratch, sems, expert):
    gate, up, down = refs
    gu_s, down_s = scratch
    width = gate.shape[2]
    return (
        pltpu.make_async_copy(gate.at[expert], gu_s.at[expert, :, pl.ds(0, width)], sems.at[0, expert]),
        pltpu.make_async_copy(up.at[expert], gu_s.at[expert, :, pl.ds(width, width)], sems.at[1, expert]),
        pltpu.make_async_copy(
            down.at[expert], down_s.at[pl.ds(pl.multiple_of(expert * width, width), width)], sems.at[2, expert]
        ),
    )


def attn_copies(refs, scratch, sems):
    query, key, value, output = refs
    joint_s, output_s = scratch
    qw, kw = query.shape[1], key.shape[1]
    return (
        pltpu.make_async_copy(query, joint_s.at[:, pl.ds(0, qw)], sems.at[0]),
        pltpu.make_async_copy(key, joint_s.at[:, pl.ds(qw, kw)], sems.at[1]),
        pltpu.make_async_copy(value, joint_s.at[:, pl.ds(qw + kw, kw)], sems.at[2]),
        pltpu.make_async_copy(output, output_s, sems.at[3]),
    )


def turned(block):
    lane = lax.broadcasted_iota(jnp.int32, block.shape, 1)
    half = HD // 2
    return jnp.where(
        lane % HD < half, pltpu.roll(block, block.shape[1] - half, 1), pltpu.roll(block, half, 1)
    )


def column(table, index):
    lane = lax.broadcasted_iota(jnp.int32, table.shape, 1)
    return jnp.sum(jnp.where(lane == index, table, 0.0), axis=1, keepdims=True)


def swap_copies(own, other, sems, piece):
    sends, recvs = sems
    names = len(own)
    if isinstance(piece, tuple):
        name, expert = piece
        source, target = own[name].at[expert], other[name].at[expert]
        index = 4 + (name - 4) * own[4].shape[0] + expert
    else:
        source, target, index = own[piece], other[piece], piece
    return pltpu.make_async_remote_copy(
        src_ref=source, dst_ref=target, send_sem=sends.at[index], recv_sem=recvs.at[index],
        device_id=core_peer(), device_id_type=MESH,
    )


def forward_kernel(layer, count, swap, *refs):
    refs = list(refs)

    def take(number):
        taken = refs[:number]
        del refs[:number]
        return taken

    stream, attn_gain, expert_gain, router, cosine, sine, bias, picked, kept = take(9)
    own = take(7)
    other = None if swap else take(7)
    (out, mid_out, expert_rows_out, qs_out, keys_out, values_out, probs_out, gate_out,
     attn_in_out, expert_in_out, gated_out, attended_out, pre_out) = take(13)
    if swap:
        other = take(7)
    scratch = take(4)
    joint_s, output_s, gu_s, down_s = scratch
    (ag1, ag2, part, landing1, landing2, pre_s, gated_s, attended_s, send_s, recv_s, attn_sems,
     expert_sems, pre_sems, *core_sems) = refs[:16]
    swap_sems = refs[16:]
    rows, width = stream.shape
    tokens = ag1.shape[0]
    experts = gu_s.shape[0]
    hidden_width = gu_s.shape[2] // 2
    kw = keys_out.shape[1]
    qw = attended_s.shape[1]
    heads, key_heads = qw // HD, kw // HD
    group = heads // key_heads
    me = lax.axis_index("tensor")
    own_rows = pl.ds(pl.multiple_of(me * rows, rows), rows)
    use_own = lax.axis_index("section") == layer

    def start_attn(w):
        for copy in attn_copies(w[:4], scratch[:2], attn_sems):
            copy.start()

    def wait_attn(w):
        for copy in attn_copies(w[:4], scratch[:2], attn_sems):
            copy.wait()

    def start_expert(w, expert):
        for copy in weight_copies(w[4:], scratch[2:], expert_sems, expert):
            copy.start()

    def wait_expert(w, expert):
        for copy in weight_copies(w[4:], scratch[2:], expert_sems, expert):
            copy.wait()

    def each_expert(run):
        def step(expert, carry):
            run(expert)
            return carry

        lax.fori_loop(0, experts, step, 0)

    def swap_expert(expert):
        return [swap_copies(own, other, swap_sems, (name, expert)) for name in (4, 5, 6)]

    value = stream[...].astype(bf16).astype(f32)
    ag1[own_rows, :] = (value * norm_scale(value) * attn_gain[...]).astype(bf16)
    greet(tensor_peers(count) + [core_peer()])
    first = spread(count, ag1, rows, send_s.at[0], recv_s.at[0])
    if swap:
        for piece in range(4):
            swap_copies(own, other, swap_sems, piece).start()
        each_expert(lambda expert: [c.start() for c in swap_expert(expert)] and None)

        @pl.when(use_own)
        def _():
            start_attn(own)
            each_expert(lambda expert: start_expert(own, expert))

        @pl.when(jnp.logical_not(use_own))
        def _():
            for piece in range(4):
                swap_copies(own, other, swap_sems, piece).wait_recv()
            start_attn(other)
    else:
        either(use_own, own, other, start_attn)
        either(use_own, own, other, lambda w: each_expert(lambda expert: start_expert(w, expert)))
    wait_all(first)
    handed = hand_halves(ag1, attn_in_out, core_sems, 0)
    either(use_own, own, other, wait_attn)
    proj = dot(ag1[...], joint_s[...], NN)
    for chunk in range(qw // 128):
        block = proj[:, chunk * 128 : chunk * 128 + 128]
        block = (block * cosine[...] + turned(block) * sine[...]).astype(bf16)
        for part_index in range(128 // HD):
            head = chunk * (128 // HD) + part_index
            qs_out[pl.ds(head * tokens, tokens), :] = block[:, part_index * HD : part_index * HD + HD]
    for chunk in range(kw // 128):
        block = proj[:, qw + chunk * 128 : qw + chunk * 128 + 128]
        keys_out[:, pl.ds(chunk * 128, 128)] = (
            block * cosine[...] + turned(block) * sine[...]
        ).astype(bf16)
    values_out[...] = proj[:, qw + kw :].astype(bf16)
    for g in range(key_heads):
        lanes = pl.ds(g * HD, HD)
        span = pl.ds(g * group * tokens, group * tokens)
        scores = dot(qs_out[span, :], keys_out[:, lanes], NT) * 0.125
        scores = (scores.reshape(group, tokens, tokens) + bias[...][None]).reshape(
            group * tokens, tokens
        )
        top = jnp.max(scores, axis=1, keepdims=True)
        weighed = jnp.exp(scores - top)
        probs = (weighed / jnp.sum(weighed, axis=1, keepdims=True)).astype(bf16)
        probs_out[span, :] = probs
        attended = dot(probs, values_out[:, lanes], NN).astype(bf16)
        for h in range(group):
            attended_s[:, pl.ds((g * group + h) * HD, HD)] = attended[h * tokens : (h + 1) * tokens]
    handed += hand_rows(attended_s, attended_out, core_sems, 1)
    part[...] = dot(attended_s[...], output_s[...], NN).astype(bf16)
    dealt = deal_out(count, part, rows, slice(None), landing1, send_s.at[1], recv_s.at[1])
    if swap:
        lead = min(4, experts)

        @pl.when(jnp.logical_not(use_own))
        def _():
            for expert in range(lead):
                for copy in swap_expert(expert):
                    copy.wait_recv()
                start_expert(other, expert)

    wait_all(dealt)
    mid = value + part[own_rows, :].astype(f32)
    for step in range(count - 1):
        mid = mid + landing1[step].astype(f32)
    mid_out[...] = mid
    expert_rows = (mid * norm_scale(mid) * expert_gain[...]).astype(bf16)
    expert_rows_out[...] = expert_rows
    ag2[own_rows, :] = expert_rows
    wait_all(spread(count, ag2, rows, send_s.at[2], recv_s.at[2]))
    handed += hand_halves(ag2, expert_in_out, core_sems, 2)
    logits = dot(ag2[...], router[...], NN)
    chosen = picked[...] > 0
    top = jnp.max(jnp.where(chosen, logits, masked_score), axis=1, keepdims=True)
    weighed = jnp.where(chosen, jnp.exp(logits - top), 0.0)
    gate_out[...] = weighed / jnp.sum(weighed, axis=1, keepdims=True)

    def expert_step(expert, carry):
        if swap:

            @pl.when(jnp.logical_not(use_own) & (expert + lead < experts))
            def _():
                for copy in swap_expert(expert + lead):
                    copy.wait_recv()
                start_expert(other, expert + lead)

        either(use_own, own, other, lambda w: wait_expert(w, expert))
        pre = dot(ag2[...], gu_s[expert], NN)
        pre_s[expert] = pre
        pltpu.make_async_copy(pre_s.at[expert], pre_out.at[expert], pre_sems.at[expert]).start()
        gate_pre, up_pre = pre[:, :hidden_width], pre[:, hidden_width:]
        hidden = (gate_pre / (1.0 + jnp.exp(-gate_pre)) * up_pre).astype(bf16).astype(f32)
        weight = column(gate_out[...] * kept[...], expert)
        gated_s[:, pl.ds(pl.multiple_of(expert * hidden_width, hidden_width), hidden_width)] = (
            hidden * weight
        ).astype(bf16)
        return carry

    lax.fori_loop(0, experts, expert_step, 0)
    handed += hand_rows(gated_s, gated_out, core_sems, 3)
    copies = []
    tile = width // 4
    for t in range(4):
        columns = pl.ds(t * tile, tile)
        part[:, columns] = dot(gated_s[...], down_s[:, columns], NN).astype(bf16)
        copies += deal_out(count, part, rows, columns, landing2, send_s.at[3 + t], recv_s.at[3 + t])
    wait_all(copies)
    total = mid_out[...] + part[own_rows, :].astype(f32)
    for step in range(count - 1):
        total = total + landing2[step].astype(f32)
    out[...] = total
    wait_all(handed)
    if swap:
        for piece in range(4):
            swap_copies(own, other, swap_sems, piece).wait_send()
        each_expert(lambda expert: [c.wait_send() for c in swap_expert(expert)] and None)

        @pl.when(use_own)
        def _():
            for piece in range(4):
                swap_copies(own, other, swap_sems, piece).wait_recv()
            each_expert(lambda expert: [c.wait_recv() for c in swap_expert(expert)] and None)

    def finish(expert, carry):
        pltpu.make_async_copy(pre_s.at[expert], pre_out.at[expert], pre_sems.at[expert]).wait()
        return carry

    lax.fori_loop(0, experts, finish, 0)


def weight_scratch(own):
    query, key, value, output, gate, up, down = own
    depth = query.shape[0]
    experts, _, hidden_width = gate.shape
    return [
        pltpu.VMEM((depth, query.shape[1] + 2 * key.shape[1]), bf16),
        pltpu.VMEM(output.shape, bf16),
        pltpu.VMEM((experts, depth, 2 * hidden_width), bf16),
        pltpu.VMEM((experts * hidden_width, depth), bf16),
    ]


def layer_forward(layer, gains, own, other, stream, tables, masks, bias):
    count = lax.axis_size("tensor")
    attn_gain, expert_gain, router = gains
    picked, kept = masks
    rows, width = stream.shape
    tokens = bias.shape[0]
    qw, kw = own[0].shape[1], own[1].shape[1]
    experts, _, hidden_width = own[4].shape
    heads = qw // HD
    swap = other is None
    vmem = pl.BlockSpec(memory_space=pltpu.VMEM)
    hbm = pl.BlockSpec(memory_space=pl.ANY)
    shape = jax.ShapeDtypeStruct
    dma = pltpu.SemaphoreType.DMA
    pieces = 4 + 3 * experts
    found = pl.pallas_call(
        functools.partial(forward_kernel, layer, count, swap),
        name=f"layer_forward_{layer}",
        out_shape=(
            shape((rows, width), f32),
            shape((rows, width), f32),
            shape((rows, width), bf16),
            shape((heads * tokens, HD), bf16),
            shape((tokens, kw), bf16),
            shape((tokens, kw), bf16),
            shape((heads * tokens, tokens), bf16),
            shape((tokens, experts), f32),
            shape((2 * tokens, width // 2), bf16),
            shape((2 * tokens, width // 2), bf16),
            shape((2 * tokens, experts * hidden_width), bf16),
            shape((2 * tokens, qw), bf16),
            shape((experts, tokens, 2 * hidden_width), f32),
        )
        + (tuple(shape(w.shape, w.dtype) for w in own) if swap else ()),
        in_specs=[vmem] * 9 + [hbm] * (7 if swap else 14),
        out_specs=(vmem,) * 8 + (hbm,) * (12 if swap else 5),
        scratch_shapes=weight_scratch(own)
        + [
            pltpu.VMEM((tokens, width), bf16),
            pltpu.VMEM((tokens, width), bf16),
            pltpu.VMEM((tokens, width), bf16),
            pltpu.VMEM((count - 1, rows, width), bf16),
            pltpu.VMEM((count - 1, rows, width), bf16),
            pltpu.VMEM((experts, tokens, 2 * hidden_width), f32),
            pltpu.VMEM((tokens, experts * hidden_width), bf16),
            pltpu.VMEM((tokens, qw), bf16),
            dma((7, count - 1)),
            dma((7, count - 1)),
            dma((4,)),
            dma((3, experts)),
            dma((experts,)),
            dma((4,)),
            dma((4,)),
            dma((4,)),
        ]
        + ([dma((pieces,)), dma((pieces,))] if swap else []),
        compiler_params=params(1 + layer),
    )(stream, attn_gain, expert_gain, router, *tables, bias, picked, kept, *own,
      *(() if swap else other))
    return found[:13], found[13:]


def norm_back(value, gain, out_grad):
    scale = norm_scale(value)
    scaled = value * scale
    gain_grad = jnp.sum(out_grad * scaled, axis=0, keepdims=True)
    inner = out_grad * gain
    value_grad = scale * (inner - scaled * jnp.mean(inner * scaled, axis=-1, keepdims=True))
    return value_grad, gain_grad


def experts_back_kernel(layer, count, beside, *refs):
    refs = list(refs)

    def take(number):
        taken = refs[:number]
        del refs[:number]
        return taken

    out_grad, mid, expert_gain, router, kept, gate, expert_rows, pre_in = take(8)
    own, other = take(3), take(3)
    beside_in = take(len(beside.inputs))
    mid_grad_out, router_out, expert_gain_out, og_out, gpu_out = take(5)
    beside_out = take(len(beside.outputs))
    scratch = take(2)
    gu_s, down_s = scratch
    (ag1, part, landing1, pre_s, gpu_s, acc, gate_part, gate_land, send_s, recv_s, expert_sems,
     pre_sems, beside_send, beside_recv, *core_sems) = refs
    rows, width = mid.shape
    experts = gu_s.shape[0]
    hidden_width = gu_s.shape[2] // 2
    me = lax.axis_index("tensor")
    own_rows = pl.ds(pl.multiple_of(me * rows, rows), rows)
    use_own = lax.axis_index("section") == layer

    def start_expert(expert, carry):
        either(use_own, own, other,
               lambda w: [c.start() for c in weight_copies(w, scratch, expert_sems, expert)])
        pltpu.make_async_copy(pre_in.at[expert], pre_s.at[expert], pre_sems.at[expert]).start()
        return carry

    ag1[own_rows, :] = out_grad[...].astype(bf16)
    greet(tensor_peers(count) + [core_peer()] + beside.peers())
    first = spread(count, ag1, rows, send_s.at[0], recv_s.at[0])
    lax.fori_loop(0, experts, start_expert, 0)
    behind = beside.make(beside_in, beside_out, beside_send, beside_recv)
    for copy in behind:
        copy.start()
    gate_part[...] = jnp.zeros_like(gate_part)
    wait_all(first)
    handed = hand_halves(ag1, og_out, core_sems, 0)

    def expert_step(expert, carry):
        either(use_own, own, other,
               lambda w: [c.wait() for c in weight_copies(w, scratch, expert_sems, expert)])
        pltpu.make_async_copy(pre_in.at[expert], pre_s.at[expert], pre_sems.at[expert]).wait()
        lanes = pl.ds(pl.multiple_of(expert * hidden_width, hidden_width), hidden_width)
        plain = dot(ag1[...], down_s[lanes, :], NT)
        gate_pre = pre_s[expert, :, pl.ds(0, hidden_width)]
        up_pre = pre_s[expert, :, pl.ds(hidden_width, hidden_width)]
        sig = 1.0 / (1.0 + jnp.exp(-gate_pre))
        act = gate_pre * sig
        hidden = (act * up_pre).astype(bf16).astype(f32)
        held = column(kept[...], expert)
        weight = column(gate[...], expert) * held
        summed = jnp.sum(hidden * plain, axis=1, keepdims=True) * held
        lane = lax.broadcasted_iota(jnp.int32, gate_part.shape, 1)
        gate_part[...] += jnp.where(lane == expert, summed, 0.0)
        hidden_grad = plain * weight
        gpu_s[expert, :, pl.ds(0, hidden_width)] = (
            hidden_grad * up_pre * (sig * (1.0 + gate_pre * (1.0 - sig)))
        ).astype(bf16)
        gpu_s[expert, :, pl.ds(hidden_width, hidden_width)] = (hidden_grad * act).astype(bf16)
        back = dot(gpu_s[expert], gu_s[expert], NT)

        @pl.when(expert == 0)
        def _():
            acc[...] = back

        @pl.when(expert > 0)
        def _():
            acc[...] += back

        return carry

    lax.fori_loop(0, experts, expert_step, 0)
    tokens = ag1.shape[0]
    handed += hand_over(
        gpu_s, gpu_s, gpu_out.at[:, pl.ds(0, tokens)], gpu_out.at[:, pl.ds(tokens, tokens)], core_sems, 1
    )
    part[...] = acc[...].astype(bf16)
    copies = deal_out(count, part, rows, slice(None), landing1, send_s.at[1], recv_s.at[1])
    copies += deal_out(count, gate_part, rows, slice(None), gate_land, send_s.at[2], recv_s.at[2])
    wait_all(copies)
    in_grad = acc[own_rows, :]
    gate_grad = gate_part[own_rows, :]
    for step in range(count - 1):
        in_grad = in_grad + landing1[step].astype(f32)
        gate_grad = gate_grad + gate_land[step]
    gate_grad = gate_grad[:, :experts]
    gate_rows = gate[own_rows, :]
    logits_grad = (
        gate_rows * (gate_grad - jnp.sum(gate_rows * gate_grad, axis=1, keepdims=True))
    ).astype(bf16)
    router_out[...] = dot(logits_grad, expert_rows[...], TN)
    in_grad = in_grad + dot(logits_grad, router[...], NT)
    mid_part, expert_gain_grad = norm_back(mid[...], expert_gain[...], in_grad)
    expert_gain_out[...] = expert_gain_grad
    mid_grad_out[...] = ag1[own_rows, :].astype(f32) + mid_part
    wait_all(handed)
    wait_all(behind)


def experts_back(layer, gains, own, other, out_grad, state, masks, beside):
    count = lax.axis_size("tensor")
    _, expert_gain, router = gains
    mid, gate, expert_rows, pre = state
    rows, width = mid.shape
    tokens = gate.shape[0]
    own, other = own[4:], other[4:]
    experts, depth, hidden_width = own[0].shape
    vmem = pl.BlockSpec(memory_space=pltpu.VMEM)
    hbm = pl.BlockSpec(memory_space=pl.ANY)
    shape = jax.ShapeDtypeStruct
    found = pl.pallas_call(
        functools.partial(experts_back_kernel, layer, count, beside),
        name=f"experts_back_{layer}",
        out_shape=(
            shape((rows, width), f32),
            shape((experts, width), f32),
            shape((1, width), f32),
            shape((2 * tokens, width // 2), bf16),
            shape((experts, 2 * tokens, 2 * hidden_width), bf16),
            *beside.outputs,
        ),
        in_specs=[vmem] * 7 + [hbm] * (7 + len(beside.inputs)),
        out_specs=(vmem, vmem, vmem, hbm, hbm) + (hbm,) * len(beside.outputs),
        scratch_shapes=[
            pltpu.VMEM((experts, depth, 2 * hidden_width), bf16),
            pltpu.VMEM((experts * hidden_width, depth), bf16),
            pltpu.VMEM((tokens, width), bf16),
            pltpu.VMEM((tokens, width), bf16),
            pltpu.VMEM((count - 1, rows, width), bf16),
            pltpu.VMEM((experts, tokens, 2 * hidden_width), f32),
            pltpu.VMEM((experts, tokens, 2 * hidden_width), bf16),
            pltpu.VMEM((tokens, width), f32),
            pltpu.VMEM((tokens, 128), f32),
            pltpu.VMEM((count - 1, rows, 128), f32),
            pltpu.SemaphoreType.DMA((3, count - 1)),
            pltpu.SemaphoreType.DMA((3, count - 1)),
            pltpu.SemaphoreType.DMA((3, experts)),
            pltpu.SemaphoreType.DMA((experts,)),
            *beside.sems,
            *[pltpu.SemaphoreType.DMA((2,)) for _ in range(3)],
        ],
        compiler_params=params(3 + layer),
    )(out_grad, mid, expert_gain, router, masks[1], gate, expert_rows, pre, *own, *other,
      *beside.inputs)
    return found[:5], beside.results(found[5:])


def attention_back_kernel(layer, count, beside, *refs):
    refs = list(refs)

    def take(number):
        taken = refs[:number]
        del refs[:number]
        return taken

    mid_grad, stream, attn_gain, cosine, sine, qs, keys, values, probs = take(9)
    own, other = take(4), take(4)
    beside_in = take(len(beside.inputs))
    grad_out, attn_gain_out, ao_out, joint_out = take(4)
    beside_out = take(len(beside.outputs))
    scratch = take(2)
    joint_s, output_s = scratch
    (ag2, part, landing2, ag_stack, dq_s, joint_rows, send_s, recv_s, attn_sems, beside_send,
     beside_recv, *core_sems) = refs
    rows, width = stream.shape
    tokens = ag2.shape[0]
    kw = keys.shape[1]
    qw = output_s.shape[0]
    heads, key_heads = qw // HD, kw // HD
    group = heads // key_heads
    me = lax.axis_index("tensor")
    own_rows = pl.ds(pl.multiple_of(me * rows, rows), rows)
    use_own = lax.axis_index("section") == layer
    ag2[own_rows, :] = mid_grad[...].astype(bf16)
    greet(tensor_peers(count) + [core_peer()] + beside.peers())
    first = spread(count, ag2, rows, send_s.at[0], recv_s.at[0])
    either(use_own, own, other, lambda w: [c.start() for c in attn_copies(w, scratch, attn_sems)])
    behind = beside.make(beside_in, beside_out, beside_send, beside_recv)
    for copy in behind:
        copy.start()
    wait_all(first)
    handed = hand_halves(ag2, ao_out, core_sems, 0)
    either(use_own, own, other, lambda w: [c.wait() for c in attn_copies(w, scratch, attn_sems)])
    attended_grad = dot(ag2[...], output_s[...], NT).astype(bf16)
    for h in range(heads):
        ag_stack[pl.ds(h * tokens, tokens), :] = attended_grad[:, h * HD : (h + 1) * HD]
    for g in range(key_heads):
        lanes = pl.ds(g * HD, HD)
        span = pl.ds(g * group * tokens, group * tokens)
        soft_b = probs[span, :]
        soft = soft_b.astype(f32)
        soft_grad = dot(ag_stack[span, :], values[:, lanes], NT)
        inner = jnp.sum(soft * soft_grad, axis=1, keepdims=True)
        score_grad = (soft * (soft_grad - inner)).astype(bf16)
        dq = dot(score_grad, keys[:, lanes], NN) * 0.125
        for h in range(group):
            dq_s[:, pl.ds((g * group + h) * HD, HD)] = dq[h * tokens : (h + 1) * tokens]
        dq_s[:, pl.ds(qw + g * HD, HD)] = dot(score_grad, qs[span, :], TN) * 0.125
        joint_rows[:, pl.ds(qw + kw + g * HD, HD)] = dot(soft_b, ag_stack[span, :], TN).astype(bf16)
    for chunk in range((qw + kw) // 128):
        lanes = pl.ds(chunk * 128, 128)
        block = dq_s[:, lanes]
        joint_rows[:, lanes] = (block * cosine[...] - turned(block) * sine[...]).astype(bf16)
    handed += hand_rows(joint_rows, joint_out, core_sems, 1)
    copies = []
    tile = width // 2
    for t in range(2):
        columns = pl.ds(t * tile, tile)
        part[:, columns] = dot(joint_rows[...], joint_s[columns, :], NT).astype(bf16)
        copies += deal_out(count, part, rows, columns, landing2, send_s.at[1 + t], recv_s.at[1 + t])
    wait_all(copies)
    in_grad = part[own_rows, :].astype(f32)
    for step in range(count - 1):
        in_grad = in_grad + landing2[step].astype(f32)
    stream_part, attn_gain_grad = norm_back(
        stream[...].astype(bf16).astype(f32), attn_gain[...], in_grad
    )
    attn_gain_out[...] = attn_gain_grad
    grad_out[...] = mid_grad[...] + stream_part
    wait_all(handed)
    wait_all(behind)


def attention_back(layer, gains, own, other, mid_grad, stream, state, tables, beside):
    count = lax.axis_size("tensor")
    attn_gain = gains[0]
    qs, keys, values, probs = state
    rows, width = stream.shape
    tokens = keys.shape[0]
    own, other = own[:4], other[:4]
    qw, kw = own[0].shape[1], own[1].shape[1]
    heads = qw // HD
    vmem = pl.BlockSpec(memory_space=pltpu.VMEM)
    hbm = pl.BlockSpec(memory_space=pl.ANY)
    shape = jax.ShapeDtypeStruct
    found = pl.pallas_call(
        functools.partial(attention_back_kernel, layer, count, beside),
        name=f"attention_back_{layer}",
        out_shape=(
            shape((rows, width), f32),
            shape((1, width), f32),
            shape((2 * tokens, width // 2), bf16),
            shape((2 * tokens, qw + 2 * kw), bf16),
            *beside.outputs,
        ),
        in_specs=[vmem] * 9 + [hbm] * (8 + len(beside.inputs)),
        out_specs=(vmem, vmem, hbm, hbm) + (hbm,) * len(beside.outputs),
        scratch_shapes=[
            pltpu.VMEM((width, qw + 2 * kw), bf16),
            pltpu.VMEM((qw, width), bf16),
            pltpu.VMEM((tokens, width), bf16),
            pltpu.VMEM((tokens, width), bf16),
            pltpu.VMEM((count - 1, rows, width), bf16),
            pltpu.VMEM((heads * tokens, HD), bf16),
            pltpu.VMEM((tokens, qw + kw), f32),
            pltpu.VMEM((tokens, qw + 2 * kw), bf16),
            pltpu.SemaphoreType.DMA((3, count - 1)),
            pltpu.SemaphoreType.DMA((3, count - 1)),
            pltpu.SemaphoreType.DMA((4,)),
            *beside.sems,
            *[pltpu.SemaphoreType.DMA((2,)) for _ in range(3)],
        ],
        compiler_params=params(5 + layer),
    )(mid_grad, stream, attn_gain, *tables, qs, keys, values, probs, *own, *other, *beside.inputs)
    return found[:4], beside.results(found[4:])


def finish_kernel(beside, *refs):
    refs = list(refs)

    def take(number):
        taken = refs[:number]
        del refs[:number]
        return taken

    small, dense, *beside_in = take(2 + len(beside.inputs))
    small_out, whole_out, *beside_out = take(2 + len(beside.outputs))
    (landing, block, small_z, small_dp, small_core, small_sum, small_mid, small_last, small_whole,
     sends, recvs, local_sems, z_sends, z_recvs, dp_sends, dp_recvs, core_sends, core_recvs,
     beside_send, beside_recv) = refs
    count = dense.shape[0]
    tensor = small_z.shape[0] + 1
    lanes = small_z.shape[2]
    me = lax.axis_index("dp")
    here = lax.axis_index("tensor")
    groups = [{"dp": lax.rem(me + step, count)} for step in range(1, count)]
    greet(groups + tensor_peers(tensor) + [core_peer()])

    def remote(src, dst, send, recv, device):
        copy = pltpu.make_async_remote_copy(
            src_ref=src, dst_ref=dst, send_sem=send, recv_sem=recv, device_id=device, device_id_type=MESH
        )
        copy.start()
        return copy

    def columns(place):
        return pl.ds(pl.multiple_of(place * lanes, lanes), lanes)

    first = []
    for step in range(1, tensor):
        place = lax.rem(here + step, tensor)
        first.append(
            remote(small.at[:, columns(place)], small_z.at[step - 1], z_sends.at[0, step - 1],
                   z_recvs.at[0, step - 1], {"tensor": place})
        )
    copies = []
    for step in range(1, count):
        place = lax.rem(me + step, count)
        copies.append(
            remote(dense.at[place], landing.at[step - 1], sends.at[0, step - 1],
                   recvs.at[0, step - 1], {"dp": place})
        )
    behind = beside.make(beside_in, beside_out, beside_send, beside_recv)
    for copy in behind:
        copy.start()
    mine = pltpu.make_async_copy(dense.at[me], block, local_sems.at[0])
    mine.start()
    wait_all(first)
    total = small[:, columns(here)]
    for step in range(tensor - 1):
        total = total + small_z[step]
    small_sum[...] = total
    second = [
        remote(small_sum, small_dp.at[step], dp_sends.at[step], dp_recvs.at[step], groups[step])
        for step in range(count - 1)
    ]
    mine.wait()
    wait_all(copies)
    total = block[...].astype(f32)
    for step in range(count - 1):
        total = total + landing[step].astype(f32)
    block[...] = total.astype(bf16)
    copies = [
        remote(block, whole_out.at[me], sends.at[1, step], recvs.at[1, step], groups[step])
        for step in range(count - 1)
    ]
    mine = pltpu.make_async_copy(block, whole_out.at[me], local_sems.at[1])
    mine.start()
    wait_all(second)
    total = small_sum[...]
    for step in range(count - 1):
        total = total + small_dp[step]
    small_mid[...] = total
    third = remote(small_mid, small_core, core_sends.at[0], core_recvs.at[0], core_peer())
    third.wait()
    small_last[...] = small_mid[...] + small_core[...]
    last = [
        remote(small_last, small_whole.at[:, columns(here)], z_sends.at[1, step - 1],
               z_recvs.at[1, step - 1], {"tensor": lax.rem(here + step, tensor)})
        for step in range(1, tensor)
    ]
    small_whole[:, columns(here)] = small_last[...]
    wait_all(last)
    small_out[...] = small_whole[...]
    mine.wait()
    wait_all(copies)
    wait_all(behind)


def finish(small, dense, beside):
    count = lax.axis_size("dp")
    tensor = lax.axis_size("tensor")
    rows = dense.shape[0] // count
    lanes = small.shape[1] // tensor
    hbm = pl.BlockSpec(memory_space=pl.ANY)
    vmem = pl.BlockSpec(memory_space=pltpu.VMEM)
    dma = pltpu.SemaphoreType.DMA
    found = pl.pallas_call(
        functools.partial(finish_kernel, beside),
        name="finish",
        out_shape=(
            jax.ShapeDtypeStruct(small.shape, f32),
            jax.ShapeDtypeStruct((count, rows, dense.shape[1]), bf16),
            *beside.outputs,
        ),
        in_specs=[vmem] + [hbm] * (1 + len(beside.inputs)),
        out_specs=(vmem,) + (hbm,) * (1 + len(beside.outputs)),
        scratch_shapes=[
            pltpu.VMEM((count - 1, rows, dense.shape[1]), bf16),
            pltpu.VMEM((rows, dense.shape[1]), bf16),
            pltpu.VMEM((tensor - 1, small.shape[0], lanes), f32),
            pltpu.VMEM((count - 1, small.shape[0], lanes), f32),
            pltpu.VMEM((small.shape[0], lanes), f32),
            pltpu.VMEM((small.shape[0], lanes), f32),
            pltpu.VMEM((small.shape[0], lanes), f32),
            pltpu.VMEM((small.shape[0], lanes), f32),
            pltpu.VMEM(small.shape, f32),
            dma((2, count - 1)),
            dma((2, count - 1)),
            dma((2,)),
            dma((2, tensor - 1)),
            dma((2, tensor - 1)),
            dma((count - 1,)),
            dma((count - 1,)),
            dma((1,)),
            dma((1,)),
            *beside.sems,
        ],
        compiler_params=params(7),
    )(small, dense.reshape(count, rows, dense.shape[1]), *beside.inputs)
    return found[0], found[1].reshape(dense.shape), beside.results(found[2:])


def expert_grads_kernel(x, og, gpu, gated, pair, down, turned_x):
    @pl.when(pl.program_id(0) == 0)
    def _():
        turned_x[...] = x[...].T

    pair[0] = dot(turned_x[...], gpu[0], NN).astype(bf16)
    down[0] = dot(gated[...], og[...], TN).astype(bf16)


def expert_grads(x, og, gpu, gated):
    tokens, half = x.shape
    experts, _, wide = gpu.shape
    hidden_width = wide // 2
    return pl.pallas_call(
        expert_grads_kernel,
        name="expert_grads",
        grid=(experts,),
        out_shape=(
            jax.ShapeDtypeStruct((experts, half, wide), bf16),
            jax.ShapeDtypeStruct((experts, hidden_width, half), bf16),
        ),
        in_specs=[
            pl.BlockSpec((tokens, half), lambda e: (0, 0)),
            pl.BlockSpec((tokens, half), lambda e: (0, 0)),
            pl.BlockSpec((1, tokens, wide), lambda e: (e, 0, 0)),
            pl.BlockSpec((tokens, hidden_width), lambda e: (0, e)),
        ],
        out_specs=(
            pl.BlockSpec((1, half, wide), lambda e: (e, 0, 0)),
            pl.BlockSpec((1, hidden_width, half), lambda e: (e, 0, 0)),
        ),
        scratch_shapes=[pltpu.VMEM((half, tokens), bf16)],
        compiler_params=pltpu.CompilerParams(vmem_limit_bytes=32 * 2**20),
    )(x, og, gpu, gated)


def dense_grads_kernel(ai, ao, joint_rows, attended, grads):
    wide = joint_rows.shape[1]
    grads[:, :wide] = dot(ai[...], joint_rows[...], TN).astype(bf16)
    grads[:, wide:] = dot(ao[...], attended[...], TN).astype(bf16)


def dense_grads(ai, ao, joint_rows, attended):
    return pl.pallas_call(
        dense_grads_kernel,
        name="dense_grads",
        out_shape=jax.ShapeDtypeStruct((ai.shape[1], joint_rows.shape[1] + attended.shape[1]), bf16),
        compiler_params=pltpu.CompilerParams(vmem_limit_bytes=32 * 2**20),
    )(ai, ao, joint_rows, attended)


def shards(
    tokens_in, out_cotangent, attn_gain, query_weight, key_weight, value_weight, output_weight,
    expert_gain, router_weight, gate_weight, up_weight, down_weight, lengths, dealing,
    slot_order, routes,
):
    section = lax.axis_index("section")
    first = section == 0

    def pick(pair):
        return lax.dynamic_index_in_dim(pair, section, 0, keepdims=False)

    qw = query_weight.shape[2]
    kw = key_weight.shape[2]
    own = (query_weight[0], key_weight[0], value_weight[0], output_weight[0], gate_weight[0],
           up_weight[0], down_weight[0])
    held = (attn_gain, expert_gain, router_weight[0])
    held_other = [swapped(v) for v in held]
    gains = (
        [jnp.where(first, a, b) for a, b in zip(held, held_other)],
        [jnp.where(first, b, a) for a, b in zip(held, held_other)],
    )
    tokens_pack = slot_order.shape[3]
    segment, position, dealt = token_places(pick(lengths)[0], pick(dealing)[0], tokens_pack)
    cosine, sine = rope_tables(position, HD)
    low_half = jnp.arange(HD) < HD // 2
    tables = tuple(jnp.tile(v, (1, 128 // HD)) for v in (cosine, jnp.where(low_half, -sine, sine)))
    token_index = jnp.arange(tokens_pack, dtype=jnp.int32)
    allowed = (segment[:, None] == segment[None, :]) & (token_index[None, :] <= token_index[:, None])
    bias = jnp.where(allowed, 0.0, masked_score).astype(f32)
    orders = slot_order[0, :, 0]
    order_own, order_sent = pick(orders), pick(orders[::-1])
    routes_own, routes_sent = pick(routes[0]), pick(routes[0][::-1])
    order_other, routes_other = swapped(order_sent), swapped(routes_sent)
    masks = (
        expert_masks(dealt, jnp.where(first, order_own, order_other),
                     jnp.where(first, routes_own, routes_other)),
        expert_masks(dealt, jnp.where(first, order_other, order_own),
                     jnp.where(first, routes_other, routes_own)),
    )
    stream = pick(tokens_in).astype(f32)
    (out0, *state0), other = layer_forward(0, gains[0], own, None, stream, tables, masks[0], bias)
    (out1, *state1), _ = layer_forward(1, gains[1], own, other, out0, tables, masks[1], bias)
    saved = (state0, state1)
    streams = (stream, out0)

    def experts(layer, out_grad, jobs):
        mid, expert_rows, qs, keys, values, probs, gate, ai, x, gated, attended, pre = saved[layer]
        (mid_grad, router_part, gain_part, og, gpu), done = experts_back(
            layer, gains[layer], own, other, out_grad, (mid, gate, expert_rows, pre), masks[layer],
            Beside(jobs)
        )
        return mid_grad, (gain_part, router_part), expert_grads(x, og, gpu, gated), done

    def attention(layer, mid_grad, jobs):
        mid, expert_rows, qs, keys, values, probs, gate, ai, x, gated, attended, pre = saved[layer]
        (grad, gain_part, ao, joint_rows), done = attention_back(
            layer, gains[layer], own, other, mid_grad, streams[layer], (qs, keys, values, probs),
            tables, Beside(jobs)
        )
        return grad, gain_part, dense_grads(ai, ao, joint_rows, attended), done

    mid_grad, small1, (pair, down), _ = experts(1, pick(out_cotangent), [])
    grad1, gain1, dense1, (pair, down) = attention(
        1, mid_grad, [FirstStage(pair, 1), FirstStage(down, 2)]
    )
    mid_grad, small0, (pair0, down0), (pair1, down1, dense1) = experts(
        0, grad1.astype(bf16), [SecondStage(*pair, 1), SecondStage(*down, 2), Scatter(dense1)]
    )
    grad0, gain0, dense0, (pair, down, dense1) = attention(
        0, mid_grad, [FirstStage(pair0, 1), FirstStage(down0, 2), Gather(dense1)]
    )
    blank = jnp.zeros((6, gain0.shape[1]), f32)
    small = jnp.concatenate([small0[1], gain0, small0[0], blank, small1[1], gain1, small1[0], blank])
    small, dense0, (pair0, down0) = finish(
        small, dense0, Beside([SecondStage(*pair, 1), SecondStage(*down, 2)])
    )

    def by_layer(zero, one):
        mine = jnp.where(first, zero, one)
        theirs = swapped(jnp.where(first, one, zero))
        return jnp.where(first, jnp.stack([mine, theirs]), jnp.stack([theirs, mine]))[None]

    layer_outputs = by_layer(out0, out1)
    input_grads = by_layer(grad0, grad1)

    def joined(zero, one, axis):
        mine = jnp.where(first, zero, one).astype(bf16)
        theirs = swapped(jnp.where(first, one, zero).astype(bf16))
        return jnp.where(
            first,
            jnp.concatenate([mine, theirs], axis=axis),
            jnp.concatenate([theirs, mine], axis=axis),
        ).astype(f32)

    pair = joined(pair0, pair1, 1)
    down = joined(down0, down1, 2)
    dense = joined(dense0, dense1, 0)
    hidden_width = pair.shape[2] // 2
    small = jnp.where(first, small[: small.shape[0] // 2], small[small.shape[0] // 2 :])
    router_grad, attn_gain_grad, expert_gain_grad = small[:E].T, small[E : E + 1], small[E + 1 : E + 2]
    joint, output = dense[:, : qw + 2 * kw], dense[:, qw + 2 * kw :].T
    gate, up = pair[:, :, :hidden_width], pair[:, :, hidden_width:]
    return (
        layer_outputs,
        input_grads,
        attn_gain_grad,
        joint[:, :qw][None],
        joint[:, qw : qw + kw][None],
        joint[:, qw + kw :][None],
        output[None],
        expert_gain_grad,
        router_grad[None],
        gate[None],
        up[None],
        down[None],
    )


def solution(mesh):
    return jax.shard_map(
        shards,
        mesh=mesh,
        in_specs=(
            P(None, ("dp", "tensor"), None),
            P(None, ("dp", "tensor"), None),
            P("section", None),
            P("section", None, "tensor"),
            P("section", None, "tensor"),
            P("section", None, "tensor"),
            P("section", "tensor", None),
            P("section", None),
            P("section", None, None),
            P("section", None, None, "tensor"),
            P("section", None, None, "tensor"),
            P("section", None, "tensor", None),
            P(None, "dp", None),
            P(None, "dp", None),
            P("section", None, "dp", None),
            P("section", None, "dp", None),
        ),
        out_specs=(
            P("section", None, ("dp", "tensor"), None),
            P("section", None, ("dp", "tensor"), None),
            P("section", None),
            P("section", None, "tensor"),
            P("section", None, "tensor"),
            P("section", None, "tensor"),
            P("section", "tensor", None),
            P("section", None),
            P("section", None, None),
            P("section", "dp", None, "tensor"),
            P("section", "dp", None, "tensor"),
            P("section", "dp", "tensor", None),
        ),
        check_vma=False,
    )
```

time: 1040 us -> 623 us (0.60)
  waiting for transfers between devices: 534 us -> 0.03 us
  Pallas kernels: 0 us -> 519 us
  blocking collectives: 194 us -> 0 us
  matrix products: 128 us -> 0.46 us
  other arithmetic: 78.8 us -> 37.4 us
  local copies, waits for them, and re-layouts: 73 us -> 53.6 us
  between operations: 16.2 us -> 1.9 us
    pallas_call x0 -> x11, Pallas kernels: none -> 519 us  [the longest x2 176 us: layer_forward(): pl.pallas_call(functools.partial(forward_kernel, layer, count, swap), nam...]
    reduce_scatter x14 -> x0, waiting for transfers between devices: 378 us -> none  [the longest x6 224 us: reduced(): lax.psum_scatter(v, 'dp', scatter_dimension=0, tiled=True)]
    all_gather x8 -> x0, blocking collectives: 153 us -> none  [gathered(): return lax.all_gather(rows_in, 'tensor', axis=0, tiled=True)]
    psum x2 -> x0, waiting for transfers between devices: 127 us -> none  [the longest x1 87.4 us: reduced(): joint, output = lax.psum((joint, output), 'dp')]
    dot_general x24 -> x0, matrix products: 66.8 us -> none  [the longest x2 17.1 us: layer_backward(): plain = jnp.einsum('td,efd->tef', grad_full, dw, preferred_element_type=f32)]
    dot_general x22 -> x2, matrix products: 47.5 us -> 0.46 us  [dot(): return lax.dot_general(a, b, (dims, ((), ())), preferred_element_type=f32)]
    psum x1 -> x0, blocking collectives: 41.1 us -> none  [shards(): lax.psum((a, b), ('section', 'dp', 'tensor'))]
    select_n x4 -> x0, local copies, waits for them, and re-layouts: 34.6 us -> none  [the longest x2 17.3 us: shards(): jnp.where(first, b, a)]
  transfers between devices with their start and end apart: 53 -> 10, of which waited for: 25 -> 0; matrix products, arithmetic and copies ran while one was open for 18% -> 4% of each run, Pallas kernels for 0% -> 0%
where the time goes in v2:
time: 623 us; the launch traced here: 615 us
  Pallas kernels  519 us (83%)
  local copies, waits for them, and re-layouts  53.6 us (9%)
  other arithmetic  37.4 us (6%)
    pallas_call x2, Pallas kernels, layer_forward(): pl.pallas_call(functools.partial(forward_kernel, layer, count, swap), nam...  176 us
    pallas_call x2, Pallas kernels, attention_back(): pl.pallas_call(functools.partial(attention_back_kernel, layer, count, bes...  132 us
    pallas_call x2, Pallas kernels, experts_back(): pl.pallas_call(functools.partial(experts_back_kernel, layer, count, besid...  123 us
    pallas_call x1, Pallas kernels, finish(): pl.pallas_call(functools.partial(finish_kernel, beside), name='finish', o...  68.1 us
    unnamed x135, local copies, waits for them, and re-layouts  26.9 us
    pallas_call x2, Pallas kernels, expert_grads(): pl.pallas_call(expert_grads_kernel, name='expert_grads', grid=(experts,),...  17.9 us
    convert_element_type x8, other arithmetic, sums(): return (row.astype(bf16), col.astype(bf16))  14.5 us
  transfers between devices with their start and end apart: 10, of which 0 were waited for; matrix products, arithmetic and copies ran while one was open for 4% of the time, Pallas kernels for 0%

profile of v2, /device:TPU:0, one launch (start us, length us, event | category | flops | bytes accessed | tf_op | source)
XLA Modules:
  0.0 615.0 jit_solution(13221676522663034782)
XLA Ops:
  2.8 1.0 copy.74
  7.7 1.7 bitcast_convert_fusion.refs_0_.refs_1_
  17.8 90.8 %layer_forward_0.1 = (f32[64,1536]{1,0:T(8,128)}, f32[64,1536]{1,0:T(8,128)}, bf16[64,1536]{1,0:T(8,128)(2,1)}, bf16[1536,64]{1,0:T(8,128)(2,1)}, bf16[256,128]{...) custom-call(f32[64,1536]{1,0:T(8,128)} %bitcast_convert_fusion.refs_, ...), custom_call_target="tpu_custom_call" | custom-call | tf_op jit(solution)/shard_map/layer_forward_0/pallas_call | solution.py:660
  108.6 85.5 %layer_forward_1.1 = (f32[64,1536]{1,0:T(8,128)}, f32[64,1536]{1,0:T(8,128)}, bf16[64,1536]{1,0:T(8,128)(2,1)}, bf16[1536,64]{1,0:T(8,128)(2,1)}, bf16[256,128]{...) custom-call(f32[64,1536]{1,0:T(8,128)} %get-tuple-element.87.refs_0_, ...), custom_call_target="tpu_custom_call" | custom-call | tf_op jit(solution)/shard_map/layer_forward_1/pallas_call | solution.py:660
  194.1 62.0 %experts_back_1.1 = (f32[64,1536]{1,0:T(8,128)}, f32[16,1536]{1,0:T(8,128)}, f32[1,1536]{1,0:T(1,128)}, bf16[512,768]{1,0:T(8,128)(2,1)}, bf16[16,512,256]{2,1,0:T(8,128)(2,1)}) custom-call(bf16[64,1536]{1,0:T(8,128)(2,1)} %dynamic-slice_bitcast_fusion.refs_0_, f32[64,1536]{1,0:T(8,128)} %get-tuple-element.96.refs_1_, f32[1,1536]{1,0:T(1,128)} %get-tuple-element.234.refs_2_, ...), custom_call_target="tpu_custom_call" | custom-call | tf_op jit(solution)/shard_map/experts_back_1/pallas_call | solution.py:829
  256.1 2.2 copy-done.9
  258.3 1.6 copy-done.11
  259.9 1.1 copy-done.19
  261.0 8.9 %expert_grads.2 = (bf16[16,768,256]{2,1,0:T(8,128)(2,1)S(1)}, bf16[16,128,768]{2,1,0:T(8,128)(2,1)S(1)}) custom-call(bf16[512,768]{1,0:T(8,128)(2,1)S(1)} %copy-done.17, bf16[512,768]{1,0:T(8,128)(2,1)S(1)} %copy-done.19, bf16[16,512,256]{2,1,0:T(8,128)(2,1)S(1)} %copy-done.9, bf16[512,2048]{1,0:T(8,128)(2,1)S(1)} %copy-done.11), custom_call_target="tpu_custom_call" | custom-call | tf_op jit(solution)/shard_map/expert_grads/pallas_call | solution.py:1135
  270.0 2.1 fusion.29
  272.1 1.0 copy-done.3
  273.1 3.1 fusion.27
  276.2 58.5 %attention_back_1.1 = (f32[64,1536]{1,0:T(8,128)}, f32[1,1536]{1,0:T(1,128)}, bf16[512,768]{1,0:T(8,128)(2,1)}, bf16[512,640]{1,0:T(8,128)(2,1)}, bf16[1,2,4,384...) custom-call(f32[64,1536]{1,0:T(8,128)} %get-tuple-element.100.refs_0, ...), custom_call_target="tpu_custom_call" | custom-call | tf_op jit(solution)/shard_map/attention_back_1/pallas_call | solution.py:954
  334.6 1.8 convert_element_type.289.refs_0_
  336.5 2.2 add_convert_fusion.3
  338.7 1.6 add_convert_fusion.1
  340.3 1.1 fusion.8.refs_16_
  342.3 1.6 fusion.3.refs_14_
  344.5 1.2 dense_grads.2
  345.8 1.1 copy-done.6
  346.9 60.6 %experts_back_0.1 = (f32[64,1536]{1,0:T(8,128)}, f32[16,1536]{1,0:T(8,128)}, f32[1,1536]{1,0:T(1,128)}, bf16[512,768]{1,0:T(8,128)(2,1)}, bf16[16,512,256]{2,1,0...) custom-call(bf16[64,1536]{1,0:T(8,128)(2,1)} %convert_element_type.2, ...), custom_call_target="tpu_custom_call" | custom-call | tf_op jit(solution)/shard_map/experts_back_0/pallas_call | solution.py:829
  407.6 2.2 copy-done.8
  409.8 1.6 copy-done.10
  411.4 1.1 copy-done.18
  412.5 8.9 %expert_grads.3 = (bf16[16,768,256]{2,1,0:T(8,128)(2,1)S(1)}, bf16[16,128,768]{2,1,0:T(8,128)(2,1)S(1)}) custom-call(bf16[512,768]{1,0:T(8,128)(2,1)S(1)} %copy-done.16, bf16[512,768]{1,0:T(8,128)(2,1)S(1)} %copy-done.18, bf16[16,512,256]{2,1,0:T(8,128)(2,1)S(1)} %copy-done.8, bf16[512,2048]{1,0:T(8,128)(2,1)S(1)} %copy-done.10), custom_call_target="tpu_custom_call" | custom-call | tf_op jit(solution)/shard_map/expert_grads/pallas_call | solution.py:1135
  421.5 2.3 fusion.28
  424.6 3.0 fusion.26
  427.6 2.0 add_convert_fusion.4
  429.7 73.3 %attention_back_0.1 = (f32[64,1536]{1,0:T(8,128)}, f32[1,1536]{1,0:T(1,128)}, bf16[512,768]{1,0:T(8,128)(2,1)}, bf16[512,640]{1,0:T(8,128)(2,1)}, bf16[1,2,4,384...) custom-call(f32[64,1536]{1,0:T(8,128)} %get-tuple-element.124.refs_0, ...), custom_call_target="tpu_custom_call" | custom-call | tf_op jit(solution)/shard_map/attention_back_0/pallas_call | solution.py:954
  503.0 2.4 add_convert_fusion.2
  505.3 2.3 fusion.7.refs_4_
  507.7 1.6 add_convert_fusion
  510.6 1.6 fusion.2.refs_2_
  512.8 1.2 dense_grads.3
  514.1 1.1 copy-done.7
  515.3 2.6 concatenate.112.refs_0_
  517.9 68.1 %finish.1 = (f32[48,1536]{1,0:T(8,128)}, bf16[4,192,1024]{2,1,0:T(8,128)(2,1)}, bf16[1,4,384,256]{3,2,1,0:T(8,128)(2,1)}, bf16[1,4,384,256]{3,2,1,0:T(8,128)(2,1...) custom-call(f32[48,1536]{1,0:T(8,128)} %concatenate.112.refs_0_, bf16[4,192,1024]{2,1,0:T(8,128)(2,1)} %bitcast.140, ...), custom_call_target="tpu_custom_call" | custom-call | tf_op jit(solution)/shard_map/finish/pallas_call | solution.py:1086
  586.0 1.1 slice_select_fusion
  588.4 1.2 add_bitcast_fusion.3
  589.6 1.1 fusion.11
  592.0 1.1 copy-done.27
  595.2 1.1 copy-done.26
  601.7 2.2 fusion.4
  603.8 1.8 fusion
  605.7 1.3 slice_bitcast_fusion.4
  607.0 1.8 slice_bitcast_fusion.2
  609.4 3.1 slice_bitcast_fusion
  612.6 1.9 copy.93
  (200 shorter events, 29.0 us)
Async XLA Ops:
  0.6 8.7 %copy-start = (bf16[2,64,1536]{2,1,0:T(8,128)(2,1)S(1)}, bf16[2,64,1536]{2,1,0:T(8,128)(2,1)}, u32[]{:S(2)}) copy-start(bf16[2,64,1536]{2,1,0:T(8,128)(2,1)} %param.17) | copy-start | bytes 1179652
  0.7 12.5 %copy-start.59 = (s32[1,2,256,8]{2,3,1,0:T(8,128)S(1)}, s32[1,2,256,8]{2,3,1,0:T(8,128)}, u32[]{:S(2)}) copy-start(s32[1,2,256,8]{2,3,1,0:T(8,128)} %param.31) | copy-start | bytes 49156
  0.7 11.3 %copy-start.64 = (f32[1,1536]{1,0:T(1,128)S(1)}, f32[1,1536]{1,0:T(1,128)}, u32[]{:S(2)}) copy-start(f32[1,1536]{1,0:T(1,128)} %param.23) | copy-start | bytes 18436
  0.7 11.9 %copy-start.65 = (f32[1,1536]{1,0:T(1,128)S(1)}, f32[1,1536]{1,0:T(1,128)}, u32[]{:S(2)}) copy-start(f32[1,1536]{1,0:T(1,128)} %param.18) | copy-start | bytes 18436
  1.5 10.2 %collective-permute-start.4 = (s32[256]{0:T(256)S(1)}, s32[256]{0:T(256)S(1)}, u32[]{:S(2)}, u32[]{:S(2)}) collective-permute-start(s32[256]{0:T(256)S(1)} %bitcast.185), channel_id=1, source_target_pairs={{0,16},{16,0},{1,17},{17,1},{2,18},{18,2},{3,19},{19,3},{4,20},{20... | collective-permute-start | bytes 3080 | tf_op jit(solution)/shard_map/ppermute | solution.py:35
  2.8 10.4 %collective-permute-start.3 = (s32[256,8]{0,1:T(8,128)S(1)}, s32[256,8]{0,1:T(8,128)S(1)}, u32[]{:S(2)}, u32[]{:S(2)}) collective-permute-start(s32[256,8]{0,1:T(8,128)S(1)} %dynamic-slice_bitcast_fusion.1), channel_id=1, source_target_pairs={{0,16},{16,0},{1,17},{17,1},{2,18},{18,2},{3,19},{19,3},{4,20},{20... | collective-permute-start | bytes 24584 | tf_op jit(solution)/shard_map/ppermute | solution.py:35
  3.8 13.0 %collective-permute-start.2 = (bf16[1536,16]{1,0:T(8,128)(2,1)S(1)}, bf16[1536,16]{1,0:T(8,128)(2,1)S(1)}, u32[]{:S(2)}, u32[]{:S(2)}) collective-permute-start(bf16[1536,16]{1,0:T(8,128)(2,1)S(1)} %bitcast.175), channel_id=1, source_target_pairs={{0,16},{16,0},{1,17},{17,1},{2,18},{18,2},{3,19},{19,3},{4,20},{20... | collective-permute-start | bytes 147464 | tf_op jit(solution)/shard_map/ppermute | solution.py:35
  4.4 7.6 %collective-permute-start.1 = (f32[1,1536]{1,0:T(1,128)}, f32[1,1536]{1,0:T(1,128)S(1)}, u32[]{:S(2)}, u32[]{:S(2)}) collective-permute-start(f32[1,1536]{1,0:T(1,128)} %param.23), channel_id=1, source_target_pairs={{0,16},{16,0},{1,17},{17,1},{2,18},{18,2},{3,19},{19,3},{4,20},{20... | collective-permute-start | bytes 18440 | tf_op jit(solution)/shard_map/ppermute | solution.py:35
  4.4 8.1 %collective-permute-start = (f32[1,1536]{1,0:T(1,128)}, f32[1,1536]{1,0:T(1,128)S(1)}, u32[]{:S(2)}, u32[]{:S(2)}) collective-permute-start(f32[1,1536]{1,0:T(1,128)} %param.18), channel_id=1, source_target_pairs={{0,16},{16,0},{1,17},{17,1},{2,18},{18,2},{3,19},{19,3},{4,20},{20... | collective-permute-start | bytes 18440 | tf_op jit(solution)/shard_map/ppermute | solution.py:35
  194.1 62.0 %copy-start.17 = (bf16[512,768]{1,0:T(8,128)(2,1)S(1)}, bf16[512,768]{1,0:T(8,128)(2,1)}, u32[]{:S(2)}) copy-start(bf16[512,768]{1,0:T(8,128)(2,1)} %get-tuple-element.105.x) | copy-start | bytes 2359300
  256.1 2.2 copy-start.9
  270.0 3.1 copy-start.3
  270.0 6.2 %copy-start.5 = (bf16[16,128,768]{2,1,0:T(8,128)(2,1)}, bf16[16,128,768]{2,1,0:T(8,128)(2,1)S(1)}, u32[]{:S(2)}) copy-start(bf16[16,128,768]{2,1,0:T(8,128)(2,1)S(1)} %get-tuple-element.110) | copy-start | bytes 9437188
  276.2 60.3 %copy-start.37 = (bf16[2,2,4,128,384]{4,3,2,1,0:T(8,128)(2,1)S(1)}, bf16[2,2,4,128,384]{4,3,2,1,0:T(8,128)(2,1)}, u32[]{:S(2)}) copy-start(bf16[2,2,4,128,384]{4,3,2,1,0:T(8,128)(2,1)} %get-tuple-element.220) | copy-start | bytes 4718596
  276.2 62.5 %copy-start.31 = (bf16[2,2,4,384,256]{4,3,2,1,0:T(8,128)(2,1)S(1)}, bf16[2,2,4,384,256]{4,3,2,1,0:T(8,128)(2,1)}, u32[]{:S(2)}) copy-start(bf16[2,2,4,384,256]{4,3,2,1,0:T(8,128)(2,1)} %get-tuple-element.212) | copy-start | bytes 9437188
  334.6 4.0 copy-start.43
  338.7 2.7 copy-start.30
  342.3 2.2 copy-start.23
  346.9 60.6 %copy-start.16 = (bf16[512,768]{1,0:T(8,128)(2,1)S(1)}, bf16[512,768]{1,0:T(8,128)(2,1)}, u32[]{:S(2)}) copy-start(bf16[512,768]{1,0:T(8,128)(2,1)} %get-tuple-element.129.x) | copy-start | bytes 2359300
  407.6 2.2 copy-start.8
  421.5 3.2 copy-start.2
  421.5 6.2 %copy-start.4 = (bf16[16,128,768]{2,1,0:T(8,128)(2,1)}, bf16[16,128,768]{2,1,0:T(8,128)(2,1)S(1)}, u32[]{:S(2)}) copy-start(bf16[16,128,768]{2,1,0:T(8,128)(2,1)S(1)} %get-tuple-element.134) | copy-start | bytes 9437188
  424.6 3.0 copy-start.47
  429.7 73.3 %copy-start.36 = (bf16[2,2,4,128,384]{4,3,2,1,0:T(8,128)(2,1)S(1)}, bf16[2,2,4,128,384]{4,3,2,1,0:T(8,128)(2,1)}, u32[]{:S(2)}) copy-start(bf16[2,2,4,128,384]{4,3,2,1,0:T(8,128)(2,1)} %get-tuple-element.218) | copy-start | bytes 4718596
  502.9 4.7 copy-start.29
  505.3 2.3 copy-start.41
  507.7 2.5 copy-start.28
  507.7 2.9 copy-start.40
  510.6 2.2 copy-start.22
  512.8 2.4 copy-start.57
  512.8 2.4 copy-start.58
  512.8 2.4 copy-start.60
  512.8 2.4 copy-start.61
  512.8 2.4 copy-start.62
  512.8 2.4 copy-start.63
  517.9 70.6 %copy-start.33 = (bf16[2,4,128,384]{3,2,1,0:T(8,128)(2,1)S(1)}, bf16[2,4,128,384]{3,2,1,0:T(8,128)(2,1)}, u32[]{:S(2)}) copy-start(bf16[2,4,128,384]{3,2,1,0:T(8,128)(2,1)} %fusion.7.refs_4_) | copy-start | bytes 2359300
  586.0 3.6 copy-start.32
  586.0 4.7 copy-start.35
  586.0 4.7 copy-start.55
  588.4 2.5 copy-start.34
  588.4 2.5 copy-start.54
  591.0 2.2 copy-start.27
  591.0 2.6 copy-start.46
  591.4 10.3 %collective-permute-start.9 = (bf16[4,128,768]{2,1,0:T(8,128)(2,1)S(1)}, bf16[4,128,768]{2,1,0:T(8,128)(2,1)S(1)}, u32[]{:S(2)}, u32[]{:S(2)}) collective-permute-start(bf16[4,128,768]{2,1,0:T(8,128)(2,1)S(1)} %get-tuple-element.223), channel_id=1, source_target_pairs={{0,16},{16,0},{1,17},{17,1},{2,18},{18,2},{3,19},{19,3},{4,20},{20... | collective-permute-start | bytes 2359304 | tf_op jit(solution)/shard_map/ppermute | solution.py:35
  593.9 9.9 %collective-permute-start.7 = (bf16[768,1024]{1,0:T(8,128)(2,1)S(1)}, bf16[768,1024]{1,0:T(8,128)(2,1)S(1)}, u32[]{:S(2)}, u32[]{:S(2)}) collective-permute-start(bf16[768,1024]{1,0:T(8,128)(2,1)S(1)} %bitcast.176), channel_id=1, source_target_pairs={{0,16},{16,0},{1,17},{17,1},{2,18},{18,2},{3,19},{19,3},{4,20},{20... | collective-permute-start | bytes 4718600 | tf_op jit(solution)/shard_map/ppermute | solution.py:35
  594.9 4.9 collective-permute-start.6
  598.6 2.2 collective-permute-start.5
  599.2 9.5 %collective-permute-start.8 = (bf16[4,768,256]{2,1,0:T(8,128)(2,1)S(1)}, bf16[4,768,256]{2,1,0:T(8,128)(2,1)S(1)}, u32[]{:S(2)}, u32[]{:S(2)}) collective-permute-start(bf16[4,768,256]{2,1,0:T(8,128)(2,1)S(1)} %get-tuple-element.215), channel_id=1, source_target_pairs={{0,16},{16,0},{1,17},{17,1},{2,18},{18,2},{3,19},{19,3},{4,20},{20... | collective-permute-start | bytes 4718600 | tf_op jit(solution)/shard_map/ppermute | solution.py:35
  (28 other events, 43.7 us)

commit v3 on v2

v3 whole, which is shorter than its diff:
```python
import functools
import math

import jax
import jax.numpy as jnp
from jax import lax
from jax.experimental import pallas as pl
from jax.experimental.pallas import tpu as pltpu
from jax.sharding import PartitionSpec as P

H = 24
KV = 8
HD = 64
E = 16
CAP = 160

epsilon = 1e-05
rope_base = 10000.0
masked_score = -1e30
bf16 = jnp.bfloat16
f32 = jnp.float32
MESH = pl.DeviceIdType.MESH


def dot(a, b, dims):
    return lax.dot_general(a, b, (dims, ((), ())), preferred_element_type=f32)


NN = ((1,), (0,))
NT = ((1,), (1,))
TN = ((0,), (0,))


def swapped(value):
    return lax.ppermute(value, "section", [(0, 1), (1, 0)])


def norm_scale(rows_in):
    return lax.rsqrt(jnp.mean(rows_in * rows_in, axis=-1, keepdims=True) + epsilon)


def params(collective_id):
    return pltpu.CompilerParams(
        collective_id=collective_id, has_side_effects=True, vmem_limit_bytes=56 * 2**20
    )


def tensor_peers(count):
    me = lax.axis_index("tensor")
    return [{"tensor": lax.rem(me + step, count)} for step in range(1, count)]


def greet(peers):
    barrier = pltpu.get_barrier_semaphore()
    for peer in peers:
        pl.semaphore_signal(barrier, inc=1, device_id=peer, device_id_type=MESH)
    pl.semaphore_wait(barrier, len(peers))


def factors(count):
    inner = math.isqrt(count)
    while count % inner:
        inner -= 1
    return count // inner, inner


def group_place(count):
    outer, inner = factors(count)
    me = lax.axis_index("dp")
    return outer, inner, me // inner, lax.rem(me, inner)


def near_groups(count):
    outer, inner, mo, mi = group_place(count)
    across = [lax.rem(mi + step, inner) for step in range(1, inner)]
    along = [lax.rem(mo + step, outer) for step in range(1, outer)]
    return (
        [(place, {"dp": mo * inner + place}) for place in across],
        [(place, {"dp": place * inner + mi}) for place in along],
    )


dma = pltpu.SemaphoreType.DMA


def remote(src, dst, send, recv, device):
    return pltpu.make_async_remote_copy(
        src_ref=src, dst_ref=dst, send_sem=send, recv_sem=recv, device_id=device, device_id_type=MESH
    )


class FirstStage:
    def __init__(self, value, axis):
        self.count = lax.axis_size("dp")
        outer, inner = factors(self.count)
        self.inputs = [value.reshape((outer, inner, value.shape[0] // self.count) + value.shape[1:])]
        self.axis = axis
        shape = list(self.inputs[0].shape[2:])
        shape[axis] //= 2
        self.shape = shape
        self.outputs = [
            jax.ShapeDtypeStruct((inner - 1, outer, *shape), value.dtype),
            jax.ShapeDtypeStruct((outer - 1, inner, *shape), value.dtype),
        ]
        self.sems = [dma((inner + outer - 2,)), dma((inner + outer - 2,))]

    def copies(self, inputs, outputs, sems):
        across, along = near_groups(self.count)
        value = inputs[0]
        half = self.shape[self.axis]
        cut = [slice(None)] * 3
        first, second = list(cut), list(cut)
        first[self.axis], second[self.axis] = pl.ds(0, half), pl.ds(half, half)
        found = []
        for slot, (place, device) in enumerate(across):
            found.append((value.at[(slice(None), place, *first)], outputs[0].at[slot], device))
        for slot, (place, device) in enumerate(along):
            found.append((value.at[(place, slice(None), *second)], outputs[1].at[slot], device))
        return [
            remote(src, dst, sems[0].at[index], sems[1].at[index], device)
            for index, (src, dst, device) in enumerate(found)
        ]

    def start(self, inputs, outputs, sems):
        for copy in self.copies(inputs, outputs, sems):
            copy.start()

    def wait(self, inputs, outputs, sems):
        for copy in self.copies(inputs, outputs, sems):
            copy.wait()

    def results(self, outputs):
        outer, inner, mo, mi = group_place(self.count)
        value = self.inputs[0]
        half = self.shape[self.axis]
        later = [0] * 5
        later[2 + self.axis] = half
        row = lax.dynamic_slice(value, (0, mi, 0, 0, 0), (outer, 1, *self.shape))[:, 0].astype(f32)
        later[0] = mo
        col = lax.dynamic_slice(value, later, (1, inner, *self.shape))[0].astype(f32)
        for slot in range(inner - 1):
            row = row + outputs[0][slot].astype(f32)
        for slot in range(outer - 1):
            col = col + outputs[1][slot].astype(f32)
        return row.astype(bf16), col.astype(bf16)


class Bring:
    def __init__(self, layer, kind, value, in_vmem=False):
        self.layer, self.kind, self.in_vmem = layer, kind, in_vmem
        count = lax.axis_size("dp")
        outer, inner = factors(count)
        self.size = {"column": outer, "row": inner, "all": count}[kind]
        block = value.shape if kind == "all" else value.shape[1:]
        self.inputs = [value]
        self.outputs = [jax.ShapeDtypeStruct((2, self.size, *block), value.dtype)]
        self.sems = [dma((self.size,)), dma((2, self.size)), dma((2,))]
        if not in_vmem:
            self.sems.append(pltpu.VMEM(block, value.dtype))

    def place(self, step):
        count = lax.axis_size("dp")
        outer, inner, mo, mi = group_place(count)
        if self.kind == "column":
            place = lax.rem(mo + step, outer)
            return place, place * inner + mi
        if self.kind == "row":
            place = lax.rem(mi + step, inner)
            return place, mo * inner + place
        place = lax.rem(lax.axis_index("dp") + step, count)
        return place, place

    def parts(self, inputs, outputs, sems):
        core = lax.axis_index("section")
        mine, _ = self.place(0)
        target = outputs[0].at[core, mine]
        recv = sems[1].at[core, mine]

        def source(place):
            return inputs[0] if self.kind == "all" else inputs[0].at[place]

        sent = []
        for step in range(1, self.size):
            place, group = self.place(step)
            sent.append(
                remote(source(place), target, sems[0].at[step - 1], recv,
                       {"dp": group, "section": self.layer})
            )
        across = remote(source(mine), target, sems[0].at[self.size - 1], recv, core_peer())
        if self.in_vmem:
            local = [pltpu.make_async_copy(source(mine), target, sems[2].at[0])]
        else:
            local = [
                pltpu.make_async_copy(source(mine), sems[3], sems[2].at[0]),
                pltpu.make_async_copy(sems[3], target, sems[2].at[1]),
            ]
        return sent, across, local

    def start(self, inputs, outputs, sems):
        sent, across, local = self.parts(inputs, outputs, sems)
        for copy in sent:
            copy.start()
        here = lax.axis_index("section") == self.layer

        @pl.when(here)
        def _():
            local[0].start()

        @pl.when(jnp.logical_not(here))
        def _():
            across.start()

    def wait(self, inputs, outputs, sems):
        sent, across, local = self.parts(inputs, outputs, sems)
        core = lax.axis_index("section")
        here = core == self.layer
        block = inputs[0] if self.kind == "all" else inputs[0].at[0]

        def arrived(which, place):
            remote(block, outputs[0].at[which, place], sems[0].at[0], sems[1].at[which, place],
                   core_peer()).wait_recv()

        for copy in sent:
            copy.wait_send()

        @pl.when(here)
        def _():
            local[0].wait()
            for copy in local[1:]:
                copy.start()
                copy.wait()
            for step in range(self.size):
                place, _ = self.place(step)
                if step:
                    arrived(core, place)
                arrived(1 - core, place)

        @pl.when(jnp.logical_not(here))
        def _():
            across.wait_send()

    def results(self, outputs):
        return outputs[0]


class Scatter:
    def __init__(self, value):
        self.count = lax.axis_size("dp")
        block = (value.shape[0] // self.count,) + value.shape[1:]
        self.inputs = [value.reshape((self.count, *block))]
        self.outputs = [jax.ShapeDtypeStruct((self.count - 1, *block), value.dtype)]
        self.sems = [dma((self.count - 1,)), dma((self.count - 1,))]

    def copies(self, inputs, outputs, sems):
        me = lax.axis_index("dp")
        found = []
        for step in range(1, self.count):
            place = lax.rem(me + step, self.count)
            found.append(
                remote(inputs[0].at[place], outputs[0].at[step - 1], sems[0].at[step - 1],
                       sems[1].at[step - 1], {"dp": place})
            )
        return found

    def start(self, inputs, outputs, sems):
        for copy in self.copies(inputs, outputs, sems):
            copy.start()

    def wait(self, inputs, outputs, sems):
        for copy in self.copies(inputs, outputs, sems):
            copy.wait()

    def results(self, outputs):
        me = lax.axis_index("dp")
        total = lax.dynamic_index_in_dim(self.inputs[0], me, 0, keepdims=False).astype(f32)
        for slot in range(self.count - 1):
            total = total + outputs[0][slot].astype(f32)
        return total.astype(bf16)


def both_cores(groups):
    core = lax.axis_index("section")
    return [{"dp": group, "section": which} for group in groups for which in (core, 1 - core)]


class Beside:
    def __init__(self, jobs):
        self.jobs = jobs
        self.inputs = [v for job in jobs for v in job.inputs]
        self.outputs = [v for job in jobs for v in job.outputs]
        self.sems = [v for job in jobs for v in job.sems]

    def peers(self):
        count = lax.axis_size("dp")
        if any(isinstance(job, Scatter) or getattr(job, "kind", "") == "all" for job in self.jobs):
            me = lax.axis_index("dp")
            return both_cores([lax.rem(me + step, count) for step in range(1, count)])
        if not self.jobs:
            return []
        across, along = near_groups(count)
        return both_cores([device["dp"] for _, device in across + along])

    def each(self, refs, run):
        inputs, outputs, sems = refs
        for job in self.jobs:
            mine, inputs = inputs[: len(job.inputs)], inputs[len(job.inputs) :]
            theirs, outputs = outputs[: len(job.outputs)], outputs[len(job.outputs) :]
            own, sems = sems[: len(job.sems)], sems[len(job.sems) :]
            run(job)(mine, theirs, own)

    def start(self, *refs):
        self.each(refs, lambda job: job.start)

    def wait(self, *refs):
        self.each(refs, lambda job: job.wait)

    def results(self, outputs):
        found = []
        for job in self.jobs:
            found.append(job.results(outputs[: len(job.outputs)]))
            outputs = outputs[len(job.outputs) :]
        return found


def spread(count, buf, rows, sends, recvs):
    me = lax.axis_index("tensor")
    own = buf.at[pl.ds(pl.multiple_of(me * rows, rows), rows)]
    copies = []
    for step in range(1, count):
        copies.append(
            pltpu.make_async_remote_copy(
                src_ref=own,
                dst_ref=own,
                send_sem=sends.at[step - 1],
                recv_sem=recvs.at[step - 1],
                device_id={"tensor": lax.rem(me + step, count)},
                device_id_type=MESH,
            )
        )
    return copies


def deal_out(count, part, rows, columns, landing, sends, recvs):
    me = lax.axis_index("tensor")
    copies = []
    for step in range(1, count):
        peer = lax.rem(me + step, count)
        copies.append(
            pltpu.make_async_remote_copy(
                src_ref=part.at[pl.ds(pl.multiple_of(peer * rows, rows), rows), columns],
                dst_ref=landing.at[step - 1, :, columns],
                send_sem=sends.at[step - 1],
                recv_sem=recvs.at[step - 1],
                device_id={"tensor": peer},
                device_id_type=MESH,
            )
        )
    for copy in copies:
        copy.start()
    return copies


def core_peer():
    return {"section": 1 - lax.axis_index("section")}


def hand_rows(value, pair, sems):
    tokens = value.shape[0]
    return [
        pltpu.make_async_copy(value, pair.at[pl.ds(0, tokens)], sems[0]),
        remote(value, pair.at[pl.ds(tokens, tokens)], sems[1], sems[2], core_peer()),
    ]


def hand_halves(value, pair, sems):
    section = lax.axis_index("section")
    tokens, half = value.shape[0], value.shape[1] // 2
    mine = value.at[:, pl.ds(pl.multiple_of(section * half, half), half)]
    other = value.at[:, pl.ds(pl.multiple_of((1 - section) * half, half), half)]
    return [
        pltpu.make_async_copy(mine, pair.at[pl.ds(0, tokens)], sems[0]),
        remote(other, pair.at[pl.ds(tokens, tokens)], sems[1], sems[2], core_peer()),
    ]


def start_all(copies):
    for copy in copies:
        copy.start()


def wait_all(copies):
    for copy in copies:
        copy.wait()


def either(use_own, own, other, run):
    @pl.when(use_own)
    def _():
        run(own)

    @pl.when(jnp.logical_not(use_own))
    def _():
        run(other)


def weight_copies(refs, scratch, sems, expert):
    gate, up, down = refs
    gu_s, down_s = scratch
    width = gate.shape[2]
    return (
        pltpu.make_async_copy(gate.at[expert], gu_s.at[expert, :, pl.ds(0, width)], sems.at[0, expert]),
        pltpu.make_async_copy(up.at[expert], gu_s.at[expert, :, pl.ds(width, width)], sems.at[1, expert]),
        pltpu.make_async_copy(
            down.at[expert], down_s.at[pl.ds(pl.multiple_of(expert * width, width), width)], sems.at[2, expert]
        ),
    )


def attn_copies(refs, scratch, sems):
    query, key, value, output = refs
    joint_s, output_s = scratch
    qw, kw = query.shape[1], key.shape[1]
    return (
        pltpu.make_async_copy(query, joint_s.at[:, pl.ds(0, qw)], sems.at[0]),
        pltpu.make_async_copy(key, joint_s.at[:, pl.ds(qw, kw)], sems.at[1]),
        pltpu.make_async_copy(value, joint_s.at[:, pl.ds(qw + kw, kw)], sems.at[2]),
        pltpu.make_async_copy(output, output_s, sems.at[3]),
    )


def turned(block):
    lane = lax.broadcasted_iota(jnp.int32, block.shape, 1)
    half = HD // 2
    return jnp.where(
        lane % HD < half, pltpu.roll(block, block.shape[1] - half, 1), pltpu.roll(block, half, 1)
    )


def column(table, index):
    lane = lax.broadcasted_iota(jnp.int32, table.shape, 1)
    return jnp.sum(jnp.where(lane == index, table, 0.0), axis=1, keepdims=True)


def swap_copies(own, other, sems, piece):
    sends, recvs = sems
    names = len(own)
    if isinstance(piece, tuple):
        name, expert = piece
        source, target = own[name].at[expert], other[name].at[expert]
        index = 4 + (name - 4) * own[4].shape[0] + expert
    else:
        source, target, index = own[piece], other[piece], piece
    return pltpu.make_async_remote_copy(
        src_ref=source, dst_ref=target, send_sem=sends.at[index], recv_sem=recvs.at[index],
        device_id=core_peer(), device_id_type=MESH,
    )


def forward_kernel(layer, count, swap, *refs):
    refs = list(refs)

    def take(number):
        taken = refs[:number]
        del refs[:number]
        return taken

    (stream_in, attn_gains, expert_gains, routers, cosine, sine, bias, pickeds, kepts) = take(9)
    attn_gain, expert_gain, router = attn_gains.at[layer], expert_gains.at[layer], routers.at[layer]
    picked, kept = pickeds.at[layer], kepts.at[layer]
    stream = stream_in.at[lax.axis_index("section")] if layer == 0 else stream_in
    own = take(7)
    other = None if swap else take(7)
    (out, mid_out, expert_rows_out, qs_out, keys_out, values_out, probs_out, gate_out,
     attn_in_out, expert_in_out, gated_out, attended_out, pre_out) = take(13)
    if swap:
        other = take(7)
    scratch = take(4)
    joint_s, output_s, gu_s, down_s = scratch
    (ag1, ag2, part, landing1, landing2, pre_s, gated_s, attended_s, send_s, recv_s, attn_sems,
     expert_sems, pre_sems, save_sems) = refs[:14]
    swap_sems = refs[14:]
    rows, width = stream.shape
    tokens = ag1.shape[0]
    experts = gu_s.shape[0]
    hidden_width = gu_s.shape[2] // 2
    kw = keys_out.shape[1]
    qw = attended_s.shape[1]
    heads, key_heads = qw // HD, kw // HD
    group = heads // key_heads
    me = lax.axis_index("tensor")
    own_rows = pl.ds(pl.multiple_of(me * rows, rows), rows)
    use_own = lax.axis_index("section") == layer

    def start_attn(w):
        for copy in attn_copies(w[:4], scratch[:2], attn_sems):
            copy.start()

    def wait_attn(w):
        for copy in attn_copies(w[:4], scratch[:2], attn_sems):
            copy.wait()

    def start_expert(w, expert):
        for copy in weight_copies(w[4:], scratch[2:], expert_sems, expert):
            copy.start()

    def wait_expert(w, expert):
        for copy in weight_copies(w[4:], scratch[2:], expert_sems, expert):
            copy.wait()

    def each_expert(run):
        def step(expert, carry):
            run(expert)
            return carry

        lax.fori_loop(0, experts, step, 0)

    def swap_expert(expert):
        return [swap_copies(own, other, swap_sems, (name, expert)) for name in (4, 5, 6)]

    value = stream[...].astype(bf16).astype(f32)
    ag1[own_rows, :] = (value * norm_scale(value) * attn_gain[...]).astype(bf16)
    greet(tensor_peers(count) + ([core_peer()] if swap else []))
    first = spread(count, ag1, rows, send_s.at[0], recv_s.at[0])
    if swap:
        lead = min(2, experts)
        for piece in range(4):
            swap_copies(own, other, swap_sems, piece).start()
        each_expert(lambda expert: [c.start() for c in swap_expert(expert)] and None)

        @pl.when(use_own)
        def _():
            start_all(first)
            start_attn(own)
            each_expert(lambda expert: start_expert(own, expert))

        @pl.when(jnp.logical_not(use_own))
        def _():
            for piece in range(4):
                swap_copies(own, other, swap_sems, piece).wait_recv()
            start_attn(other)
            for expert in range(lead):
                for copy in swap_expert(expert):
                    copy.wait_recv()
                start_expert(other, expert)
            start_all(first)
    else:
        start_all(first)
        either(use_own, own, other, start_attn)
        either(use_own, own, other, lambda w: each_expert(lambda expert: start_expert(w, expert)))
    wait_all(first)
    saved = [pltpu.make_async_copy(ag1, attn_in_out, save_sems.at[0])]
    saved[0].start()
    either(use_own, own, other, wait_attn)
    proj = dot(ag1[...], joint_s[...], NN)
    for chunk in range(qw // 128):
        block = proj[:, chunk * 128 : chunk * 128 + 128]
        block = (block * cosine[...] + turned(block) * sine[...]).astype(bf16)
        for part_index in range(128 // HD):
            head = chunk * (128 // HD) + part_index
            qs_out[pl.ds(head * tokens, tokens), :] = block[:, part_index * HD : part_index * HD + HD]
    for chunk in range(kw // 128):
        block = proj[:, qw + chunk * 128 : qw + chunk * 128 + 128]
        keys_out[:, pl.ds(chunk * 128, 128)] = (
            block * cosine[...] + turned(block) * sine[...]
        ).astype(bf16)
    values_out[...] = proj[:, qw + kw :].astype(bf16)
    for g in range(key_heads):
        lanes = pl.ds(g * HD, HD)
        span = pl.ds(g * group * tokens, group * tokens)
        scores = dot(qs_out[span, :], keys_out[:, lanes], NT) * 0.125
        scores = (scores.reshape(group, tokens, tokens) + bias[...][None]).reshape(
            group * tokens, tokens
        )
        top = jnp.max(scores, axis=1, keepdims=True)
        weighed = jnp.exp(scores - top)
        probs = (weighed / jnp.sum(weighed, axis=1, keepdims=True)).astype(bf16)
        probs_out[span, :] = probs
        attended = dot(probs, values_out[:, lanes], NN).astype(bf16)
        for h in range(group):
            attended_s[:, pl.ds((g * group + h) * HD, HD)] = attended[h * tokens : (h + 1) * tokens]
    saved.append(pltpu.make_async_copy(attended_s, attended_out, save_sems.at[1]))
    saved[1].start()
    part[...] = dot(attended_s[...], output_s[...], NN).astype(bf16)
    dealt = deal_out(count, part, rows, slice(None), landing1, send_s.at[1], recv_s.at[1])
    wait_all(dealt)
    mid = value + part[own_rows, :].astype(f32)
    for step in range(count - 1):
        mid = mid + landing1[step].astype(f32)
    mid_out[...] = mid
    expert_rows = (mid * norm_scale(mid) * expert_gain[...]).astype(bf16)
    expert_rows_out[...] = expert_rows
    ag2[own_rows, :] = expert_rows
    second = spread(count, ag2, rows, send_s.at[2], recv_s.at[2])
    start_all(second)
    wait_all(second)
    saved.append(pltpu.make_async_copy(ag2, expert_in_out, save_sems.at[2]))
    saved[2].start()
    logits = dot(ag2[...], router[...], NN)
    chosen = picked[...] > 0
    top = jnp.max(jnp.where(chosen, logits, masked_score), axis=1, keepdims=True)
    weighed = jnp.where(chosen, jnp.exp(logits - top), 0.0)
    gate_out[...] = weighed / jnp.sum(weighed, axis=1, keepdims=True)

    def expert_step(expert, carry):
        if swap:

            @pl.when(jnp.logical_not(use_own) & (expert + lead < experts))
            def _():
                for copy in swap_expert(expert + lead):
                    copy.wait_recv()
                start_expert(other, expert + lead)

        either(use_own, own, other, lambda w: wait_expert(w, expert))
        pre = dot(ag2[...], gu_s[expert], NN)
        pre_s[expert] = pre
        pltpu.make_async_copy(pre_s.at[expert], pre_out.at[expert], pre_sems.at[expert]).start()
        gate_pre, up_pre = pre[:, :hidden_width], pre[:, hidden_width:]
        hidden = (gate_pre / (1.0 + jnp.exp(-gate_pre)) * up_pre).astype(bf16).astype(f32)
        weight = column(gate_out[...] * kept[...], expert)
        gated_s[:, pl.ds(pl.multiple_of(expert * hidden_width, hidden_width), hidden_width)] = (
            hidden * weight
        ).astype(bf16)
        return carry

    lax.fori_loop(0, experts, expert_step, 0)
    saved.append(pltpu.make_async_copy(gated_s, gated_out, save_sems.at[3]))
    saved[3].start()
    copies = []
    tile = width // 4
    for t in range(4):
        columns = pl.ds(t * tile, tile)
        part[:, columns] = dot(gated_s[...], down_s[:, columns], NN).astype(bf16)
        copies += deal_out(count, part, rows, columns, landing2, send_s.at[3 + t], recv_s.at[3 + t])
    wait_all(copies)
    total = mid_out[...] + part[own_rows, :].astype(f32)
    for step in range(count - 1):
        total = total + landing2[step].astype(f32)
    out[...] = total
    wait_all(saved)
    if swap:
        for piece in range(4):
            swap_copies(own, other, swap_sems, piece).wait_send()
        each_expert(lambda expert: [c.wait_send() for c in swap_expert(expert)] and None)

        @pl.when(use_own)
        def _():
            for piece in range(4):
                swap_copies(own, other, swap_sems, piece).wait_recv()
            each_expert(lambda expert: [c.wait_recv() for c in swap_expert(expert)] and None)

    def finish(expert, carry):
        pltpu.make_async_copy(pre_s.at[expert], pre_out.at[expert], pre_sems.at[expert]).wait()
        return carry

    lax.fori_loop(0, experts, finish, 0)


def weight_scratch(own):
    query, key, value, output, gate, up, down = own
    depth = query.shape[0]
    experts, _, hidden_width = gate.shape
    return [
        pltpu.VMEM((depth, query.shape[1] + 2 * key.shape[1]), bf16),
        pltpu.VMEM(output.shape, bf16),
        pltpu.VMEM((experts, depth, 2 * hidden_width), bf16),
        pltpu.VMEM((experts * hidden_width, depth), bf16),
    ]


def layer_forward(layer, gains, own, other, stream, tables, masks):
    count = lax.axis_size("tensor")
    rows, width = stream.shape[-2:]
    tokens = tables[2].shape[0]
    qw, kw = own[0].shape[1], own[1].shape[1]
    experts, _, hidden_width = own[4].shape
    heads = qw // HD
    swap = other is None
    vmem = pl.BlockSpec(memory_space=pltpu.VMEM)
    hbm = pl.BlockSpec(memory_space=pl.ANY)
    shape = jax.ShapeDtypeStruct
    pieces = 4 + 3 * experts
    found = pl.pallas_call(
        functools.partial(forward_kernel, layer, count, swap),
        name=f"layer_forward_{layer}",
        out_shape=(
            shape((rows, width), f32),
            shape((rows, width), f32),
            shape((rows, width), bf16),
            shape((heads * tokens, HD), bf16),
            shape((tokens, kw), bf16),
            shape((tokens, kw), bf16),
            shape((heads * tokens, tokens), bf16),
            shape((tokens, experts), f32),
            shape((tokens, width), bf16),
            shape((tokens, width), bf16),
            shape((tokens, experts * hidden_width), bf16),
            shape((tokens, qw), bf16),
            shape((experts, tokens, 2 * hidden_width), f32),
        )
        + (tuple(shape(w.shape, w.dtype) for w in own) if swap else ()),
        in_specs=[vmem] * 9 + [hbm] * (7 if swap else 14),
        out_specs=(vmem,) * 8 + (hbm,) * (12 if swap else 5),
        scratch_shapes=weight_scratch(own)
        + [
            pltpu.VMEM((tokens, width), bf16),
            pltpu.VMEM((tokens, width), bf16),
            pltpu.VMEM((tokens, width), bf16),
            pltpu.VMEM((count - 1, rows, width), bf16),
            pltpu.VMEM((count - 1, rows, width), bf16),
            pltpu.VMEM((experts, tokens, 2 * hidden_width), f32),
            pltpu.VMEM((tokens, experts * hidden_width), bf16),
            pltpu.VMEM((tokens, qw), bf16),
            dma((7, count - 1)),
            dma((7, count - 1)),
            dma((4,)),
            dma((3, experts)),
            dma((experts,)),
            dma((4,)),
        ]
        + ([dma((pieces,)), dma((pieces,))] if swap else []),
        compiler_params=params(1 + layer),
    )(stream, *gains, *tables, *masks, *own,
      *(() if swap else other))
    return found[:13], found[13:]


def norm_back(value, gain, out_grad):
    scale = norm_scale(value)
    scaled = value * scale
    gain_grad = jnp.sum(out_grad * scaled, axis=0, keepdims=True)
    inner = out_grad * gain
    value_grad = scale * (inner - scaled * jnp.mean(inner * scaled, axis=-1, keepdims=True))
    return value_grad, gain_grad


def experts_back_kernel(layer, count, beside, *refs):
    refs = list(refs)

    def take(number):
        taken = refs[:number]
        del refs[:number]
        return taken

    out_grad_in, mid, expert_gains, routers, kepts, gate, expert_rows, pre_in = take(8)
    expert_gain, router, kept = expert_gains.at[layer], routers.at[layer], kepts.at[layer]
    out_grad = out_grad_in if layer == 0 else out_grad_in.at[lax.axis_index("section")]
    x_in, gated_in = take(2)
    own, other = take(3), take(3)
    beside_in = take(len(beside.inputs))
    mid_grad_out, router_out, expert_gain_out, pair_out, down_out = take(5)
    beside_out = take(len(beside.outputs))
    scratch = take(2)
    gu_s, down_s = scratch
    (ag1, part, landing1, pre_s, gpu_s, acc, gate_part, gate_land, og_s, gpu_peer, x_s, turned_x,
     gated_s, turned_gated, pair_s, down_grad_s, send_s, recv_s, expert_sems, pre_sems, core_send,
     core_recv, local_sems, hand_send, hand_recv, save_sems) = take(26)
    beside_refs = (beside_in, beside_out, refs)
    rows, width = mid.shape
    experts = gu_s.shape[0]
    hidden_width = gu_s.shape[2] // 2
    me = lax.axis_index("tensor")
    own_rows = pl.ds(pl.multiple_of(me * rows, rows), rows)
    use_own = lax.axis_index("section") == layer

    def start_expert(expert, carry):
        either(use_own, own, other,
               lambda w: [c.start() for c in weight_copies(w, scratch, expert_sems, expert)])
        pltpu.make_async_copy(pre_in.at[expert], pre_s.at[expert], pre_sems.at[expert]).start()
        return carry

    ag1[own_rows, :] = out_grad[...].astype(bf16)
    greet(tensor_peers(count) + [core_peer()] + beside.peers())
    first = spread(count, ag1, rows, send_s.at[0], recv_s.at[0])
    start_all(first)
    lax.fori_loop(0, experts, start_expert, 0)
    loads = hand_halves(x_in, x_s, [v.at[0] for v in (local_sems, hand_send, hand_recv)])
    loads += hand_rows(gated_in, gated_s, [v.at[1] for v in (local_sems, hand_send, hand_recv)])
    for copy in loads:
        copy.start()
    beside.start(*beside_refs)
    gate_part[...] = jnp.zeros_like(gate_part)
    wait_all(loads)
    turned_x[...] = x_s[...].T
    tokens = ag1.shape[0]

    def turn_gated(expert, carry):
        lanes = pl.ds(pl.multiple_of(expert * hidden_width, hidden_width), hidden_width)
        turned_gated[lanes, :] = gated_s[:, lanes].T
        return carry

    lax.fori_loop(0, experts, turn_gated, 0)
    wait_all(first)
    core = lax.axis_index("section")
    half = width // 2
    og_s[pl.ds(0, tokens), :] = ag1[:, pl.ds(pl.multiple_of(core * half, half), half)]
    handed = [
        remote(ag1.at[:, pl.ds(pl.multiple_of((1 - core) * half, half), half)],
               og_s.at[pl.ds(tokens, tokens)], core_send.at[0], core_recv.at[0], core_peer())
    ]
    handed[0].start()

    def expert_step(expert, carry):
        either(use_own, own, other,
               lambda w: [c.wait() for c in weight_copies(w, scratch, expert_sems, expert)])
        pltpu.make_async_copy(pre_in.at[expert], pre_s.at[expert], pre_sems.at[expert]).wait()
        lanes = pl.ds(pl.multiple_of(expert * hidden_width, hidden_width), hidden_width)
        plain = dot(ag1[...], down_s[lanes, :], NT)
        gate_pre = pre_s[expert, :, pl.ds(0, hidden_width)]
        up_pre = pre_s[expert, :, pl.ds(hidden_width, hidden_width)]
        sig = 1.0 / (1.0 + jnp.exp(-gate_pre))
        act = gate_pre * sig
        hidden = (act * up_pre).astype(bf16).astype(f32)
        held = column(kept[...], expert)
        weight = column(gate[...], expert) * held
        summed = jnp.sum(hidden * plain, axis=1, keepdims=True) * held
        lane = lax.broadcasted_iota(jnp.int32, gate_part.shape, 1)
        gate_part[...] += jnp.where(lane == expert, summed, 0.0)
        hidden_grad = plain * weight
        gpu_s[expert, :, pl.ds(0, hidden_width)] = (
            hidden_grad * up_pre * (sig * (1.0 + gate_pre * (1.0 - sig)))
        ).astype(bf16)
        gpu_s[expert, :, pl.ds(hidden_width, hidden_width)] = (hidden_grad * act).astype(bf16)
        back = dot(gpu_s[expert], gu_s[expert], NT)

        @pl.when(expert == 0)
        def _():
            acc[...] = back

        @pl.when(expert > 0)
        def _():
            acc[...] += back

        return carry

    lax.fori_loop(0, experts, expert_step, 0)
    handed.append(remote(gpu_s, gpu_peer, core_send.at[1], core_recv.at[1], core_peer()))
    handed[1].start()
    part[...] = acc[...].astype(bf16)
    copies = deal_out(count, part, rows, slice(None), landing1, send_s.at[1], recv_s.at[1])
    copies += deal_out(count, gate_part, rows, slice(None), gate_land, send_s.at[2], recv_s.at[2])
    wait_all(handed)

    def saves(expert):
        lanes = pl.ds(pl.multiple_of(expert * hidden_width, hidden_width), hidden_width)
        return (
            pltpu.make_async_copy(pair_s.at[expert], pair_out.at[expert], save_sems.at[0, expert]),
            pltpu.make_async_copy(down_grad_s.at[lanes], down_out.at[expert], save_sems.at[1, expert]),
        )

    def grads_step(expert, carry):
        lanes = pl.ds(pl.multiple_of(expert * hidden_width, hidden_width), hidden_width)
        pair_s[expert] = (
            dot(turned_x[:, :tokens], gpu_s[expert], NN)
            + dot(turned_x[:, tokens:], gpu_peer[expert], NN)
        ).astype(bf16)
        down_grad_s[lanes, :] = dot(turned_gated[lanes, :], og_s[...], NN).astype(bf16)
        for copy in saves(expert):
            copy.start()
        return carry

    lax.fori_loop(0, experts, grads_step, 0)
    wait_all(copies)
    in_grad = acc[own_rows, :]
    gate_grad = gate_part[own_rows, :]
    for step in range(count - 1):
        in_grad = in_grad + landing1[step].astype(f32)
        gate_grad = gate_grad + gate_land[step]
    gate_grad = gate_grad[:, :experts]
    gate_rows = gate[own_rows, :]
    logits_grad = (
        gate_rows * (gate_grad - jnp.sum(gate_rows * gate_grad, axis=1, keepdims=True))
    ).astype(bf16)
    router_out[...] = dot(logits_grad, expert_rows[...], TN)
    in_grad = in_grad + dot(logits_grad, router[...], NT)
    mid_part, expert_gain_grad = norm_back(mid[...], expert_gain[...], in_grad)
    expert_gain_out[...] = expert_gain_grad
    mid_grad_out[...] = ag1[own_rows, :].astype(f32) + mid_part

    def finish_save(expert, carry):
        for copy in saves(expert):
            copy.wait()
        return carry

    lax.fori_loop(0, experts, finish_save, 0)
    beside.wait(*beside_refs)


def experts_back(layer, gains, own, other, out_grad, state, pairs, masks, beside):
    count = lax.axis_size("tensor")
    mid, gate, expert_rows, pre = state
    rows, width = mid.shape
    tokens = gate.shape[0]
    own, other = own[4:], other[4:]
    experts, depth, hidden_width = own[0].shape
    vmem = pl.BlockSpec(memory_space=pltpu.VMEM)
    hbm = pl.BlockSpec(memory_space=pl.ANY)
    shape = jax.ShapeDtypeStruct
    found = pl.pallas_call(
        functools.partial(experts_back_kernel, layer, count, beside),
        name=f"experts_back_{layer}",
        out_shape=(
            shape((rows, width), f32),
            shape((experts, width), f32),
            shape((1, width), f32),
            shape((experts, width // 2, 2 * hidden_width), bf16),
            shape((experts, hidden_width, width // 2), bf16),
            *beside.outputs,
        ),
        in_specs=[vmem] * 7 + [hbm] * (9 + len(beside.inputs)),
        out_specs=(vmem, vmem, vmem, hbm, hbm) + (hbm,) * len(beside.outputs),
        scratch_shapes=[
            pltpu.VMEM((experts, depth, 2 * hidden_width), bf16),
            pltpu.VMEM((experts * hidden_width, depth), bf16),
            pltpu.VMEM((tokens, width), bf16),
            pltpu.VMEM((tokens, width), bf16),
            pltpu.VMEM((count - 1, rows, width), bf16),
            pltpu.VMEM((experts, tokens, 2 * hidden_width), f32),
            pltpu.VMEM((experts, tokens, 2 * hidden_width), bf16),
            pltpu.VMEM((tokens, width), f32),
            pltpu.VMEM((tokens, 128), f32),
            pltpu.VMEM((count - 1, rows, 128), f32),
            pltpu.VMEM((2 * tokens, width // 2), bf16),
            pltpu.VMEM((experts, tokens, 2 * hidden_width), bf16),
            pltpu.VMEM((2 * tokens, width // 2), bf16),
            pltpu.VMEM((width // 2, 2 * tokens), bf16),
            pltpu.VMEM((2 * tokens, experts * hidden_width), bf16),
            pltpu.VMEM((experts * hidden_width, 2 * tokens), bf16),
            pltpu.VMEM((experts, width // 2, 2 * hidden_width), bf16),
            pltpu.VMEM((experts * hidden_width, width // 2), bf16),
            pltpu.SemaphoreType.DMA((3, count - 1)),
            pltpu.SemaphoreType.DMA((3, count - 1)),
            pltpu.SemaphoreType.DMA((3, experts)),
            pltpu.SemaphoreType.DMA((experts,)),
            *[pltpu.SemaphoreType.DMA((2,)) for _ in range(5)],
            pltpu.SemaphoreType.DMA((2, experts)),
            *beside.sems,
        ],
        compiler_params=params(3 + layer),
    )(out_grad, mid, *gains[1:], masks[1], gate, expert_rows, pre, *pairs, *own, *other,
      *beside.inputs)
    return found[:5], beside.results(found[5:])


def attention_back_kernel(layer, count, beside, *refs):
    refs = list(refs)

    def take(number):
        taken = refs[:number]
        del refs[:number]
        return taken

    mid_grad, stream_in, attn_gains, cosine, sine, qs, keys, values, probs = take(9)
    attn_gain = attn_gains.at[layer]
    stream = stream_in.at[lax.axis_index("section")] if layer == 0 else stream_in
    ai_in, attended_in = take(2)
    own, other = take(4), take(4)
    beside_in = take(len(beside.inputs))
    grad_out, attn_gain_out, dense_out = take(3)
    beside_out = take(len(beside.outputs))
    scratch = take(2)
    joint_s, output_s = scratch
    (ag2, part, landing2, ag_stack, dq_s, joint_rows, joint_peer, ao_s, ai_s, turned_ai, attended_s,
     dense_s, send_s, recv_s, attn_sems, core_send, core_recv, local_sems,
     hand_send, hand_recv) = take(20)
    beside_refs = (beside_in, beside_out, refs)
    rows, width = stream.shape
    tokens = ag2.shape[0]
    kw = keys.shape[1]
    qw = output_s.shape[0]
    heads, key_heads = qw // HD, kw // HD
    group = heads // key_heads
    me = lax.axis_index("tensor")
    own_rows = pl.ds(pl.multiple_of(me * rows, rows), rows)
    use_own = lax.axis_index("section") == layer
    ag2[own_rows, :] = mid_grad[...].astype(bf16)
    greet(tensor_peers(count) + [core_peer()] + beside.peers())
    first = spread(count, ag2, rows, send_s.at[0], recv_s.at[0])
    start_all(first)
    either(use_own, own, other, lambda w: [c.start() for c in attn_copies(w, scratch, attn_sems)])
    loads = hand_halves(ai_in, ai_s, [v.at[0] for v in (local_sems, hand_send, hand_recv)])
    loads += hand_rows(attended_in, attended_s, [v.at[1] for v in (local_sems, hand_send, hand_recv)])
    for copy in loads:
        copy.start()
    beside.start(*beside_refs)
    wait_all(loads)
    turned_ai[...] = ai_s[...].T
    wait_all(first)
    core = lax.axis_index("section")
    half = width // 2
    ao_s[pl.ds(0, tokens), :] = ag2[:, pl.ds(pl.multiple_of(core * half, half), half)]
    handed = [
        remote(ag2.at[:, pl.ds(pl.multiple_of((1 - core) * half, half), half)],
               ao_s.at[pl.ds(tokens, tokens)], core_send.at[0], core_recv.at[0], core_peer())
    ]
    handed[0].start()
    either(use_own, own, other, lambda w: [c.wait() for c in attn_copies(w, scratch, attn_sems)])
    attended_grad = dot(ag2[...], output_s[...], NT).astype(bf16)
    for h in range(heads):
        ag_stack[pl.ds(h * tokens, tokens), :] = attended_grad[:, h * HD : (h + 1) * HD]
    for g in range(key_heads):
        lanes = pl.ds(g * HD, HD)
        span = pl.ds(g * group * tokens, group * tokens)
        soft_b = probs[span, :]
        soft = soft_b.astype(f32)
        soft_grad = dot(ag_stack[span, :], values[:, lanes], NT)
        inner = jnp.sum(soft * soft_grad, axis=1, keepdims=True)
        score_grad = (soft * (soft_grad - inner)).astype(bf16)
        dq = dot(score_grad, keys[:, lanes], NN) * 0.125
        for h in range(group):
            dq_s[:, pl.ds((g * group + h) * HD, HD)] = dq[h * tokens : (h + 1) * tokens]
        dq_s[:, pl.ds(qw + g * HD, HD)] = dot(score_grad, qs[span, :], TN) * 0.125
        joint_rows[:, pl.ds(qw + kw + g * HD, HD)] = dot(soft_b, ag_stack[span, :], TN).astype(bf16)
    for chunk in range((qw + kw) // 128):
        lanes = pl.ds(chunk * 128, 128)
        block = dq_s[:, lanes]
        joint_rows[:, lanes] = (block * cosine[...] - turned(block) * sine[...]).astype(bf16)
    handed.append(remote(joint_rows, joint_peer, core_send.at[1], core_recv.at[1], core_peer()))
    handed[1].start()
    copies = []
    tile = width // 2
    for t in range(2):
        columns = pl.ds(t * tile, tile)
        part[:, columns] = dot(joint_rows[...], joint_s[columns, :], NT).astype(bf16)
        copies += deal_out(count, part, rows, columns, landing2, send_s.at[1 + t], recv_s.at[1 + t])
    wait_all(handed)
    wide = qw + 2 * kw
    dense_s[:, :wide] = (
        dot(turned_ai[:, :tokens], joint_rows[...], NN) + dot(turned_ai[:, tokens:], joint_peer[...], NN)
    ).astype(bf16)
    dense_s[:, wide:] = dot(ao_s[...], attended_s[...], TN).astype(bf16)
    save = pltpu.make_async_copy(dense_s, dense_out, local_sems.at[0])
    save.start()
    wait_all(copies)
    in_grad = part[own_rows, :].astype(f32)
    for step in range(count - 1):
        in_grad = in_grad + landing2[step].astype(f32)
    stream_part, attn_gain_grad = norm_back(
        stream[...].astype(bf16).astype(f32), attn_gain[...], in_grad
    )
    attn_gain_out[...] = attn_gain_grad
    grad_out[...] = mid_grad[...] + stream_part
    save.wait()
    beside.wait(*beside_refs)


def attention_back(layer, gains, own, other, mid_grad, stream, state, pairs, tables, beside):
    count = lax.axis_size("tensor")
    qs, keys, values, probs = state
    rows, width = mid_grad.shape
    tokens = keys.shape[0]
    own, other = own[:4], other[:4]
    qw, kw = own[0].shape[1], own[1].shape[1]
    heads = qw // HD
    vmem = pl.BlockSpec(memory_space=pltpu.VMEM)
    hbm = pl.BlockSpec(memory_space=pl.ANY)
    shape = jax.ShapeDtypeStruct
    found = pl.pallas_call(
        functools.partial(attention_back_kernel, layer, count, beside),
        name=f"attention_back_{layer}",
        out_shape=(
            shape((rows, width), f32),
            shape((1, width), f32),
            shape((width // 2, 2 * qw + 2 * kw), bf16),
            *beside.outputs,
        ),
        in_specs=[vmem] * 9 + [hbm] * (10 + len(beside.inputs)),
        out_specs=(vmem, vmem, hbm) + (hbm,) * len(beside.outputs),
        scratch_shapes=[
            pltpu.VMEM((width, qw + 2 * kw), bf16),
            pltpu.VMEM((qw, width), bf16),
            pltpu.VMEM((tokens, width), bf16),
            pltpu.VMEM((tokens, width), bf16),
            pltpu.VMEM((count - 1, rows, width), bf16),
            pltpu.VMEM((heads * tokens, HD), bf16),
            pltpu.VMEM((tokens, qw + kw), f32),
            pltpu.VMEM((tokens, qw + 2 * kw), bf16),
            pltpu.VMEM((tokens, qw + 2 * kw), bf16),
            pltpu.VMEM((2 * tokens, width // 2), bf16),
            pltpu.VMEM((2 * tokens, width // 2), bf16),
            pltpu.VMEM((width // 2, 2 * tokens), bf16),
            pltpu.VMEM((2 * tokens, qw), bf16),
            pltpu.VMEM((width // 2, 2 * qw + 2 * kw), bf16),
            pltpu.SemaphoreType.DMA((3, count - 1)),
            pltpu.SemaphoreType.DMA((3, count - 1)),
            pltpu.SemaphoreType.DMA((4,)),
            *[pltpu.SemaphoreType.DMA((2,)) for _ in range(5)],
            *beside.sems,
        ],
        compiler_params=params(5 + layer),
    )(mid_grad, stream, gains[0], *tables[:2], qs, keys, values, probs, *pairs, *own, *other,
      *beside.inputs)
    return found[:3], beside.results(found[3:])


def finish_kernel(bring, beside, *refs):
    refs = list(refs)

    def take(number):
        taken = refs[:number]
        del refs[:number]
        return taken

    *small_parts, dense = take(7)
    beside_in = take(len(beside.inputs))
    small_out, whole_out, *beside_out = take(2 + len(beside.outputs))
    (landing, block, small_z, small_dp, small_core, small_sum, small_mid, small_last, small_whole,
     sends, recvs, local_sems, z_sends, z_recvs, dp_sends, dp_recvs, core_sends,
     core_recvs, small) = take(19)
    bring_sems = take(len(bring.sems))
    beside_refs = (beside_in, beside_out, refs)
    count = dense.shape[0]
    tensor = small_z.shape[0] + 1
    lanes = small_z.shape[2]
    me = lax.axis_index("dp")
    here = lax.axis_index("tensor")
    groups = [{"dp": lax.rem(me + step, count)} for step in range(1, count)]
    greet(both_cores([group["dp"] for group in groups]) + tensor_peers(tensor) + [core_peer()])

    def launch(*args):
        copy = remote(*args)
        copy.start()
        return copy

    def columns(place):
        return pl.ds(pl.multiple_of(place * lanes, lanes), lanes)

    place = 0
    for index, value in enumerate(small_parts):
        if index % 3 == 0:
            place = index // 3 * (small.shape[0] // 2)
        small[pl.ds(place, value.shape[0]), :] = value[...]
        place += value.shape[0]
    first = []
    for step in range(1, tensor):
        place = lax.rem(here + step, tensor)
        first.append(
            launch(small.at[:, columns(place)], small_z.at[step - 1], z_sends.at[0, step - 1],
                   z_recvs.at[0, step - 1], {"tensor": place})
        )
    copies = []
    for step in range(1, count):
        place = lax.rem(me + step, count)
        copies.append(
            launch(dense.at[place], landing.at[step - 1], sends.at[0, step - 1],
                   recvs.at[0, step - 1], {"dp": place})
        )
    beside.start(*beside_refs)
    mine = pltpu.make_async_copy(dense.at[me], block, local_sems.at[0])
    mine.start()
    wait_all(first)
    total = small[:, columns(here)]
    for step in range(tensor - 1):
        total = total + small_z[step]
    small_sum[...] = total
    second = [
        launch(small_sum, small_dp.at[step], dp_sends.at[step], dp_recvs.at[step], groups[step])
        for step in range(count - 1)
    ]
    mine.wait()
    wait_all(copies)
    total = block[...].astype(f32)
    for step in range(count - 1):
        total = total + landing[step].astype(f32)
    block[...] = total.astype(bf16)
    bring.start([block], [whole_out], bring_sems)
    wait_all(second)
    total = small_sum[...]
    for step in range(count - 1):
        total = total + small_dp[step]
    small_mid[...] = total
    third = launch(small_mid, small_core, core_sends.at[0], core_recvs.at[0], core_peer())
    third.wait()
    small_last[...] = small_mid[...] + small_core[...]
    last = [
        launch(small_last, small_whole.at[:, columns(here)], z_sends.at[1, step - 1],
               z_recvs.at[1, step - 1], {"tensor": lax.rem(here + step, tensor)})
        for step in range(1, tensor)
    ]
    small_whole[:, columns(here)] = small_last[...]
    wait_all(last)
    small_out[...] = small_whole[...]
    bring.wait([block], [whole_out], bring_sems)
    beside.wait(*beside_refs)


def finish(small_parts, dense, layer, beside):
    count = lax.axis_size("dp")
    tensor = lax.axis_size("tensor")
    rows = dense.shape[0] // count
    depth = -(-sum(v.shape[0] for v in small_parts[:3]) // 8) * 8
    small = jax.ShapeDtypeStruct((2 * depth, small_parts[0].shape[1]), f32)
    lanes = small.shape[1] // tensor
    hbm = pl.BlockSpec(memory_space=pl.ANY)
    vmem = pl.BlockSpec(memory_space=pltpu.VMEM)
    bring = Bring(layer, "all", jax.ShapeDtypeStruct((rows, dense.shape[1]), bf16), True)
    found = pl.pallas_call(
        functools.partial(finish_kernel, bring, beside),
        name="finish",
        out_shape=(
            jax.ShapeDtypeStruct(small.shape, f32),
            *bring.outputs,
            *beside.outputs,
        ),
        in_specs=[vmem] * 6 + [hbm] * (1 + len(beside.inputs)),
        out_specs=(vmem,) + (hbm,) * (1 + len(beside.outputs)),
        scratch_shapes=[
            pltpu.VMEM((count - 1, rows, dense.shape[1]), bf16),
            pltpu.VMEM((rows, dense.shape[1]), bf16),
            pltpu.VMEM((tensor - 1, small.shape[0], lanes), f32),
            pltpu.VMEM((count - 1, small.shape[0], lanes), f32),
            pltpu.VMEM((small.shape[0], lanes), f32),
            pltpu.VMEM((small.shape[0], lanes), f32),
            pltpu.VMEM((small.shape[0], lanes), f32),
            pltpu.VMEM((small.shape[0], lanes), f32),
            pltpu.VMEM(small.shape, f32),
            dma((1, count - 1)),
            dma((1, count - 1)),
            dma((1,)),
            dma((2, tensor - 1)),
            dma((2, tensor - 1)),
            dma((count - 1,)),
            dma((count - 1,)),
            dma((1,)),
            dma((1,)),
            pltpu.VMEM(small.shape, f32),
            *bring.sems,
            *beside.sems,
        ],
        compiler_params=params(7),
    )(*small_parts, dense.reshape(count, rows, dense.shape[1]), *beside.inputs)
    return found[0], found[1], beside.results(found[2:])


def prepare_kernel(lengths, dealing, order, routes, attn_gain, expert_gain, router, freqs,
                   cosine, sine, bias, picked, kept, attn_gains, expert_gains, routers,
                   order_peer, routes_peer, sends, recvs):
    core = lax.axis_index("section")
    attn_gains[core] = attn_gain[...]
    expert_gains[core] = expert_gain[...]
    routers[core] = router[...]
    greet([core_peer()])
    copies = [
        remote(source, target, sends.at[index], recvs.at[index], core_peer())
        for index, (source, target) in enumerate((
            (order.at[1 - core], order_peer),
            (routes.at[1 - core], routes_peer),
            (attn_gain, attn_gains.at[core]),
            (expert_gain, expert_gains.at[core]),
            (router, routers.at[core]),
        ))
    ]
    start_all(copies)
    tokens = bias.shape[0]
    sequences = lengths.shape[1]
    tall = lax.broadcasted_iota(jnp.int32, (tokens, 1), 0)
    wide = lax.broadcasted_iota(jnp.int32, (1, tokens), 1)
    sizes = [lengths[core, index] for index in range(sequences)]
    starts = [sum(sizes[:index], 0) for index in range(sequences)]
    ranks = [
        sum(jnp.where(dealing[core, place] == index, place, 0) for place in range(sequences))
        for index in range(sequences)
    ]
    dealt_starts = [
        sum(jnp.where(ranks[before] < ranks[index], sizes[before], 0) for before in range(sequences))
        for index in range(sequences)
    ]

    def places(token):
        segment = sum((token >= starts[index] + sizes[index]).astype(jnp.int32)
                      for index in range(sequences))
        position, dealt = token, token
        for index in range(sequences):
            inside = segment == index
            position = jnp.where(inside, token - starts[index], position)
            dealt = jnp.where(inside, token - starts[index] + dealt_starts[index], dealt)
        return segment, position, dealt

    segment, position, dealt = places(tall)
    segment_wide, _, dealt_wide = places(wide)
    allowed = (segment == segment_wide) & (wide <= tall)
    bias[...] = jnp.where(allowed, 0.0, masked_score).astype(f32)
    angles = position.astype(f32) * freqs[...]
    cosine[...] = jnp.cos(angles)
    lane = lax.broadcasted_iota(jnp.int32, (1, freqs.shape[1]), 1)
    sine[...] = jnp.sin(angles) * jnp.where(lane % HD < HD // 2, -1.0, 1.0)

    def masks(order_row, route_rows):
        order_wide = order_row.astype(f32)
        order_tall = jnp.sum(jnp.where(tall == wide, order_wide, 0.0), axis=1, keepdims=True)
        first = jnp.sum(jnp.where(dealt == wide, order_wide, 0.0), axis=1, keepdims=True)
        first_wide = jnp.sum(jnp.where(dealt_wide == tall, order_tall, 0.0), axis=0, keepdims=True)
        earlier = jnp.where(first_wide < first, 1.0, 0.0).astype(bf16)
        experts = picked.shape[2]
        index = lax.broadcasted_iota(jnp.int32, (tokens, experts), 1)
        chosen = jnp.zeros((tokens, experts), f32)
        for k in range(route_rows.shape[1]):
            chosen = jnp.where(route_rows[:, k : k + 1] == index, 1.0, chosen)
        rank = dot(earlier, chosen.astype(bf16), NN)
        return chosen, jnp.where(rank < CAP, chosen, 0.0)

    picked[core], kept[core] = masks(order[core], routes[core])
    wait_all(copies)
    picked[1 - core], kept[1 - core] = masks(order_peer[...], routes_peer[...])


def prepare(lengths, dealing, order, routes, attn_gain, expert_gain, router):
    tokens = order.shape[2]
    width = attn_gain.shape[1]
    half = HD // 2
    freqs = jnp.tile(rope_base ** (-2.0 * jnp.arange(half, dtype=f32) / HD), 128 // half)[None]
    vmem = pl.BlockSpec(memory_space=pltpu.VMEM)
    smem = pl.BlockSpec(memory_space=pltpu.SMEM)
    shape = jax.ShapeDtypeStruct
    found = pl.pallas_call(
        prepare_kernel,
        name="prepare",
        out_shape=(
            shape((tokens, 128), f32),
            shape((tokens, 128), f32),
            shape((tokens, tokens), f32),
            shape((2, tokens, E), f32),
            shape((2, tokens, E), f32),
            shape((2, 1, width), f32),
            shape((2, 1, width), f32),
            shape((2, *router.shape), bf16),
        ),
        in_specs=[smem] * 2 + [vmem] * 6,
        out_specs=(vmem,) * 8,
        scratch_shapes=[
            pltpu.VMEM(order.shape[1:], order.dtype),
            pltpu.VMEM(routes.shape[1:], routes.dtype),
            dma((5,)),
            dma((5,)),
        ],
        compiler_params=params(8),
    )(lengths, dealing, order, routes, attn_gain, expert_gain, router, freqs)
    return found[:3], found[3:5], found[5:]


def assemble_kernel(section, *refs):
    expert_refs, dense_refs, outs = (refs[:4], refs[4:8]), refs[8:10], refs[10:]
    query, key, value, output, gate, up, down = outs
    hidden_width = gate.shape[2]
    qw, kw = query.shape[1], key.shape[1]

    def write(parts, dense):
        cores = range(2)
        pair = [[jnp.sum(v[core, :, 0].astype(f32), axis=0) for v in parts[:2]] for core in cores]
        depth = 0
        for block in pair[0] + pair[1]:
            rows = pl.ds(depth, block.shape[0])
            gate[0, rows, :] = block[:, :hidden_width]
            up[0, rows, :] = block[:, hidden_width:]
            depth += block.shape[0]
        depth = 0
        for core in cores:
            for v in parts[2:]:
                block = jnp.sum(v[core, :, 0].astype(f32), axis=0)
                down[0, :, pl.ds(depth, block.shape[1])] = block
                depth += block.shape[1]
        rows = dense[...].astype(f32)
        query[...] = rows[:, :qw]
        key[...] = rows[:, qw : qw + kw]
        value[...] = rows[:, qw + kw : qw + 2 * kw]
        output[...] = rows[:, qw + 2 * kw :].T

    pl.when(section[0] == 0)(lambda: write(expert_refs[0], dense_refs[0]))
    pl.when(section[0] == 1)(lambda: write(expert_refs[1], dense_refs[1]))


def assemble(parts, denses, qw, kw):
    groups = parts[0][0].shape[2]
    hidden_width = parts[0][2].shape[3]
    dense = [v.reshape(-1, v.shape[3]) for v in denses]
    depth = dense[0].shape[0]
    rows = depth // groups

    def part_spec(layer, shape):
        block = (*shape[:2], 1, *shape[3:])
        return pl.BlockSpec(block, lambda e, s: (0, 0, jnp.where(s[0] == layer, e, 0), 0, 0))

    def dense_spec(layer, width):
        return pl.BlockSpec((rows, width), lambda e, s: (jnp.where(s[0] == layer, e, 0), 0))

    shape = jax.ShapeDtypeStruct
    return pl.pallas_call(
        assemble_kernel,
        name="assemble",
        out_shape=(
            shape((depth, qw), f32),
            shape((depth, kw), f32),
            shape((depth, kw), f32),
            shape((qw, depth), f32),
            shape((groups, depth, hidden_width), f32),
            shape((groups, depth, hidden_width), f32),
            shape((groups, hidden_width, depth), f32),
        ),
        grid_spec=pltpu.PrefetchScalarGridSpec(
            num_scalar_prefetch=1,
            grid=(groups,),
            in_specs=[part_spec(layer, v.shape) for layer in range(2) for v in parts[layer]]
            + [dense_spec(layer, dense[layer].shape[1]) for layer in range(2)],
            out_specs=(
                pl.BlockSpec((rows, qw), lambda e, s: (e, 0)),
                pl.BlockSpec((rows, kw), lambda e, s: (e, 0)),
                pl.BlockSpec((rows, kw), lambda e, s: (e, 0)),
                pl.BlockSpec((qw, rows), lambda e, s: (0, e)),
                pl.BlockSpec((1, depth, hidden_width), lambda e, s: (e, 0, 0)),
                pl.BlockSpec((1, depth, hidden_width), lambda e, s: (e, 0, 0)),
                pl.BlockSpec((1, hidden_width, depth), lambda e, s: (e, 0, 0)),
            ),
        ),
        compiler_params=pltpu.CompilerParams(vmem_limit_bytes=48 * 2**20),
    )(lax.axis_index("section").astype(jnp.int32)[None], *parts[0], *parts[1], *dense)


def shards(
    tokens_in, out_cotangent, attn_gain, query_weight, key_weight, value_weight, output_weight,
    expert_gain, router_weight, gate_weight, up_weight, down_weight, lengths, dealing,
    slot_order, routes,
):
    first = lax.axis_index("section") == 0
    qw, kw = query_weight.shape[2], key_weight.shape[2]
    own = (query_weight[0], key_weight[0], value_weight[0], output_weight[0], gate_weight[0],
           up_weight[0], down_weight[0])
    tables, masks, gains = prepare(lengths[:, 0], dealing[:, 0], slot_order[0], routes[0], attn_gain,
                                   expert_gain, router_weight[0])
    (out0, *state0), other = layer_forward(0, gains, own, None, tokens_in, tables, masks)
    (out1, *state1), _ = layer_forward(1, gains, own, other, out0, tables, masks)
    saved = (state0, state1)
    streams = (tokens_in, out0)

    def experts(layer, out_grad, jobs):
        mid, expert_rows, qs, keys, values, probs, gate, ai, x, gated, attended, pre = saved[layer]
        (mid_grad, router_part, gain_part, pair, down), done = experts_back(
            layer, gains, own, other, out_grad, (mid, gate, expert_rows, pre), (x, gated), masks,
            Beside(jobs)
        )
        return mid_grad, (gain_part, router_part), [FirstStage(pair, 1), FirstStage(down, 2)], done

    def attention(layer, mid_grad, jobs):
        mid, expert_rows, qs, keys, values, probs, gate, ai, x, gated, attended, pre = saved[layer]
        (grad, gain_part, dense), done = attention_back(
            layer, gains, own, other, mid_grad, streams[layer], (qs, keys, values, probs),
            (ai, attended), tables, Beside(jobs)
        )
        return grad, gain_part, dense, done

    def second(layer, sums):
        return [Bring(layer, kind, v) for pair in sums for kind, v in zip(("column", "row"), pair)]

    mid_grad, small1, stage, _ = experts(1, out_cotangent, [])
    grad1, gain1, dense1, sums = attention(1, mid_grad, stage)
    mid_grad, small0, stage, (*parts1, dense1) = experts(
        0, grad1.astype(bf16), second(1, sums) + [Scatter(dense1)]
    )
    grad0, gain0, dense0, (*sums, dense1) = attention(
        0, mid_grad, stage + [Bring(1, "all", dense1)]
    )
    small, dense0, parts0 = finish(
        (small0[1], gain0, small0[0], small1[1], gain1, small1[0]), dense0, 0, Beside(second(0, sums))
    )

    def by_layer(zero, one):
        mine = jnp.where(first, zero, one)
        theirs = swapped(jnp.where(first, one, zero))
        return jnp.where(first, jnp.stack([mine, theirs]), jnp.stack([theirs, mine]))[None]

    layer_outputs = by_layer(out0, out1)
    input_grads = by_layer(grad0, grad1)

    query, key, value, output, gate, up, down = assemble((parts0, parts1), (dense0, dense1), qw, kw)
    small = jnp.where(first, small[: small.shape[0] // 2], small[small.shape[0] // 2 :])
    router_grad, attn_gain_grad, expert_gain_grad = small[:E].T, small[E : E + 1], small[E + 1 : E + 2]
    return (
        layer_outputs,
        input_grads,
        attn_gain_grad,
        query[None],
        key[None],
        value[None],
        output[None],
        expert_gain_grad,
        router_grad[None],
        gate[None],
        up[None],
        down[None],
    )


def solution(mesh):
    return jax.shard_map(
        shards,
        mesh=mesh,
        in_specs=(
            P(None, ("dp", "tensor"), None),
            P(None, ("dp", "tensor"), None),
            P("section", None),
            P("section", None, "tensor"),
            P("section", None, "tensor"),
            P("section", None, "tensor"),
            P("section", "tensor", None),
            P("section", None),
            P("section", None, None),
            P("section", None, None, "tensor"),
            P("section", None, None, "tensor"),
            P("section", None, "tensor", None),
            P(None, "dp", None),
            P(None, "dp", None),
            P("section", None, "dp", None),
            P("section", None, "dp", None),
        ),
        out_specs=(
            P("section", None, ("dp", "tensor"), None),
            P("section", None, ("dp", "tensor"), None),
            P("section", None),
            P("section", None, "tensor"),
            P("section", None, "tensor"),
            P("section", None, "tensor"),
            P("section", "tensor", None),
            P("section", None),
            P("section", None, None),
            P("section", "dp", None, "tensor"),
            P("section", "dp", None, "tensor"),
            P("section", "dp", "tensor", None),
        ),
        check_vma=False,
    )
```

time: 623 us -> 560 us (0.90)
  local copies, waits for them, and re-layouts: 53.6 us -> 7.99 us
  Pallas kernels: 519 us -> 504 us
  other arithmetic: 37.4 us -> 27.3 us
  starting transfers between devices: 2.44 us -> 11.8 us
    unnamed x135 -> x32, local copies, waits for them, and re-layouts: 26.9 us -> 6.14 us
    pallas_call x2, Pallas kernels: 176 us -> 157 us  [layer_forward(): pl.pallas_call(functools.partial(forward_kernel, layer, count, swap), nam...]
    split x4 -> x0, local copies, waits for them, and re-layouts: 10.6 us -> none  [sums(): first, second = jnp.split(value, 2, axis=2 + self.axis)]
    ppermute x10 -> x2, starting transfers between devices: 2.44 us -> 11.8 us  [swapped(): return lax.ppermute(value, 'section', [(0, 1), (1, 0)])]
    broadcast_in_dim x5 -> x0, local copies, waits for them, and re-layouts: 6.84 us -> none  [the longest x1 3.12 us: shards(): up[None]]
    convert_element_type x17 -> x8, other arithmetic: 22.8 us -> 17 us  [results(): return (row.astype(bf16), col.astype(bf16))]
    pallas_call x5 -> x3, Pallas kernels: 88.4 us -> 89.8 us  [the longest x1 73.7 us: finish(): pl.pallas_call(functools.partial(finish_kernel, bring, beside), name='fin...]
  transfers between devices with their start and end apart: 10 -> 2, of which waited for: 0 -> 0; matrix products, arithmetic and copies ran while one was open for 4% -> 5% of each run, Pallas kernels for 0% -> 62%
where the time goes in v3:
time: 560 us; the launch traced here: 553 us
  Pallas kernels  504 us (90%)
  other arithmetic  27.3 us (5%)
  starting transfers between devices  11.8 us (2%)
  local copies, waits for them, and re-layouts  7.99 us (1%)
    pallas_call x2, Pallas kernels, layer_forward(): pl.pallas_call(functools.partial(forward_kernel, layer, count, swap), nam...  157 us
    pallas_call x2, Pallas kernels, attention_back(): pl.pallas_call(functools.partial(attention_back_kernel, layer, count, bes...  131 us
    pallas_call x2, Pallas kernels, experts_back(): pl.pallas_call(functools.partial(experts_back_kernel, layer, count, besid...  127 us
    pallas_call x1, Pallas kernels, finish(): pl.pallas_call(functools.partial(finish_kernel, bring, beside), name='fin...  73.7 us
    convert_element_type x8, other arithmetic, results(): return (row.astype(bf16), col.astype(bf16))  17 us
    ppermute x2, starting transfers between devices, swapped(): return lax.ppermute(value, 'section', [(0, 1), (1, 0)])  11.8 us
  transfers between devices with their start and end apart: 2, of which 0 were waited for; matrix products, arithmetic and copies ran while one was open for 5% of the time, Pallas kernels for 62%

profile of v3, /device:TPU:0, one launch (start us, length us, event | category | flops | bytes accessed | tf_op | source)
XLA Modules:
  0.0 552.6 jit_solution(1381986765731429429)
XLA Ops:
  0.7 0.6 broadcast_in_dim_tile.3.freqs
  1.3 1.6 copy.28
  2.8 1.7 copy.29
  4.5 4.9 prepare.1
  9.4 79.8 %layer_forward_0.1 = (f32[64,1536]{1,0:T(8,128)}, f32[64,1536]{1,0:T(8,128)}, bf16[64,1536]{1,0:T(8,128)(2,1)}, bf16[1536,64]{1,0:T(8,128)(2,1)}, bf16[256,128]{...) custom-call(bf16[2,64,1536]{2,1,0:T(8,128)(2,1)} %refs_1_.1, ...), custom_call_target="tpu_custom_call" | custom-call | tf_op jit(solution)/shard_map/layer_forward_0/pallas_call | solution.py:682
  89.3 0.0 copy-start.4
  89.3 77.0 %layer_forward_1.1 = (f32[64,1536]{1,0:T(8,128)}, f32[64,1536]{1,0:T(8,128)}, bf16[64,1536]{1,0:T(8,128)(2,1)}, bf16[1536,64]{1,0:T(8,128)(2,1)}, bf16[256,128]{...) custom-call(f32[64,1536]{1,0:T(8,128)} %get-tuple-element.104.refs_0, ...), custom_call_target="tpu_custom_call" | custom-call | tf_op jit(solution)/shard_map/layer_forward_1/pallas_call | solution.py:682
  166.3 0.0 copy-done.4
  166.3 1.9 select_bitcast_fusion.1
  168.2 9.0 %collective-permute-start = (f32[64,1536]{1,0:T(8,128)}, f32[64,1536]{1,0:T(8,128)}, u32[]{:S(2)}, u32[]{:S(2)}) collective-permute-start(f32[64,1536]{1,0:T(8,128)} %get-tuple-element.183), channel_id=1, source_target_pairs={{0,16},{16,0},{1,17},{17,1},{2,18},{18,2},{3,19},{19,3},{4,20},{20... | collective-permute-start | bytes 1179656 | tf_op jit(solution)/shard_map/ppermute | solution.py:35
  177.3 62.8 %experts_back_1.1 = (f32[64,1536]{1,0:T(8,128)}, f32[16,1536]{1,0:T(8,128)}, f32[1,1536]{1,0:T(1,128)}, bf16[16,768,256]{2,1,0:T(8,128)(2,1)}, bf16[16,128,768]{2,1,0:T(8,128)(2,1)}) custom-call(bf16[2,64,1536]{2,1,0:T(8,128)(2,1)} %refs_0_.3, f32[64,1536]{1,0:T(8,128)} %get-tuple-element.113.refs_1_, f32[2,1,1536]{2,1,0:T(1,128)} %get-tuple-element.97.refs_2_, ...), custom_call_target="tpu_custom_call" | custom-call | tf_op jit(solution)/shard_map/experts_back_1/pallas_call | solution.py:898
  240.1 57.9 %attention_back_1.1 = (f32[64,1536]{1,0:T(8,128)}, f32[1,1536]{1,0:T(1,128)}, bf16[768,1024]{1,0:T(8,128)(2,1)}, bf16[1,2,4,384,256]{4,3,2,1,0:T(8,128)(2,1)}, b...) custom-call(f32[64,1536]{1,0:T(8,128)} %get-tuple-element.119.refs_0_, ...), custom_call_target="tpu_custom_call" | custom-call | tf_op jit(solution)/shard_map/attention_back_1/pallas_call | solution.py:1057
  298.0 0.0 copy-start.3
  298.1 0.0 copy-start.12
  298.1 3.6 fusion.1.refs_16_
  301.6 0.0 copy-done.3
  301.6 0.0 copy-done.12
  301.6 1.1 fusion.5.refs_18_
  302.7 3.5 fusion.2.refs_17_
  306.2 0.0 copy-done.11
  306.2 1.1 fusion.6.refs_19_
  307.3 0.0 copy-done.7
  307.3 0.7 convert_element_type.132.refs_0_
  308.0 63.8 %experts_back_0.1 = (f32[64,1536]{1,0:T(8,128)}, f32[16,1536]{1,0:T(8,128)}, f32[1,1536]{1,0:T(1,128)}, bf16[16,768,256]{2,1,0:T(8,128)(2,1)}, bf16[16,128,768]{...) custom-call(bf16[64,1536]{1,0:T(8,128)(2,1)} %convert_element_type.1, ...), custom_call_target="tpu_custom_call" | custom-call | tf_op jit(solution)/shard_map/experts_back_0/pallas_call | solution.py:898
  371.8 0.0 slice-start
  371.8 2.5 fusion.8.refs_21_
  374.3 73.1 %attention_back_0.1 = (f32[64,1536]{1,0:T(8,128)}, f32[1,1536]{1,0:T(1,128)}, bf16[768,1024]{1,0:T(8,128)(2,1)}, bf16[1,2,4,384,256]{4,3,2,1,0:T(8,128)(2,1)}, b...) custom-call(f32[64,1536]{1,0:T(8,128)} %get-tuple-element.140.refs_0, ...), custom_call_target="tpu_custom_call" | custom-call | tf_op jit(solution)/shard_map/attention_back_0/pallas_call | solution.py:1057
  447.4 0.0 copy-start.10
  447.4 1.1 select_bitcast_fusion
  448.6 0.0 copy-start.9
  448.6 2.7 collective-permute-start.1
  451.3 2.2 fusion.4.refs_9_
  453.6 2.3 fusion.7.refs_10_
  455.9 0.0 slice-done
  455.9 0.0 copy-done.6
  455.9 1.6 fusion.3.refs_8_
  457.5 1.6 fusion.refs_7_
  459.1 73.7 %finish.1 = (f32[48,1536]{1,0:T(8,128)}, bf16[2,4,192,1024]{3,2,1,0:T(8,128)(2,1)}, bf16[2,2,4,384,256]{4,3,2,1,0:T(8,128)(2,1)}, bf16[2,2,4,384,256]{4,3,2,1,0:...) custom-call(f32[16,1536]{1,0:T(8,128)} %get-tuple-element.151.refs_0_, ...), custom_call_target="tpu_custom_call" | custom-call | tf_op jit(solution)/shard_map/finish/pallas_call | solution.py:1196
  532.9 1.0 slice_select_fusion
  533.9 0.6 slice_bitcast_fusion
  534.5 0.6 fusion.9
  535.1 1.4 copy-done.1
  536.6 1.4 copy-done.2
  538.0 11.1 %assemble.1 = (f32[1536,384]{1,0:T(8,128)}, f32[1536,128]{1,0:T(8,128)}, f32[1536,128]{1,0:T(8,128)}, f32[384,1536]{1,0:T(8,128)}, f32[4,1536,128]{2,1,0:T(8,128...) custom-call(s32[1]{0:T(128)} %bitcast.35.section, bf16[2,2,4,384,256]{4,3,2,1,0:T(8,128)(2,1)} %get-tuple-element.163.refs_0_, ...), custom_call_target="tpu_custom_call" | custom-call | tf_op jit(solution)/shard_map/assemble/pallas_call | solution.py:1386
  549.1 0.0 collective-permute-done
  549.1 2.1 maximum_select_fusion
  551.2 0.0 collective-permute-done.1
  551.2 0.9 maximum_select_fusion.1
  (18 shorter events, 0.0 us)
Async XLA Ops:
  89.3 77.0 %copy-start.4 = (f32[64,1536]{1,0:T(8,128)S(1)}, f32[64,1536]{1,0:T(8,128)}, u32[]{:S(2)}) copy-start(f32[64,1536]{1,0:T(8,128)} %get-tuple-element.104.refs_0_.refs_1_) | copy-start | bytes 1179652
  168.2 380.9 %collective-permute-start = (f32[64,1536]{1,0:T(8,128)}, f32[64,1536]{1,0:T(8,128)}, u32[]{:S(2)}, u32[]{:S(2)}) collective-permute-start(f32[64,1536]{1,0:T(8,128)} %get-tuple-element.183), channel_id=1, source_target_pairs={{0,16},{16,0},{1,17},{17,1},{2,18},{18,2},{3,19},{19,3},{4,20},{20... | collective-permute-start | bytes 1179656 | tf_op jit(solution)/shard_map/ppermute | solution.py:35
  298.0 3.6 copy-start.3
  298.1 3.6 copy-start.12
  302.7 3.5 copy-start.11
  306.2 1.1 copy-start.7
  371.8 84.1 %slice-start = ((s8[6291456]{0:T(1024)(128)(4,1)}), s8[4194304]{0:T(1024)(128)(4,1)S(1)}, s32[]{:S(2)}) async-start(s8[6291456]{0:T(1024)(128)(4,1)} %bitcast.93), calls=%async_computation | async-start | bytes 8388608
  374.3 81.6 %slice-start.1 = ((s8[6291456]{0:T(1024)(128)(4,1)}), s8[2097152]{0:T(1024)(128)(4,1)S(1)}, s32[]{:S(2)}) async-start(s8[6291456]{0:T(1024)(128)(4,1)} %bitcast.93), calls=%async_computation.1 | async-start | bytes 4194304
  447.4 3.9 copy-start.10
  448.6 5.0 copy-start.9
  448.6 102.6 %collective-permute-start.1 = (f32[64,1536]{1,0:T(8,128)S(1)}, f32[64,1536]{1,0:T(8,128)S(1)}, u32[]{:S(2)}, u32[]{:S(2)}) collective-permute-start(f32[64,1536]{1,0:T(8,128)S(1)} %get-tuple-element.181), channel_id=1, source_target_pairs={{0,16},{16,0},{1,17},{17,1},{2,18},{18,2},{3,19},{19,3},{4,20},{20... | collective-permute-start | bytes 1179656 | tf_op jit(solution)/shard_map/ppermute | solution.py:35
  453.6 2.3 copy-start.6
  455.9 1.6 copy-start.5
  459.1 76.0 %copy-start = (bf16[2,2,4,128,384]{4,3,2,1,0:T(8,128)(2,1)S(1)}, bf16[2,2,4,128,384]{4,3,2,1,0:T(8,128)(2,1)}, u32[]{:S(2)}) copy-start(bf16[2,2,4,128,384]{4,3,2,1,0:T(8,128)(2,1)} %get-tuple-element.169.refs_6_) | copy-start | bytes 4718596
  535.1 1.4 copy-start.1
  536.6 1.4 copy-start.2
  538.0 11.2 %copy-start.8 = (f32[1,1,64,1536]{3,2,1,0:T(8,128)S(1)}, f32[1,1,64,1536]{3,2,1,0:T(8,128)}, u32[]{:S(2)}) copy-start(f32[1,1,64,1536]{3,2,1,0:T(8,128)} %get-tuple-element.182) | copy-start | bytes 1179652

commit v4 on v3

--- a/solution.py
+++ b/solution.py
@@ -29,10 +29,6 @@
 NN = ((1,), (0,))
 NT = ((1,), (1,))
 TN = ((0,), (0,))
-
-
-def swapped(value):
-    return lax.ppermute(value, "section", [(0, 1), (1, 0)])
 
 
 def norm_scale(rows_in):
@@ -87,62 +83,6 @@
     return pltpu.make_async_remote_copy(
         src_ref=src, dst_ref=dst, send_sem=send, recv_sem=recv, device_id=device, device_id_type=MESH
     )
-
-
-class FirstStage:
-    def __init__(self, value, axis):
-        self.count = lax.axis_size("dp")
-        outer, inner = factors(self.count)
-        self.inputs = [value.reshape((outer, inner, value.shape[0] // self.count) + value.shape[1:])]
-        self.axis = axis
-        shape = list(self.inputs[0].shape[2:])
-        shape[axis] //= 2
-        self.shape = shape
-        self.outputs = [
-            jax.ShapeDtypeStruct((inner - 1, outer, *shape), value.dtype),
-            jax.ShapeDtypeStruct((outer - 1, inner, *shape), value.dtype),
-        ]
-        self.sems = [dma((inner + outer - 2,)), dma((inner + outer - 2,))]
-
-    def copies(self, inputs, outputs, sems):
-        across, along = near_groups(self.count)
-        value = inputs[0]
-        half = self.shape[self.axis]
-        cut = [slice(None)] * 3
-        first, second = list(cut), list(cut)
-        first[self.axis], second[self.axis] = pl.ds(0, half), pl.ds(half, half)
-        found = []
-        for slot, (place, device) in enumerate(across):
-            found.append((value.at[(slice(None), place, *first)], outputs[0].at[slot], device))
-        for slot, (place, device) in enumerate(along):
-            found.append((value.at[(place, slice(None), *second)], outputs[1].at[slot], device))
-        return [
-            remote(src, dst, sems[0].at[index], sems[1].at[index], device)
-            for index, (src, dst, device) in enumerate(found)
-        ]
-
-    def start(self, inputs, outputs, sems):
-        for copy in self.copies(inputs, outputs, sems):
-            copy.start()
-
-    def wait(self, inputs, outputs, sems):
-        for copy in self.copies(inputs, outputs, sems):
-            copy.wait()
-
-    def results(self, outputs):
-        outer, inner, mo, mi = group_place(self.count)
-        value = self.inputs[0]
-        half = self.shape[self.axis]
-        later = [0] * 5
-        later[2 + self.axis] = half
-        row = lax.dynamic_slice(value, (0, mi, 0, 0, 0), (outer, 1, *self.shape))[:, 0].astype(f32)
-        later[0] = mo
-        col = lax.dynamic_slice(value, later, (1, inner, *self.shape))[0].astype(f32)
-        for slot in range(inner - 1):
-            row = row + outputs[0][slot].astype(f32)
-        for slot in range(outer - 1):
-            col = col + outputs[1][slot].astype(f32)
-        return row.astype(bf16), col.astype(bf16)
 
 
 class Bring:
@@ -243,39 +183,261 @@
         return outputs[0]
 
 
-class Scatter:
-    def __init__(self, value):
+class FirstStage:
+    def __init__(self, value, axis, layer=None):
         self.count = lax.axis_size("dp")
-        block = (value.shape[0] // self.count,) + value.shape[1:]
-        self.inputs = [value.reshape((self.count, *block))]
-        self.outputs = [jax.ShapeDtypeStruct((self.count - 1, *block), value.dtype)]
-        self.sems = [dma((self.count - 1,)), dma((self.count - 1,))]
-
-    def copies(self, inputs, outputs, sems):
+        outer, inner = factors(self.count)
+        self.inputs = [value.reshape((outer, inner, value.shape[0] // self.count) + value.shape[1:])]
+        self.axis = axis
+        shape = list(self.inputs[0].shape[2:])
+        shape[axis] //= 2
+        self.shape = shape
+        sums = [
+            jax.ShapeDtypeStruct((outer, *shape), value.dtype),
+            jax.ShapeDtypeStruct((inner, *shape), value.dtype),
+        ]
+        self.sems = [
+            dma((inner + outer - 2,)),
+            dma((inner + outer - 2,)),
+            pltpu.VMEM((inner - 1, outer, *shape), value.dtype),
+            pltpu.VMEM((outer - 1, inner, *shape), value.dtype),
+            *[pltpu.VMEM(v.shape, v.dtype) for v in sums],
+            dma((2,)),
+            dma((2,)),
+        ]
+        self.outputs = sums
+        self.brings = []
+        if layer is not None:
+            self.brings = [Bring(layer, kind, v, True) for kind, v in zip(("column", "row"), sums)]
+            self.outputs = [v for bring in self.brings for v in bring.outputs]
+            self.sems += [v for bring in self.brings for v in bring.sems]
+
+    def copies(self, inputs, sems):
+        across, along = near_groups(self.count)
+        _, _, mo, mi = group_place(self.count)
+        value = inputs[0]
+        half = self.shape[self.axis]
+        cut = [slice(None)] * 3
+        first, second = list(cut), list(cut)
+        first[self.axis], second[self.axis] = pl.ds(0, half), pl.ds(half, half)
+        found = []
+        for slot, (place, device) in enumerate(across):
+            found.append((value.at[(slice(None), place, *first)], sems[2].at[slot], device))
+        for slot, (place, device) in enumerate(along):
+            found.append((value.at[(place, slice(None), *second)], sems[3].at[slot], device))
+        sent = [
+            remote(src, dst, sems[0].at[index], sems[1].at[index], device)
+            for index, (src, dst, device) in enumerate(found)
+        ]
+        loads = [
+            pltpu.make_async_copy(value.at[(slice(None), mi, *first)], sems[4], sems[6].at[0]),
+            pltpu.make_async_copy(value.at[(mo, slice(None), *second)], sems[5], sems[6].at[1]),
+        ]
+        return sent + loads
+
+    def onward(self, outputs, sems):
+        place = 8
+        found = []
+        for index, bring in enumerate(self.brings):
+            found.append((bring, [sems[4 + index]], [outputs[index]], sems[place : place + len(bring.sems)]))
+            place += len(bring.sems)
+        return found
+
+    def saves(self, outputs, sems):
+        return [pltpu.make_async_copy(sems[4 + k], outputs[k], sems[7].at[k]) for k in range(2)]
+
+    def start(self, inputs, outputs, sems):
+        start_all(self.copies(inputs, sems))
+
+    def middle(self, inputs, outputs, sems):
+        wait_all(self.copies(inputs, sems))
+        for total, landed in ((sems[4], sems[2]), (sems[5], sems[3])):
+            depth = total.shape[1]
+
+            def add(index, carry, total=total, landed=landed, depth=depth):
+                place, expert = index // depth, lax.rem(index, depth)
+                value = total[place, expert].astype(f32)
+                for slot in range(landed.shape[0]):
+                    value = value + landed[slot, place, expert].astype(f32)
+                total[place, expert] = value.astype(bf16)
+                return carry
+
+            lax.fori_loop(0, total.shape[0] * depth, add, 0)
+        if self.brings:
+            for bring, *refs in self.onward(outputs, sems):
+                bring.start(*refs)
+        else:
+            start_all(self.saves(outputs, sems))
+
+    def wait(self, inputs, outputs, sems):
+        if self.brings:
+            for bring, *refs in self.onward(outputs, sems):
+                bring.wait(*refs)
+        else:
+            wait_all(self.saves(outputs, sems))
+
+    def results(self, outputs):
+        return outputs
+
+
+class DenseSum:
+    kind = "all"
+
+    def __init__(self, value, layer):
+        count = lax.axis_size("dp")
+        self.rows, width = value.shape[0] // count, value.shape[1]
+        self.bring = Bring(layer, "all", jax.ShapeDtypeStruct((self.rows, width), bf16), True)
+        self.inputs = [value]
+        self.outputs = self.bring.outputs
+        self.sems = [
+            dma((count - 1,)),
+            dma((count - 1,)),
+            pltpu.VMEM((count - 1, self.rows, width), bf16),
+            pltpu.VMEM((self.rows, width), bf16),
+            dma((1,)),
+            *self.bring.sems,
+        ]
+
+    def copies(self, inputs, sems):
+        count = lax.axis_size("dp")
         me = lax.axis_index("dp")
-        found = []
-        for step in range(1, self.count):
-            place = lax.rem(me + step, self.count)
+
+        def block(place):
+            return inputs[0].at[pl.ds(pl.multiple_of(place * self.rows, self.rows), self.rows)]
+
+        found = [pltpu.make_async_copy(block(me), sems[3], sems[4].at[0])]
+        for step in range(1, count):
+            place = lax.rem(me + step, count)
             found.append(
-                remote(inputs[0].at[place], outputs[0].at[step - 1], sems[0].at[step - 1],
-                       sems[1].at[step - 1], {"dp": place})
+                remote(block(place), sems[2].at[step - 1], sems[0].at[step - 1], sems[1].at[step - 1],
+                       {"dp": place})
             )
         return found
 
     def start(self, inputs, outputs, sems):
-        for copy in self.copies(inputs, outputs, sems):
-            copy.start()
+        start_all(self.copies(inputs, sems))
+
+    def middle(self, inputs, outputs, sems):
+        wait_all(self.copies(inputs, sems))
+        total = sems[3][...].astype(f32)
+        for slot in range(sems[2].shape[0]):
+            total = total + sems[2][slot].astype(f32)
+        sems[3][...] = total.astype(bf16)
+        self.bring.start([sems[3]], outputs, sems[5:])
 
     def wait(self, inputs, outputs, sems):
-        for copy in self.copies(inputs, outputs, sems):
-            copy.wait()
+        self.bring.wait([sems[3]], outputs, sems[5:])
 
     def results(self, outputs):
+        return outputs[0]
+
+
+class SmallSum:
+    def __init__(self, depth, width):
+        self.tensor, self.count = lax.axis_size("tensor"), lax.axis_size("dp")
+        self.lanes = width // self.tensor
+        self.depth = depth
+        part = (depth, self.lanes)
+        self.sems = [
+            pltpu.VMEM((depth, width), f32),
+            pltpu.VMEM((self.tensor - 1, *part), f32),
+            pltpu.VMEM((self.count - 1, *part), f32),
+            *[pltpu.VMEM(part, f32) for _ in range(4)],
+            pltpu.VMEM((depth, width), f32),
+            dma((2, self.tensor - 1)),
+            dma((2, self.tensor - 1)),
+            dma((self.count,)),
+            dma((self.count,)),
+        ]
+
+    def columns(self, place):
+        return pl.ds(pl.multiple_of(place * self.lanes, self.lanes), self.lanes)
+
+    def over_tensor(self, sems):
+        here = lax.axis_index("tensor")
+        found = []
+        for step in range(1, self.tensor):
+            place = lax.rem(here + step, self.tensor)
+            found.append(
+                remote(sems[0].at[:, self.columns(place)], sems[1].at[step - 1],
+                       sems[8].at[0, step - 1], sems[9].at[0, step - 1], {"tensor": place})
+            )
+        return found
+
+    def over_groups(self, sems):
         me = lax.axis_index("dp")
-        total = lax.dynamic_index_in_dim(self.inputs[0], me, 0, keepdims=False).astype(f32)
+        return [
+            remote(sems[3], sems[2].at[step - 1], sems[10].at[step - 1], sems[11].at[step - 1],
+                   {"dp": lax.rem(me + step, self.count)})
+            for step in range(1, self.count)
+        ]
+
+    def over_cores(self, sems):
+        last = self.count - 1
+        return [remote(sems[4], sems[5], sems[10].at[last], sems[11].at[last], core_peer())]
+
+    def back(self, sems):
+        here = lax.axis_index("tensor")
+        own = sems[7].at[:, self.columns(here)]
+        return [
+            remote(sems[6], own, sems[8].at[1, step - 1], sems[9].at[1, step - 1],
+                   {"tensor": lax.rem(here + step, self.tensor)})
+            for step in range(1, self.tensor)
+        ]
+
+    def first(self, sems):
+        start_all(self.over_tensor(sems))
+
+    def second(self, sems):
+        wait_all(self.over_tensor(sems))
+        total = sems[0][:, self.columns(lax.axis_index("tensor"))]
+        for slot in range(self.tensor - 1):
+            total = total + sems[1][slot]
+        sems[3][...] = total
+        start_all(self.over_groups(sems))
+
+    def third(self, sems):
+        wait_all(self.over_groups(sems))
+        total = sems[3][...]
         for slot in range(self.count - 1):
-            total = total + outputs[0][slot].astype(f32)
-        return total.astype(bf16)
+            total = total + sems[2][slot]
+        sems[4][...] = total
+        copies = self.over_cores(sems)
+        start_all(copies)
+        wait_all(copies)
+        sems[6][...] = sems[4][...] + sems[5][...]
+        start_all(self.back(sems))
+        sems[7][:, self.columns(lax.axis_index("tensor"))] = sems[6][...]
+
+    def last(self, sems, out):
+        wait_all(self.back(sems))
+        out[...] = sems[7][...]
+
+
+class Trade:
+    def __init__(self, shape):
+        self.sems = [pltpu.VMEM((2, *shape), f32), dma((1,)), dma((1,))]
+
+    def copy(self, value, sems):
+        core = lax.axis_index("section")
+        return remote(value, sems[0].at[core], sems[1].at[0], sems[2].at[0], core_peer())
+
+    def start(self, zero, one, sems):
+        core = lax.axis_index("section")
+
+        @pl.when(core == 0)
+        def _():
+            self.copy(one, sems).start()
+            sems[0][0] = zero[...]
+
+        @pl.when(core == 1)
+        def _():
+            self.copy(zero, sems).start()
+            sems[0][1] = one[...]
+
+    def wait(self, zero, out, sems):
+        self.copy(zero, sems).wait()
+        out[...] = sems[0][...]
 
 
 def both_cores(groups):
@@ -292,7 +454,7 @@
 
     def peers(self):
         count = lax.axis_size("dp")
-        if any(isinstance(job, Scatter) or getattr(job, "kind", "") == "all" for job in self.jobs):
+        if any(getattr(job, "kind", "") == "all" for job in self.jobs):
             me = lax.axis_index("dp")
             return both_cores([lax.rem(me + step, count) for step in range(1, count)])
         if not self.jobs:
@@ -310,6 +472,9 @@
 
     def start(self, *refs):
         self.each(refs, lambda job: job.start)
+
+    def middle(self, *refs):
+        self.each(refs, lambda job: getattr(job, "middle", lambda *refs: None))
 
     def wait(self, *refs):
         self.each(refs, lambda job: job.wait)
@@ -733,7 +898,7 @@
     return value_grad, gain_grad
 
 
-def experts_back_kernel(layer, count, beside, *refs):
+def experts_back_kernel(layer, count, trade, beside, *refs):
     refs = list(refs)
 
     def take(number):
@@ -746,14 +911,17 @@
     out_grad = out_grad_in if layer == 0 else out_grad_in.at[lax.axis_index("section")]
     x_in, gated_in = take(2)
     own, other = take(3), take(3)
+    traded = take(2 if trade else 0)
     beside_in = take(len(beside.inputs))
     mid_grad_out, router_out, expert_gain_out, pair_out, down_out = take(5)
+    traded_out = take(1 if trade else 0)
     beside_out = take(len(beside.outputs))
     scratch = take(2)
     gu_s, down_s = scratch
     (ag1, part, landing1, pre_s, gpu_s, acc, gate_part, gate_land, og_s, gpu_peer, x_s, turned_x,
      gated_s, turned_gated, pair_s, down_grad_s, send_s, recv_s, expert_sems, pre_sems, core_send,
      core_recv, local_sems, hand_send, hand_recv, save_sems) = take(26)
+    trade_sems = take(len(trade.sems) if trade else 0)
     beside_refs = (beside_in, beside_out, refs)
     rows, width = mid.shape
     experts = gu_s.shape[0]
@@ -778,6 +946,8 @@
     for copy in loads:
         copy.start()
     beside.start(*beside_refs)
+    if trade:
+        trade.start(*traded, trade_sems)
     gate_part[...] = jnp.zeros_like(gate_part)
     wait_all(loads)
     turned_x[...] = x_s[...].T
@@ -859,6 +1029,7 @@
         return carry
 
     lax.fori_loop(0, experts, grads_step, 0)
+    beside.middle(*beside_refs)
     wait_all(copies)
     in_grad = acc[own_rows, :]
     gate_grad = gate_part[own_rows, :]
@@ -882,21 +1053,24 @@
         return carry
 
     lax.fori_loop(0, experts, finish_save, 0)
+    if trade:
+        trade.wait(traded[0], traded_out[0], trade_sems)
     beside.wait(*beside_refs)
 
 
-def experts_back(layer, gains, own, other, out_grad, state, pairs, masks, beside):
+def experts_back(layer, gains, own, other, out_grad, state, pairs, masks, traded, beside):
     count = lax.axis_size("tensor")
     mid, gate, expert_rows, pre = state
     rows, width = mid.shape
     tokens = gate.shape[0]
     own, other = own[4:], other[4:]
+    trade = Trade((rows, width)) if traded else None
     experts, depth, hidden_width = own[0].shape
     vmem = pl.BlockSpec(memory_space=pltpu.VMEM)
     hbm = pl.BlockSpec(memory_space=pl.ANY)
     shape = jax.ShapeDtypeStruct
     found = pl.pallas_call(
-        functools.partial(experts_back_kernel, layer, count, beside),
+        functools.partial(experts_back_kernel, layer, count, trade, beside),
         name=f"experts_back_{layer}",
         out_shape=(
             shape((rows, width), f32),
@@ -904,10 +1078,11 @@
             shape((1, width), f32),
             shape((experts, width // 2, 2 * hidden_width), bf16),
             shape((experts, hidden_width, width // 2), bf16),
+            *((shape((2, rows, width), f32),) if traded else ()),
             *beside.outputs,
         ),
-        in_specs=[vmem] * 7 + [hbm] * (9 + len(beside.inputs)),
-        out_specs=(vmem, vmem, vmem, hbm, hbm) + (hbm,) * len(beside.outputs),
+        in_specs=[vmem] * 7 + [hbm] * 9 + [vmem] * len(traded) + [hbm] * len(beside.inputs),
+        out_specs=(vmem, vmem, vmem, hbm, hbm) + (vmem,) * bool(traded) + (hbm,) * len(beside.outputs),
         scratch_shapes=[
             pltpu.VMEM((experts, depth, 2 * hidden_width), bf16),
             pltpu.VMEM((experts * hidden_width, depth), bf16),
@@ -933,15 +1108,17 @@
             pltpu.SemaphoreType.DMA((experts,)),
             *[pltpu.SemaphoreType.DMA((2,)) for _ in range(5)],
             pltpu.SemaphoreType.DMA((2, experts)),
+            *(trade.sems if trade else ()),
             *beside.sems,
         ],
         compiler_params=params(3 + layer),
     )(out_grad, mid, *gains[1:], masks[1], gate, expert_rows, pre, *pairs, *own, *other,
-      *beside.inputs)
-    return found[:5], beside.results(found[5:])
-
-
-def attention_back_kernel(layer, count, beside, *refs):
+      *traded, *beside.inputs)
+    kept = 6 if traded else 5
+    return found[:kept], beside.results(found[kept:])
+
+
+def attention_back_kernel(layer, count, last, beside, *refs):
     refs = list(refs)
 
     def take(number):
@@ -954,14 +1131,24 @@
     stream = stream_in.at[lax.axis_index("section")] if layer == 0 else stream_in
     ai_in, attended_in = take(2)
     own, other = take(4), take(4)
+    small_parts = take(5 if last else 0)
+    later_grad = take(1 if last else 0)
     beside_in = take(len(beside.inputs))
-    grad_out, attn_gain_out, dense_out = take(3)
+    if last:
+        dense_sum, small_sum, trade = last
+        traded_out, small_out, whole_out = take(3)
+    else:
+        grad_out, attn_gain_out, dense_out = take(3)
     beside_out = take(len(beside.outputs))
     scratch = take(2)
     joint_s, output_s = scratch
     (ag2, part, landing2, ag_stack, dq_s, joint_rows, joint_peer, ao_s, ai_s, turned_ai, attended_s,
      dense_s, send_s, recv_s, attn_sems, core_send, core_recv, local_sems,
      hand_send, hand_recv) = take(20)
+    if last:
+        grad_s, trade_sems = refs.pop(0), take(len(trade.sems))
+        dense_sems, small_sems = take(len(dense_sum.sems)), take(len(small_sum.sems))
+        dense_refs = ([dense_s], [whole_out], dense_sems)
     beside_refs = (beside_in, beside_out, refs)
     rows, width = stream.shape
     tokens = ag2.shape[0]
@@ -973,7 +1160,8 @@
     own_rows = pl.ds(pl.multiple_of(me * rows, rows), rows)
     use_own = lax.axis_index("section") == layer
     ag2[own_rows, :] = mid_grad[...].astype(bf16)
-    greet(tensor_peers(count) + [core_peer()] + beside.peers())
+    everyone = Beside([*beside.jobs, dense_sum]) if last else beside
+    greet(tensor_peers(count) + [core_peer()] + everyone.peers())
     first = spread(count, ag2, rows, send_s.at[0], recv_s.at[0])
     start_all(first)
     either(use_own, own, other, lambda w: [c.start() for c in attn_copies(w, scratch, attn_sems)])
@@ -1028,8 +1216,11 @@
         dot(turned_ai[:, :tokens], joint_rows[...], NN) + dot(turned_ai[:, tokens:], joint_peer[...], NN)
     ).astype(bf16)
     dense_s[:, wide:] = dot(ao_s[...], attended_s[...], TN).astype(bf16)
-    save = pltpu.make_async_copy(dense_s, dense_out, local_sems.at[0])
-    save.start()
+    if last:
+        dense_sum.start(*dense_refs)
+    else:
+        save = pltpu.make_async_copy(dense_s, dense_out, local_sems.at[0])
+        save.start()
     wait_all(copies)
     in_grad = part[own_rows, :].astype(f32)
     for step in range(count - 1):
@@ -1037,13 +1228,38 @@
     stream_part, attn_gain_grad = norm_back(
         stream[...].astype(bf16).astype(f32), attn_gain[...], in_grad
     )
-    attn_gain_out[...] = attn_gain_grad
-    grad_out[...] = mid_grad[...] + stream_part
-    save.wait()
+    grad = mid_grad[...] + stream_part
+    if not last:
+        attn_gain_out[...] = attn_gain_grad
+        grad_out[...] = grad
+        save.wait()
+        beside.middle(*beside_refs)
+        beside.wait(*beside_refs)
+        return
+    small = small_sems[0]
+    router0, gain0, router1, attn_gain1, gain1 = small_parts
+    place = 0
+    for value in (router0[...], attn_gain_grad, gain0[...]):
+        small[pl.ds(place, value.shape[0]), :] = value
+        place += value.shape[0]
+    place = small.shape[0] // 2
+    for value in (router1[...], attn_gain1[...], gain1[...]):
+        small[pl.ds(place, value.shape[0]), :] = value
+        place += value.shape[0]
+    small_sum.first(small_sems)
+    grad_s[...] = grad
+    trade.start(grad_s, later_grad[0], trade_sems)
+    beside.middle(*beside_refs)
+    small_sum.second(small_sems)
+    dense_sum.middle(*dense_refs)
+    small_sum.third(small_sems)
+    trade.wait(grad_s, traded_out, trade_sems)
+    small_sum.last(small_sems, small_out)
+    dense_sum.wait(*dense_refs)
     beside.wait(*beside_refs)
 
 
-def attention_back(layer, gains, own, other, mid_grad, stream, state, pairs, tables, beside):
+def attention_back(layer, gains, own, other, mid_grad, stream, state, pairs, tables, ending, beside):
     count = lax.axis_size("tensor")
     qs, keys, values, probs = state
     rows, width = mid_grad.shape
@@ -1054,16 +1270,20 @@
     vmem = pl.BlockSpec(memory_space=pltpu.VMEM)
     hbm = pl.BlockSpec(memory_space=pl.ANY)
     shape = jax.ShapeDtypeStruct
+    dense = shape((width // 2, 2 * qw + 2 * kw), bf16)
+    if ending:
+        depth = 2 * (-(-(ending[0].shape[0] + 2) // 8) * 8)
+        last = (DenseSum(dense, layer), SmallSum(depth, width), Trade((rows, width)))
+        own_outs = (shape((2, rows, width), f32), shape((depth, width), f32), *last[0].outputs)
+        more = [pltpu.VMEM((rows, width), f32), *last[2].sems, *last[0].sems, *last[1].sems]
+    else:
+        last, more = None, []
+        own_outs = (shape((rows, width), f32), shape((1, width), f32), dense)
     found = pl.pallas_call(
-        functools.partial(attention_back_kernel, layer, count, beside),
+        functools.partial(attention_back_kernel, layer, count, last, beside),
         name=f"attention_back_{layer}",
-        out_shape=(
-            shape((rows, width), f32),
-            shape((1, width), f32),
-            shape((width // 2, 2 * qw + 2 * kw), bf16),
-            *beside.outputs,
-        ),
-        in_specs=[vmem] * 9 + [hbm] * (10 + len(beside.inputs)),
+        out_shape=(*own_outs, *beside.outputs),
+        in_specs=[vmem] * 9 + [hbm] * 10 + [vmem] * len(ending) + [hbm] * len(beside.inputs),
         out_specs=(vmem, vmem, hbm) + (hbm,) * len(beside.outputs),
         scratch_shapes=[
             pltpu.VMEM((width, qw + 2 * kw), bf16),
@@ -1084,151 +1304,13 @@
             pltpu.SemaphoreType.DMA((3, count - 1)),
             pltpu.SemaphoreType.DMA((4,)),
             *[pltpu.SemaphoreType.DMA((2,)) for _ in range(5)],
+            *more,
             *beside.sems,
         ],
         compiler_params=params(5 + layer),
     )(mid_grad, stream, gains[0], *tables[:2], qs, keys, values, probs, *pairs, *own, *other,
-      *beside.inputs)
+      *ending, *beside.inputs)
     return found[:3], beside.results(found[3:])
-
-
-def finish_kernel(bring, beside, *refs):
-    refs = list(refs)
-
-    def take(number):
-        taken = refs[:number]
-        del refs[:number]
-        return taken
-
-    *small_parts, dense = take(7)
-    beside_in = take(len(beside.inputs))
-    small_out, whole_out, *beside_out = take(2 + len(beside.outputs))
-    (landing, block, small_z, small_dp, small_core, small_sum, small_mid, small_last, small_whole,
-     sends, recvs, local_sems, z_sends, z_recvs, dp_sends, dp_recvs, core_sends,
-     core_recvs, small) = take(19)
-    bring_sems = take(len(bring.sems))
-    beside_refs = (beside_in, beside_out, refs)
-    count = dense.shape[0]
-    tensor = small_z.shape[0] + 1
-    lanes = small_z.shape[2]
-    me = lax.axis_index("dp")
-    here = lax.axis_index("tensor")
-    groups = [{"dp": lax.rem(me + step, count)} for step in range(1, count)]
-    greet(both_cores([group["dp"] for group in groups]) + tensor_peers(tensor) + [core_peer()])
-
-    def launch(*args):
-        copy = remote(*args)
-        copy.start()
-        return copy
-
-    def columns(place):
-        return pl.ds(pl.multiple_of(place * lanes, lanes), lanes)
-
-    place = 0
-    for index, value in enumerate(small_parts):
-        if index % 3 == 0:
-            place = index // 3 * (small.shape[0] // 2)
-        small[pl.ds(place, value.shape[0]), :] = value[...]
-        place += value.shape[0]
-    first = []
-    for step in range(1, tensor):
-        place = lax.rem(here + step, tensor)
-        first.append(
-            launch(small.at[:, columns(place)], small_z.at[step - 1], z_sends.at[0, step - 1],
-                   z_recvs.at[0, step - 1], {"tensor": place})
-        )
-    copies = []
-    for step in range(1, count):
-        place = lax.rem(me + step, count)
-        copies.append(
-            launch(dense.at[place], landing.at[step - 1], sends.at[0, step - 1],
-                   recvs.at[0, step - 1], {"dp": place})
-        )
-    beside.start(*beside_refs)
-    mine = pltpu.make_async_copy(dense.at[me], block, local_sems.at[0])
-    mine.start()
-    wait_all(first)
-    total = small[:, columns(here)]
-    for step in range(tensor - 1):
-        total = total + small_z[step]
-    small_sum[...] = total
-    second = [
-        launch(small_sum, small_dp.at[step], dp_sends.at[step], dp_recvs.at[step], groups[step])
-        for step in range(count - 1)
-    ]
-    mine.wait()
-    wait_all(copies)
-    total = block[...].astype(f32)
-    for step in range(count - 1):
-        total = total + landing[step].astype(f32)
-    block[...] = total.astype(bf16)
-    bring.start([block], [whole_out], bring_sems)
-    wait_all(second)
-    total = small_sum[...]
-    for step in range(count - 1):
-        total = total + small_dp[step]
-    small_mid[...] = total
-    third = launch(small_mid, small_core, core_sends.at[0], core_recvs.at[0], core_peer())
-    third.wait()
-    small_last[...] = small_mid[...] + small_core[...]
-    last = [
-        launch(small_last, small_whole.at[:, columns(here)], z_sends.at[1, step - 1],
-               z_recvs.at[1, step - 1], {"tensor": lax.rem(here + step, tensor)})
-        for step in range(1, tensor)
-    ]
-    small_whole[:, columns(here)] = small_last[...]
-    wait_all(last)
-    small_out[...] = small_whole[...]
-    bring.wait([block], [whole_out], bring_sems)
-    beside.wait(*beside_refs)
-
-
-def finish(small_parts, dense, layer, beside):
-    count = lax.axis_size("dp")
-    tensor = lax.axis_size("tensor")
-    rows = dense.shape[0] // count
-    depth = -(-sum(v.shape[0] for v in small_parts[:3]) // 8) * 8
-    small = jax.ShapeDtypeStruct((2 * depth, small_parts[0].shape[1]), f32)
-    lanes = small.shape[1] // tensor
-    hbm = pl.BlockSpec(memory_space=pl.ANY)
-    vmem = pl.BlockSpec(memory_space=pltpu.VMEM)
-    bring = Bring(layer, "all", jax.ShapeDtypeStruct((rows, dense.shape[1]), bf16), True)
-    found = pl.pallas_call(
-        functools.partial(finish_kernel, bring, beside),
-        name="finish",
-        out_shape=(
-            jax.ShapeDtypeStruct(small.shape, f32),
-            *bring.outputs,
-            *beside.outputs,
-        ),
-        in_specs=[vmem] * 6 + [hbm] * (1 + len(beside.inputs)),
-        out_specs=(vmem,) + (hbm,) * (1 + len(beside.outputs)),
-        scratch_shapes=[
-            pltpu.VMEM((count - 1, rows, dense.shape[1]), bf16),
-            pltpu.VMEM((rows, dense.shape[1]), bf16),
-            pltpu.VMEM((tensor - 1, small.shape[0], lanes), f32),
-            pltpu.VMEM((count - 1, small.shape[0], lanes), f32),
-            pltpu.VMEM((small.shape[0], lanes), f32),
-            pltpu.VMEM((small.shape[0], lanes), f32),
-            pltpu.VMEM((small.shape[0], lanes), f32),
-            pltpu.VMEM((small.shape[0], lanes), f32),
-            pltpu.VMEM(small.shape, f32),
-            dma((1, count - 1)),
-            dma((1, count - 1)),
-            dma((1,)),
-            dma((2, tensor - 1)),
-            dma((2, tensor - 1)),
-            dma((count - 1,)),
-            dma((count - 1,)),
-            dma((1,)),
-            dma((1,)),
-            pltpu.VMEM(small.shape, f32),
-            *bring.sems,
-            *beside.sems,
-        ],
-        compiler_params=params(7),
-    )(*small_parts, dense.reshape(count, rows, dense.shape[1]), *beside.inputs)
-    return found[0], found[1], beside.results(found[2:])
 
 
 def prepare_kernel(lengths, dealing, order, routes, attn_gain, expert_gain, router, freqs,
@@ -1430,51 +1512,39 @@
     saved = (state0, state1)
     streams = (tokens_in, out0)
 
-    def experts(layer, out_grad, jobs):
+    def experts(layer, out_grad, traded, jobs):
         mid, expert_rows, qs, keys, values, probs, gate, ai, x, gated, attended, pre = saved[layer]
-        (mid_grad, router_part, gain_part, pair, down), done = experts_back(
+        return experts_back(
             layer, gains, own, other, out_grad, (mid, gate, expert_rows, pre), (x, gated), masks,
-            Beside(jobs)
+            traded, Beside(jobs)
         )
-        return mid_grad, (gain_part, router_part), [FirstStage(pair, 1), FirstStage(down, 2)], done
-
-    def attention(layer, mid_grad, jobs):
+
+    def attention(layer, mid_grad, ending, jobs):
         mid, expert_rows, qs, keys, values, probs, gate, ai, x, gated, attended, pre = saved[layer]
-        (grad, gain_part, dense), done = attention_back(
+        return attention_back(
             layer, gains, own, other, mid_grad, streams[layer], (qs, keys, values, probs),
-            (ai, attended), tables, Beside(jobs)
+            (ai, attended), tables, ending, Beside(jobs)
         )
-        return grad, gain_part, dense, done
-
-    def second(layer, sums):
-        return [Bring(layer, kind, v) for pair in sums for kind, v in zip(("column", "row"), pair)]
-
-    mid_grad, small1, stage, _ = experts(1, out_cotangent, [])
-    grad1, gain1, dense1, sums = attention(1, mid_grad, stage)
-    mid_grad, small0, stage, (*parts1, dense1) = experts(
-        0, grad1.astype(bf16), second(1, sums) + [Scatter(dense1)]
+
+    (mid_grad, router1, gain1, pair, down, layer_outputs), _ = experts(1, out_cotangent, (out0, out1), [])
+    (grad1, attn_gain1, dense1), sums = attention(
+        1, mid_grad, (), [FirstStage(pair, 1), FirstStage(down, 2)]
     )
-    grad0, gain0, dense0, (*sums, dense1) = attention(
-        0, mid_grad, stage + [Bring(1, "all", dense1)]
+    jobs = [Bring(1, kind, v) for stage in sums for kind, v in zip(("column", "row"), stage)]
+    (mid_grad, router0, gain0, pair, down), (*parts1, dense1) = experts(
+        0, grad1, (), jobs + [DenseSum(dense1, 1)]
     )
-    small, dense0, parts0 = finish(
-        (small0[1], gain0, small0[0], small1[1], gain1, small1[0]), dense0, 0, Beside(second(0, sums))
+    (input_grads, small, dense0), parts0 = attention(
+        0, mid_grad, (router0, gain0, router1, attn_gain1, gain1, grad1),
+        [FirstStage(pair, 1, 0), FirstStage(down, 2, 0)]
     )
-
-    def by_layer(zero, one):
-        mine = jnp.where(first, zero, one)
-        theirs = swapped(jnp.where(first, one, zero))
-        return jnp.where(first, jnp.stack([mine, theirs]), jnp.stack([theirs, mine]))[None]
-
-    layer_outputs = by_layer(out0, out1)
-    input_grads = by_layer(grad0, grad1)
-
+    parts0 = [v for stage in parts0 for v in stage]
     query, key, value, output, gate, up, down = assemble((parts0, parts1), (dense0, dense1), qw, kw)
     small = jnp.where(first, small[: small.shape[0] // 2], small[small.shape[0] // 2 :])
     router_grad, attn_gain_grad, expert_gain_grad = small[:E].T, small[E : E + 1], small[E + 1 : E + 2]
     return (
-        layer_outputs,
-        input_grads,
+        layer_outputs[None],
+        input_grads[None],
         attn_gain_grad,
         query[None],
         key[None],

time: 560 us -> 511 us (0.912); the launches traced: 553 us -> 510 us
  other arithmetic: 27.3 us -> 0.03 us
  starting transfers between devices: 11.8 us -> 0 us
    convert_element_type x9 -> x0, other arithmetic: 17.7 us -> none  [the longest x8 17 us: results(): return (row.astype(bf16), col.astype(bf16))]
    ppermute x2 -> x0, starting transfers between devices: 11.8 us -> none  [swapped(): return lax.ppermute(value, 'section', [(0, 1), (1, 0)])]
    pallas_call x5 -> x4, Pallas kernels: 331 us -> 327 us  [the longest x2 186 us: attention_back(): pl.pallas_call(functools.partial(attention_back_kernel, layer, count, las...]
  transfers between devices with their start and end apart: 2 -> 0, of which waited for: 0 -> 0; matrix products, arithmetic and copies ran while one was open for 5% -> 0% of each run, Pallas kernels for 62% -> 0%
where the time goes in v4:
time: 511 us; the launch traced here: 510 us
  Pallas kernels  500 us (98%)
  local copies, waits for them, and re-layouts  9.71 us (2%)
    pallas_call x2, Pallas kernels, attention_back(): pl.pallas_call(functools.partial(attention_back_kernel, layer, count, las...  186 us
    pallas_call x2, Pallas kernels, layer_forward(): pl.pallas_call(functools.partial(forward_kernel, layer, count, swap), nam...  157 us
    pallas_call x2, Pallas kernels, experts_back(): pl.pallas_call(functools.partial(experts_back_kernel, layer, count, trade...  141 us
    pallas_call x1, Pallas kernels, assemble(): pl.pallas_call(assemble_kernel, name='assemble', out_shape=(shape((depth,...  11.2 us

profile of v4, /device:TPU:0, one launch (start us, length us, event | category | flops | bytes accessed | tf_op | source)
XLA Modules:
  0.0 510.3 jit_solution(7988190206607621989)
XLA Ops:
  0.6 1.7 copy.29
  2.4 1.6 copy.28
  3.9 0.6 broadcast_in_dim_tile.3.freqs
  4.5 4.9 prepare.1
  9.4 79.8 %layer_forward_0.1 = (f32[64,1536]{1,0:T(8,128)}, f32[64,1536]{1,0:T(8,128)}, bf16[64,1536]{1,0:T(8,128)(2,1)}, bf16[1536,64]{1,0:T(8,128)(2,1)}, bf16[256,128]{...) custom-call(bf16[2,64,1536]{2,1,0:T(8,128)(2,1)} %refs_1_.1, ...), custom_call_target="tpu_custom_call" | custom-call | tf_op jit(solution)/shard_map/layer_forward_0/pallas_call | solution.py:847
  89.3 76.9 %layer_forward_1.1 = (f32[64,1536]{1,0:T(8,128)}, f32[64,1536]{1,0:T(8,128)}, bf16[64,1536]{1,0:T(8,128)(2,1)}, bf16[1536,64]{1,0:T(8,128)(2,1)}, bf16[256,128]{...) custom-call(f32[64,1536]{1,0:T(8,128)} %get-tuple-element.98.refs_0_, ...), custom_call_target="tpu_custom_call" | custom-call | tf_op jit(solution)/shard_map/layer_forward_1/pallas_call | solution.py:847
  166.2 71.6 %experts_back_1.1 = (f32[64,1536]{1,0:T(8,128)}, f32[16,1536]{1,0:T(8,128)}, f32[1,1536]{1,0:T(1,128)}, bf16[16,768,256]{2,1,0:T(8,128)(2,1)}, bf16[16,128,768]{2,1,0:T(8,128)(2,1)}, /*index=5*/f32[2,64,1536]{2,1,0:T(8,128)}) custom-call(bf16[2,64,1536]{2,1,0:T(8,128)(2,1)} %refs_0_.3, f32[64,1536]{1,0:T(8,128)} %get-tuple-element.106.refs_1_, ...), custom_call_target="tpu_custom_call" | custom-call | tf_op jit(solution)/shard_map/experts_back_1/pallas_call | solution.py:1072
  237.8 60.4 %attention_back_1.1 = (f32[64,1536]{1,0:T(8,128)}, f32[1,1536]{1,0:T(1,128)}, bf16[768,1024]{1,0:T(8,128)(2,1)}, bf16[2,4,384,256]{3,2,1,0:T(8,128)(2,1)}, bf16[...) custom-call(f32[64,1536]{1,0:T(8,128)} %get-tuple-element.114.refs_0_, ...), custom_call_target="tpu_custom_call" | custom-call | tf_op jit(solution)/shard_map/attention_back_1/pallas_call | solution.py:1282
  298.2 69.6 %experts_back_0.1 = (f32[64,1536]{1,0:T(8,128)}, f32[16,1536]{1,0:T(8,128)}, f32[1,1536]{1,0:T(1,128)}, bf16[16,768,256]{2,1,0:T(8,128)(2,1)}, bf16[16,128,768]{...) custom-call(f32[64,1536]{1,0:T(8,128)} %get-tuple-element.123.refs_0, ...), custom_call_target="tpu_custom_call" | custom-call | tf_op jit(solution)/shard_map/experts_back_0/pallas_call | solution.py:1072
  367.9 0.0 copy-start
  367.9 125.3 %attention_back_0.1 = (f32[2,64,1536]{2,1,0:T(8,128)}, f32[48,1536]{1,0:T(8,128)}, bf16[2,4,192,1024]{3,2,1,0:T(8,128)(2,1)}, bf16[2,2,4,384,256]{4,3,2,1,0:T(8,...) custom-call(f32[64,1536]{1,0:T(8,128)} %get-tuple-element.135.refs_0, ...), custom_call_target="tpu_custom_call" | custom-call | tf_op jit(solution)/shard_map/attention_back_0/pallas_call | solution.py:1282
  493.2 0.0 copy-done
  493.2 0.0 copy-start.1
  493.2 1.4 copy-done.1
  494.6 0.0 copy-start.2
  494.6 1.4 copy-done.2
  496.0 0.0 copy-start.5
  496.0 0.0 copy-start.3
  496.0 0.0 copy-start.4
  496.0 11.2 %assemble.1 = (f32[1536,384]{1,0:T(8,128)}, f32[1536,128]{1,0:T(8,128)}, f32[1536,128]{1,0:T(8,128)}, f32[384,1536]{1,0:T(8,128)}, f32[4,1536,128]{2,1,0:T(8,128...) custom-call(s32[1]{0:T(128)} %bitcast.18.section, bf16[2,2,4,384,256]{4,3,2,1,0:T(8,128)(2,1)} %get-tuple-element.151.refs_0_, ...), custom_call_target="tpu_custom_call" | custom-call | tf_op jit(solution)/shard_map/assemble/pallas_call | solution.py:1468
  507.2 0.0 copy-done.5
  507.2 0.6 slice_bitcast_fusion
  507.9 0.6 fusion
  508.5 0.0 copy-done.3
  508.5 0.9 copy.32
  509.4 0.0 copy-done.4
  509.4 0.9 copy.33
  (3 shorter events, 0.0 us)
Async XLA Ops:
  367.9 125.3 %copy-start = (bf16[2,2,4,128,384]{4,3,2,1,0:T(8,128)(2,1)S(1)}, bf16[2,2,4,128,384]{4,3,2,1,0:T(8,128)(2,1)}, u32[]{:S(2)}) copy-start(bf16[2,2,4,128,384]{4,3,2,1,0:T(8,128)(2,1)} %get-tuple-element.157.refs_6_) | copy-start | bytes 4718596
  493.2 1.4 copy-start.1
  494.6 1.4 copy-start.2
  496.0 11.2 %copy-start.5 = (f32[48,1536]{1,0:T(8,128)S(1)}, f32[48,1536]{1,0:T(8,128)}, u32[]{:S(2)}) copy-start(f32[48,1536]{1,0:T(8,128)} %get-tuple-element.150) | copy-start | bytes 884740
  496.0 12.5 %copy-start.3 = (f32[2,64,1536]{2,1,0:T(8,128)S(1)}, f32[2,64,1536]{2,1,0:T(8,128)}, u32[]{:S(2)}) copy-start(f32[2,64,1536]{2,1,0:T(8,128)} %get-tuple-element.113) | copy-start | bytes 2359300
  496.0 13.4 %copy-start.4 = (f32[2,64,1536]{2,1,0:T(8,128)S(1)}, f32[2,64,1536]{2,1,0:T(8,128)}, u32[]{:S(2)}) copy-start(f32[2,64,1536]{2,1,0:T(8,128)} %get-tuple-element.149) | copy-start | bytes 2359300

commit v5 on v4

--- a/solution.py
+++ b/solution.py
@@ -86,12 +86,14 @@
 
 
 class Bring:
-    def __init__(self, layer, kind, value, in_vmem=False):
+    def __init__(self, layer, kind, value, in_vmem=False, target=None):
         self.layer, self.kind, self.in_vmem = layer, kind, in_vmem
+        self.whole = kind == "all" or target is not None
+        self.target = target or (lambda outputs, core, place: outputs[0].at[core, place])
         count = lax.axis_size("dp")
         outer, inner = factors(count)
         self.size = {"column": outer, "row": inner, "all": count}[kind]
-        block = value.shape if kind == "all" else value.shape[1:]
+        block = value.shape if self.whole else value.shape[1:]
         self.inputs = [value]
         self.outputs = [jax.ShapeDtypeStruct((2, self.size, *block), value.dtype)]
         self.sems = [dma((self.size,)), dma((2, self.size)), dma((2,))]
@@ -113,11 +115,11 @@
     def parts(self, inputs, outputs, sems):
         core = lax.axis_index("section")
         mine, _ = self.place(0)
-        target = outputs[0].at[core, mine]
+        target = self.target(outputs, core, mine)
         recv = sems[1].at[core, mine]
 
         def source(place):
-            return inputs[0] if self.kind == "all" else inputs[0].at[place]
+            return inputs[0] if self.whole else inputs[0].at[place]
 
         sent = []
         for step in range(1, self.size):
@@ -154,10 +156,10 @@
         sent, across, local = self.parts(inputs, outputs, sems)
         core = lax.axis_index("section")
         here = core == self.layer
-        block = inputs[0] if self.kind == "all" else inputs[0].at[0]
+        block = inputs[0] if self.whole else inputs[0].at[0]
 
         def arrived(which, place):
-            remote(block, outputs[0].at[which, place], sems[0].at[0], sems[1].at[which, place],
+            remote(block, self.target(outputs, which, place), sems[0].at[0], sems[1].at[which, place],
                    core_peer()).wait_recv()
 
         for copy in sent:
@@ -187,9 +189,11 @@
     def __init__(self, value, axis, layer=None):
         self.count = lax.axis_size("dp")
         outer, inner = factors(self.count)
-        self.inputs = [value.reshape((outer, inner, value.shape[0] // self.count) + value.shape[1:])]
+        self.blocks = (outer, inner, value.shape[0] // self.count, *value.shape[1:])
+        inside = isinstance(value, jax.ShapeDtypeStruct)
+        self.inputs = [] if inside else [value.reshape(self.blocks)]
         self.axis = axis
-        shape = list(self.inputs[0].shape[2:])
+        shape = list(self.blocks[2:])
         shape[axis] //= 2
         self.shape = shape
         sums = [
@@ -281,52 +285,124 @@
 
 
 class DenseSum:
-    kind = "all"
-
     def __init__(self, value, layer):
         count = lax.axis_size("dp")
-        self.rows, width = value.shape[0] // count, value.shape[1]
-        self.bring = Bring(layer, "all", jax.ShapeDtypeStruct((self.rows, width), bf16), True)
-        self.inputs = [value]
-        self.outputs = self.bring.outputs
+        outer, inner = factors(count)
+        rows, width = value.shape[2:]
+        half = width // 2
+        self.half = half
+        inside = isinstance(value, jax.ShapeDtypeStruct)
+        self.inputs = [] if inside else [value]
+        self.outputs = [jax.ShapeDtypeStruct((2, *value.shape), bf16)]
+
+        def buffer(*lead):
+            return pltpu.VMEM((*lead, rows, half), bf16)
+
+        self.brings = [
+            Bring(layer, "row", jax.ShapeDtypeStruct((outer, rows, half), bf16), True,
+                  lambda outputs, core, place: outputs[0].at[core, :, place, :, pl.ds(0, half)]),
+            Bring(layer, "column", jax.ShapeDtypeStruct((inner, rows, half), bf16), True,
+                  lambda outputs, core, place: outputs[0].at[core, place, :, :, pl.ds(half, half)]),
+        ]
+        pairs = inner + outer - 2
         self.sems = [
-            dma((count - 1,)),
-            dma((count - 1,)),
-            pltpu.VMEM((count - 1, self.rows, width), bf16),
-            pltpu.VMEM((self.rows, width), bf16),
-            dma((1,)),
-            *self.bring.sems,
+            buffer(inner - 1, outer),
+            buffer(outer - 1, inner),
+            buffer(outer),
+            buffer(inner),
+            buffer(outer - 1),
+            buffer(inner - 1),
+            buffer(outer),
+            buffer(inner),
+            dma((2,)),
+            *[dma((pairs,)) for _ in range(6)],
+            *[v for bring in self.brings for v in bring.sems],
         ]
 
-    def copies(self, inputs, sems):
+    def numbered(self, found, sems, first):
+        return [
+            remote(src, dst, sems[first].at[index], sems[first + 1].at[index], device)
+            for index, (src, dst, device) in enumerate(found)
+        ]
+
+    def sent(self, inputs, sems):
         count = lax.axis_size("dp")
-        me = lax.axis_index("dp")
-
-        def block(place):
-            return inputs[0].at[pl.ds(pl.multiple_of(place * self.rows, self.rows), self.rows)]
-
-        found = [pltpu.make_async_copy(block(me), sems[3], sems[4].at[0])]
-        for step in range(1, count):
-            place = lax.rem(me + step, count)
-            found.append(
-                remote(block(place), sems[2].at[step - 1], sems[0].at[step - 1], sems[1].at[step - 1],
-                       {"dp": place})
-            )
+        across, along = near_groups(count)
+        _, _, mo, mi = group_place(count)
+        value = inputs[0]
+        low, high = pl.ds(0, self.half), pl.ds(self.half, self.half)
+        found = [
+            (value.at[:, place, :, low], sems[0].at[slot], device)
+            for slot, (place, device) in enumerate(across)
+        ] + [
+            (value.at[place, :, :, high], sems[1].at[slot], device)
+            for slot, (place, device) in enumerate(along)
+        ]
+        loads = [
+            pltpu.make_async_copy(value.at[:, mi, :, low], sems[2], sems[8].at[0]),
+            pltpu.make_async_copy(value.at[mo, :, :, high], sems[3], sems[8].at[1]),
+        ]
+        return self.numbered(found, sems, 9) + loads
+
+    def sums(self, sems):
+        across, along = near_groups(lax.axis_size("dp"))
+        found = [
+            (sems[2].at[place], sems[4].at[slot], device) for slot, (place, device) in enumerate(along)
+        ] + [
+            (sems[3].at[place], sems[5].at[slot], device) for slot, (place, device) in enumerate(across)
+        ]
+        return self.numbered(found, sems, 11)
+
+    def blocks(self, sems):
+        count = lax.axis_size("dp")
+        across, along = near_groups(count)
+        _, _, mo, mi = group_place(count)
+        found = [(sems[6].at[mo], sems[6].at[mo], device) for _, device in along]
+        found += [(sems[7].at[mi], sems[7].at[mi], device) for _, device in across]
+        return self.numbered(found, sems, 13)
+
+    def onward(self, outputs, sems):
+        place = 15
+        found = []
+        for index, bring in enumerate(self.brings):
+            found.append((bring, [sems[6 + index]], outputs, sems[place : place + len(bring.sems)]))
+            place += len(bring.sems)
         return found
 
     def start(self, inputs, outputs, sems):
-        start_all(self.copies(inputs, sems))
-
-    def middle(self, inputs, outputs, sems):
-        wait_all(self.copies(inputs, sems))
-        total = sems[3][...].astype(f32)
-        for slot in range(sems[2].shape[0]):
-            total = total + sems[2][slot].astype(f32)
-        sems[3][...] = total.astype(bf16)
-        self.bring.start([sems[3]], outputs, sems[5:])
+        start_all(self.sent(inputs, sems))
+
+    def middle1(self, inputs, outputs, sems):
+        wait_all(self.sent(inputs, sems))
+        for total, landed in ((sems[2], sems[0]), (sems[3], sems[1])):
+            for place in range(total.shape[0]):
+                value = total[place].astype(f32)
+                for slot in range(landed.shape[0]):
+                    value = value + landed[slot, place].astype(f32)
+                total[place] = value.astype(bf16)
+        start_all(self.sums(sems))
+
+    def middle2(self, inputs, outputs, sems):
+        wait_all(self.sums(sems))
+        _, _, mo, mi = group_place(lax.axis_size("dp"))
+        for total, landed, whole, mine in (
+            (sems[2], sems[4], sems[6], mo),
+            (sems[3], sems[5], sems[7], mi),
+        ):
+            value = total[mine].astype(f32)
+            for slot in range(landed.shape[0]):
+                value = value + landed[slot].astype(f32)
+            whole[mine] = value.astype(bf16)
+        start_all(self.blocks(sems))
+
+    def middle3(self, inputs, outputs, sems):
+        wait_all(self.blocks(sems))
+        for bring, *refs in self.onward(outputs, sems):
+            bring.start(*refs)
 
     def wait(self, inputs, outputs, sems):
-        self.bring.wait([sems[3]], outputs, sems[5:])
+        for bring, *refs in self.onward(outputs, sems):
+            bring.wait(*refs)
 
     def results(self, outputs):
         return outputs[0]
@@ -445,6 +521,12 @@
     return [{"dp": group, "section": which} for group in groups for which in (core, 1 - core)]
 
 
+def whole_group():
+    count = lax.axis_size("dp")
+    me = lax.axis_index("dp")
+    return both_cores([lax.rem(me + step, count) for step in range(1, count)])
+
+
 class Beside:
     def __init__(self, jobs):
         self.jobs = jobs
@@ -454,9 +536,6 @@
 
     def peers(self):
         count = lax.axis_size("dp")
-        if any(getattr(job, "kind", "") == "all" for job in self.jobs):
-            me = lax.axis_index("dp")
-            return both_cores([lax.rem(me + step, count) for step in range(1, count)])
         if not self.jobs:
             return []
         across, along = near_groups(count)
@@ -473,8 +552,8 @@
     def start(self, *refs):
         self.each(refs, lambda job: job.start)
 
-    def middle(self, *refs):
-        self.each(refs, lambda job: getattr(job, "middle", lambda *refs: None))
+    def middle(self, *refs, step="middle"):
+        self.each(refs, lambda job: getattr(job, step, lambda *refs: None))
 
     def wait(self, *refs):
         self.each(refs, lambda job: job.wait)
@@ -487,9 +566,9 @@
         return found
 
 
-def spread(count, buf, rows, sends, recvs):
+def spread(count, buf, rows, sends, recvs, columns=slice(None)):
     me = lax.axis_index("tensor")
-    own = buf.at[pl.ds(pl.multiple_of(me * rows, rows), rows)]
+    own = buf.at[pl.ds(pl.multiple_of(me * rows, rows), rows), columns]
     copies = []
     for step in range(1, count):
         copies.append(
@@ -643,7 +722,8 @@
     joint_s, output_s, gu_s, down_s = scratch
     (ag1, ag2, part, landing1, landing2, pre_s, gated_s, attended_s, send_s, recv_s, attn_sems,
      expert_sems, pre_sems, save_sems) = refs[:14]
-    swap_sems = refs[14:]
+    if swap:
+        swap_sems = refs[14:]
     rows, width = stream.shape
     tokens = ag1.shape[0]
     experts = gu_s.shape[0]
@@ -755,18 +835,17 @@
     expert_rows = (mid * norm_scale(mid) * expert_gain[...]).astype(bf16)
     expert_rows_out[...] = expert_rows
     ag2[own_rows, :] = expert_rows
-    second = spread(count, ag2, rows, send_s.at[2], recv_s.at[2])
-    start_all(second)
-    wait_all(second)
-    saved.append(pltpu.make_async_copy(ag2, expert_in_out, save_sems.at[2]))
-    saved[2].start()
-    logits = dot(ag2[...], router[...], NN)
-    chosen = picked[...] > 0
-    top = jnp.max(jnp.where(chosen, logits, masked_score), axis=1, keepdims=True)
-    weighed = jnp.where(chosen, jnp.exp(logits - top), 0.0)
-    gate_out[...] = weighed / jnp.sum(weighed, axis=1, keepdims=True)
-
-    def expert_step(expert, carry):
+    split = width // 2
+    columns = pl.ds(0, split), pl.ds(split, split)
+    early, late = [
+        spread(count, ag2, rows, send_s.at[index], recv_s.at[index], lanes)
+        for index, lanes in zip((2, 7), columns)
+    ]
+    start_all(early)
+    start_all(late)
+    wait_all(early)
+
+    def first_step(expert, carry):
         if swap:
 
             @pl.when(jnp.logical_not(use_own) & (expert + lead < experts))
@@ -776,7 +855,21 @@
                 start_expert(other, expert + lead)
 
         either(use_own, own, other, lambda w: wait_expert(w, expert))
-        pre = dot(ag2[...], gu_s[expert], NN)
+        pre_s[expert] = dot(ag2[:, columns[0]], gu_s[expert, columns[0], :], NN)
+        return carry
+
+    lax.fori_loop(0, experts, first_step, 0)
+    wait_all(late)
+    saved.append(pltpu.make_async_copy(ag2, expert_in_out, save_sems.at[2]))
+    saved[2].start()
+    logits = dot(ag2[...], router[...], NT)
+    chosen = picked[...] > 0
+    top = jnp.max(jnp.where(chosen, logits, masked_score), axis=1, keepdims=True)
+    weighed = jnp.where(chosen, jnp.exp(logits - top), 0.0)
+    gate_out[...] = weighed / jnp.sum(weighed, axis=1, keepdims=True)
+
+    def expert_step(expert, carry):
+        pre = pre_s[expert] + dot(ag2[:, columns[1]], gu_s[expert, columns[1], :], NN)
         pre_s[expert] = pre
         pltpu.make_async_copy(pre_s.at[expert], pre_out.at[expert], pre_sems.at[expert]).start()
         gate_pre, up_pre = pre[:, :hidden_width], pre[:, hidden_width:]
@@ -875,8 +968,8 @@
             pltpu.VMEM((experts, tokens, 2 * hidden_width), f32),
             pltpu.VMEM((tokens, experts * hidden_width), bf16),
             pltpu.VMEM((tokens, qw), bf16),
-            dma((7, count - 1)),
-            dma((7, count - 1)),
+            dma((8, count - 1)),
+            dma((8, count - 1)),
             dma((4,)),
             dma((3, experts)),
             dma((experts,)),
@@ -898,7 +991,7 @@
     return value_grad, gain_grad
 
 
-def experts_back_kernel(layer, count, trade, beside, *refs):
+def experts_back_kernel(layer, count, trade, stage, beside, *refs):
     refs = list(refs)
 
     def take(number):
@@ -906,24 +999,26 @@
         del refs[:number]
         return taken
 
-    out_grad_in, mid, expert_gains, routers, kepts, gate, expert_rows, pre_in = take(8)
+    out_grad, mid, expert_gains, routers, kepts, gate, expert_rows, pre_in = take(8)
     expert_gain, router, kept = expert_gains.at[layer], routers.at[layer], kepts.at[layer]
-    out_grad = out_grad_in if layer == 0 else out_grad_in.at[lax.axis_index("section")]
     x_in, gated_in = take(2)
     own, other = take(3), take(3)
     traded = take(2 if trade else 0)
     beside_in = take(len(beside.inputs))
-    mid_grad_out, router_out, expert_gain_out, pair_out, down_out = take(5)
+    mid_grad_out, router_out, expert_gain_out, pair_out = take(4)
     traded_out = take(1 if trade else 0)
+    stage_out = take(len(stage.outputs))
     beside_out = take(len(beside.outputs))
     scratch = take(2)
     gu_s, down_s = scratch
     (ag1, part, landing1, pre_s, gpu_s, acc, gate_part, gate_land, og_s, gpu_peer, x_s, turned_x,
-     gated_s, turned_gated, pair_s, down_grad_s, send_s, recv_s, expert_sems, pre_sems, core_send,
-     core_recv, local_sems, hand_send, hand_recv, save_sems) = take(26)
+     gated_s, hidden_s, pair_s, down_grad_s, send_s, recv_s, expert_sems, pre_sems, core_send, core_recv,
+     local_sems, hand_send, hand_recv, save_sems) = take(26)
     trade_sems = take(len(trade.sems) if trade else 0)
+    stage_refs = ([down_grad_s], stage_out, take(len(stage.sems)))
     beside_refs = (beside_in, beside_out, refs)
     rows, width = mid.shape
+    tokens = ag1.shape[0]
     experts = gu_s.shape[0]
     hidden_width = gu_s.shape[2] // 2
     me = lax.axis_index("tensor")
@@ -936,10 +1031,17 @@
         pltpu.make_async_copy(pre_in.at[expert], pre_s.at[expert], pre_sems.at[expert]).start()
         return carry
 
-    ag1[own_rows, :] = out_grad[...].astype(bf16)
-    greet(tensor_peers(count) + [core_peer()] + beside.peers())
-    first = spread(count, ag1, rows, send_s.at[0], recv_s.at[0])
-    start_all(first)
+    everyone = Beside([*beside.jobs, stage])
+    if layer:
+        ag1[own_rows, :] = out_grad[lax.axis_index("section")]
+        greet(tensor_peers(count) + [core_peer()] + everyone.peers())
+        first = spread(count, ag1, rows, send_s.at[0], recv_s.at[0])
+        start_all(first)
+    else:
+        ag1[own_rows, :] = out_grad[...].astype(bf16)
+        greet(tensor_peers(count) + [core_peer()] + everyone.peers())
+        first = spread(count, ag1, rows, send_s.at[0], recv_s.at[0])
+        start_all(first)
     lax.fori_loop(0, experts, start_expert, 0)
     loads = hand_halves(x_in, x_s, [v.at[0] for v in (local_sems, hand_send, hand_recv)])
     loads += hand_rows(gated_in, gated_s, [v.at[1] for v in (local_sems, hand_send, hand_recv)])
@@ -949,16 +1051,22 @@
     if trade:
         trade.start(*traded, trade_sems)
     gate_part[...] = jnp.zeros_like(gate_part)
-    wait_all(loads)
-    turned_x[...] = x_s[...].T
-    tokens = ag1.shape[0]
-
-    def turn_gated(expert, carry):
-        lanes = pl.ds(pl.multiple_of(expert * hidden_width, hidden_width), hidden_width)
-        turned_gated[lanes, :] = gated_s[:, lanes].T
+
+    def ready_step(expert, carry):
+        pltpu.make_async_copy(pre_in.at[expert], pre_s.at[expert], pre_sems.at[expert]).wait()
+        gate_pre = pre_s[expert, :, pl.ds(0, hidden_width)]
+        up_pre = pre_s[expert, :, pl.ds(hidden_width, hidden_width)]
+        sig = 1.0 / (1.0 + jnp.exp(-gate_pre))
+        act = gate_pre * sig
+        hidden_s[expert] = (act * up_pre).astype(bf16)
+        weight = column(gate[...] * kept[...], expert)
+        pre_s[expert, :, pl.ds(0, hidden_width)] = (
+            weight * up_pre * (sig * (1.0 + gate_pre * (1.0 - sig)))
+        )
+        pre_s[expert, :, pl.ds(hidden_width, hidden_width)] = weight * act
         return carry
 
-    lax.fori_loop(0, experts, turn_gated, 0)
+    lax.fori_loop(0, experts, ready_step, 0)
     wait_all(first)
     core = lax.axis_index("section")
     half = width // 2
@@ -968,68 +1076,78 @@
                og_s.at[pl.ds(tokens, tokens)], core_send.at[0], core_recv.at[0], core_peer())
     ]
     handed[0].start()
-
-    def expert_step(expert, carry):
-        either(use_own, own, other,
-               lambda w: [c.wait() for c in weight_copies(w, scratch, expert_sems, expert)])
-        pltpu.make_async_copy(pre_in.at[expert], pre_s.at[expert], pre_sems.at[expert]).wait()
-        lanes = pl.ds(pl.multiple_of(expert * hidden_width, hidden_width), hidden_width)
+    wait_all(loads)
+    handed[0].wait()
+    _, inner, per_group = stage.blocks[:3]
+
+    def down_step(index, carry):
+        lanes = pl.ds(pl.multiple_of(index * 2 * hidden_width, 2 * hidden_width), 2 * hidden_width)
+        grads = dot(gated_s[:, lanes], og_s[...], TN).astype(bf16)
+        for k in range(2):
+            expert = 2 * index + k
+            group, place = expert // per_group, lax.rem(expert, per_group)
+            down_grad_s[group // inner, lax.rem(group, inner), place] = grads[
+                k * hidden_width : (k + 1) * hidden_width
+            ]
+        return carry
+
+    lax.fori_loop(0, experts // 2, down_step, 0)
+    stage.start(*stage_refs)
+    beside.middle(*beside_refs, step="middle1")
+
+    def expert_step(index, carry):
+        pair = (2 * index, 2 * index + 1)
+        for expert in pair:
+            either(use_own, own, other,
+                   lambda w: [c.wait() for c in weight_copies(w, scratch, expert_sems, expert)])
+        lanes = pl.ds(pl.multiple_of(index * 2 * hidden_width, 2 * hidden_width), 2 * hidden_width)
         plain = dot(ag1[...], down_s[lanes, :], NT)
-        gate_pre = pre_s[expert, :, pl.ds(0, hidden_width)]
-        up_pre = pre_s[expert, :, pl.ds(hidden_width, hidden_width)]
-        sig = 1.0 / (1.0 + jnp.exp(-gate_pre))
-        act = gate_pre * sig
-        hidden = (act * up_pre).astype(bf16).astype(f32)
-        held = column(kept[...], expert)
-        weight = column(gate[...], expert) * held
-        summed = jnp.sum(hidden * plain, axis=1, keepdims=True) * held
         lane = lax.broadcasted_iota(jnp.int32, gate_part.shape, 1)
-        gate_part[...] += jnp.where(lane == expert, summed, 0.0)
-        hidden_grad = plain * weight
-        gpu_s[expert, :, pl.ds(0, hidden_width)] = (
-            hidden_grad * up_pre * (sig * (1.0 + gate_pre * (1.0 - sig)))
-        ).astype(bf16)
-        gpu_s[expert, :, pl.ds(hidden_width, hidden_width)] = (hidden_grad * act).astype(bf16)
-        back = dot(gpu_s[expert], gu_s[expert], NT)
-
-        @pl.when(expert == 0)
+        for k, expert in enumerate(pair):
+            value = plain[:, k * hidden_width : (k + 1) * hidden_width]
+            summed = jnp.sum(hidden_s[expert].astype(f32) * value, axis=1, keepdims=True)
+            gate_part[...] += jnp.where(lane == expert, summed, 0.0)
+            for cut in (pl.ds(0, hidden_width), pl.ds(hidden_width, hidden_width)):
+                gpu_s[expert, :, cut] = (value * pre_s[expert, :, cut]).astype(bf16)
+        back = dot(gpu_s[pair[0]], gu_s[pair[0]], NT) + dot(gpu_s[pair[1]], gu_s[pair[1]], NT)
+
+        @pl.when(index == 0)
         def _():
             acc[...] = back
 
-        @pl.when(expert > 0)
+        @pl.when(index > 0)
         def _():
             acc[...] += back
 
         return carry
 
-    lax.fori_loop(0, experts, expert_step, 0)
+    lax.fori_loop(0, experts // 2, expert_step, 0)
+    gate_part[:, :experts] = gate_part[:, :experts] * kept[...]
     handed.append(remote(gpu_s, gpu_peer, core_send.at[1], core_recv.at[1], core_peer()))
     handed[1].start()
     part[...] = acc[...].astype(bf16)
     copies = deal_out(count, part, rows, slice(None), landing1, send_s.at[1], recv_s.at[1])
     copies += deal_out(count, gate_part, rows, slice(None), gate_land, send_s.at[2], recv_s.at[2])
-    wait_all(handed)
+    beside.middle(*beside_refs, step="middle2")
+    turned_x[...] = x_s[...].T
+    wait_all(handed[1:])
 
     def saves(expert):
-        lanes = pl.ds(pl.multiple_of(expert * hidden_width, hidden_width), hidden_width)
-        return (
-            pltpu.make_async_copy(pair_s.at[expert], pair_out.at[expert], save_sems.at[0, expert]),
-            pltpu.make_async_copy(down_grad_s.at[lanes], down_out.at[expert], save_sems.at[1, expert]),
-        )
+        return [pltpu.make_async_copy(pair_s.at[expert], pair_out.at[expert], save_sems.at[expert])]
 
     def grads_step(expert, carry):
-        lanes = pl.ds(pl.multiple_of(expert * hidden_width, hidden_width), hidden_width)
         pair_s[expert] = (
             dot(turned_x[:, :tokens], gpu_s[expert], NN)
             + dot(turned_x[:, tokens:], gpu_peer[expert], NN)
         ).astype(bf16)
-        down_grad_s[lanes, :] = dot(turned_gated[lanes, :], og_s[...], NN).astype(bf16)
         for copy in saves(expert):
             copy.start()
         return carry
 
     lax.fori_loop(0, experts, grads_step, 0)
-    beside.middle(*beside_refs)
+    beside.middle(*beside_refs, step="middle3")
+    if layer:
+        stage.middle(*stage_refs)
     wait_all(copies)
     in_grad = acc[own_rows, :]
     gate_grad = gate_part[own_rows, :]
@@ -1042,7 +1160,7 @@
         gate_rows * (gate_grad - jnp.sum(gate_rows * gate_grad, axis=1, keepdims=True))
     ).astype(bf16)
     router_out[...] = dot(logits_grad, expert_rows[...], TN)
-    in_grad = in_grad + dot(logits_grad, router[...], NT)
+    in_grad = in_grad + dot(logits_grad, router[...], NN)
     mid_part, expert_gain_grad = norm_back(mid[...], expert_gain[...], in_grad)
     expert_gain_out[...] = expert_gain_grad
     mid_grad_out[...] = ag1[own_rows, :].astype(f32) + mid_part
@@ -1055,6 +1173,9 @@
     lax.fori_loop(0, experts, finish_save, 0)
     if trade:
         trade.wait(traded[0], traded_out[0], trade_sems)
+    if not layer:
+        stage.middle(*stage_refs)
+    stage.wait(*stage_refs)
     beside.wait(*beside_refs)
 
 
@@ -1066,23 +1187,28 @@
     own, other = own[4:], other[4:]
     trade = Trade((rows, width)) if traded else None
     experts, depth, hidden_width = own[0].shape
+    stage = FirstStage(
+        jax.ShapeDtypeStruct((experts, hidden_width, width // 2), bf16), 2, layer if layer else None
+    )
     vmem = pl.BlockSpec(memory_space=pltpu.VMEM)
     hbm = pl.BlockSpec(memory_space=pl.ANY)
     shape = jax.ShapeDtypeStruct
     found = pl.pallas_call(
-        functools.partial(experts_back_kernel, layer, count, trade, beside),
+        functools.partial(experts_back_kernel, layer, count, trade, stage, beside),
         name=f"experts_back_{layer}",
         out_shape=(
             shape((rows, width), f32),
             shape((experts, width), f32),
             shape((1, width), f32),
             shape((experts, width // 2, 2 * hidden_width), bf16),
-            shape((experts, hidden_width, width // 2), bf16),
             *((shape((2, rows, width), f32),) if traded else ()),
+            *stage.outputs,
             *beside.outputs,
         ),
         in_specs=[vmem] * 7 + [hbm] * 9 + [vmem] * len(traded) + [hbm] * len(beside.inputs),
-        out_specs=(vmem, vmem, vmem, hbm, hbm) + (vmem,) * bool(traded) + (hbm,) * len(beside.outputs),
+        out_specs=(vmem, vmem, vmem, hbm)
+        + (vmem,) * bool(traded)
+        + (hbm,) * len(stage.outputs + beside.outputs),
         scratch_shapes=[
             pltpu.VMEM((experts, depth, 2 * hidden_width), bf16),
             pltpu.VMEM((experts * hidden_width, depth), bf16),
@@ -1099,23 +1225,25 @@
             pltpu.VMEM((2 * tokens, width // 2), bf16),
             pltpu.VMEM((width // 2, 2 * tokens), bf16),
             pltpu.VMEM((2 * tokens, experts * hidden_width), bf16),
-            pltpu.VMEM((experts * hidden_width, 2 * tokens), bf16),
+            pltpu.VMEM((experts, tokens, hidden_width), bf16),
             pltpu.VMEM((experts, width // 2, 2 * hidden_width), bf16),
-            pltpu.VMEM((experts * hidden_width, width // 2), bf16),
+            pltpu.VMEM(stage.blocks, bf16),
             pltpu.SemaphoreType.DMA((3, count - 1)),
             pltpu.SemaphoreType.DMA((3, count - 1)),
             pltpu.SemaphoreType.DMA((3, experts)),
             pltpu.SemaphoreType.DMA((experts,)),
-            *[pltpu.SemaphoreType.DMA((2,)) for _ in range(5)],
-            pltpu.SemaphoreType.DMA((2, experts)),
+            *[pltpu.SemaphoreType.DMA((3,)) for _ in range(5)],
+            pltpu.SemaphoreType.DMA((experts,)),
             *(trade.sems if trade else ()),
+            *stage.sems,
             *beside.sems,
         ],
         compiler_params=params(3 + layer),
     )(out_grad, mid, *gains[1:], masks[1], gate, expert_rows, pre, *pairs, *own, *other,
       *traded, *beside.inputs)
-    kept = 6 if traded else 5
-    return found[:kept], beside.results(found[kept:])
+    kept = 5 if traded else 4
+    parts = kept + len(stage.outputs)
+    return found[:kept], found[kept:parts], beside.results(found[parts:])
 
 
 def attention_back_kernel(layer, count, last, beside, *refs):
@@ -1161,7 +1289,7 @@
     use_own = lax.axis_index("section") == layer
     ag2[own_rows, :] = mid_grad[...].astype(bf16)
     everyone = Beside([*beside.jobs, dense_sum]) if last else beside
-    greet(tensor_peers(count) + [core_peer()] + everyone.peers())
+    greet(tensor_peers(count) + [core_peer()] + (whole_group() if last else everyone.peers()))
     first = spread(count, ag2, rows, send_s.at[0], recv_s.at[0])
     start_all(first)
     either(use_own, own, other, lambda w: [c.start() for c in attn_copies(w, scratch, attn_sems)])
@@ -1212,10 +1340,15 @@
         copies += deal_out(count, part, rows, columns, landing2, send_s.at[1 + t], recv_s.at[1 + t])
     wait_all(handed)
     wide = qw + 2 * kw
-    dense_s[:, :wide] = (
+    joint_grads = (
         dot(turned_ai[:, :tokens], joint_rows[...], NN) + dot(turned_ai[:, tokens:], joint_peer[...], NN)
     ).astype(bf16)
-    dense_s[:, wide:] = dot(ao_s[...], attended_s[...], TN).astype(bf16)
+    output_grads = dot(ao_s[...], attended_s[...], TN).astype(bf16)
+    outer, inner, depth = dense_s.shape[:3]
+    for block in range(outer * inner):
+        cut = slice(block * depth, (block + 1) * depth)
+        dense_s[block // inner, block % inner, :, :wide] = joint_grads[cut]
+        dense_s[block // inner, block % inner, :, wide:] = output_grads[cut]
     if last:
         dense_sum.start(*dense_refs)
     else:
@@ -1250,9 +1383,11 @@
     grad_s[...] = grad
     trade.start(grad_s, later_grad[0], trade_sems)
     beside.middle(*beside_refs)
+    dense_sum.middle1(*dense_refs)
     small_sum.second(small_sems)
-    dense_sum.middle(*dense_refs)
+    dense_sum.middle2(*dense_refs)
     small_sum.third(small_sems)
+    dense_sum.middle3(*dense_refs)
     trade.wait(grad_s, traded_out, trade_sems)
     small_sum.last(small_sems, small_out)
     dense_sum.wait(*dense_refs)
@@ -1270,7 +1405,8 @@
     vmem = pl.BlockSpec(memory_space=pltpu.VMEM)
     hbm = pl.BlockSpec(memory_space=pl.ANY)
     shape = jax.ShapeDtypeStruct
-    dense = shape((width // 2, 2 * qw + 2 * kw), bf16)
+    groups = lax.axis_size("dp")
+    dense = shape((*factors(groups), width // 2 // groups, 2 * qw + 2 * kw), bf16)
     if ending:
         depth = 2 * (-(-(ending[0].shape[0] + 2) // 8) * 8)
         last = (DenseSum(dense, layer), SmallSum(depth, width), Trade((rows, width)))
@@ -1299,7 +1435,7 @@
             pltpu.VMEM((2 * tokens, width // 2), bf16),
             pltpu.VMEM((width // 2, 2 * tokens), bf16),
             pltpu.VMEM((2 * tokens, qw), bf16),
-            pltpu.VMEM((width // 2, 2 * qw + 2 * kw), bf16),
+            pltpu.VMEM(dense.shape, bf16),
             pltpu.SemaphoreType.DMA((3, count - 1)),
             pltpu.SemaphoreType.DMA((3, count - 1)),
             pltpu.SemaphoreType.DMA((4,)),
@@ -1373,10 +1509,11 @@
         first_wide = jnp.sum(jnp.where(dealt_wide == tall, order_tall, 0.0), axis=0, keepdims=True)
         earlier = jnp.where(first_wide < first, 1.0, 0.0).astype(bf16)
         experts = picked.shape[2]
-        index = lax.broadcasted_iota(jnp.int32, (tokens, experts), 1)
-        chosen = jnp.zeros((tokens, experts), f32)
-        for k in range(route_rows.shape[1]):
-            chosen = jnp.where(route_rows[:, k : k + 1] == index, 1.0, chosen)
+        index = lax.broadcasted_iota(jnp.int32, (experts, tokens), 0)
+        chosen = jnp.zeros((experts, tokens), f32)
+        for k in range(route_rows.shape[0]):
+            chosen = jnp.where(route_rows[k : k + 1] == index, 1.0, chosen)
+        chosen = chosen.T
         rank = dot(earlier, chosen.astype(bf16), NN)
         return chosen, jnp.where(rank < CAP, chosen, 0.0)
 
@@ -1453,7 +1590,7 @@
 def assemble(parts, denses, qw, kw):
     groups = parts[0][0].shape[2]
     hidden_width = parts[0][2].shape[3]
-    dense = [v.reshape(-1, v.shape[3]) for v in denses]
+    dense = [v.reshape(-1, v.shape[-1]) for v in denses]
     depth = dense[0].shape[0]
     rows = depth // groups
 
@@ -1492,7 +1629,7 @@
                 pl.BlockSpec((1, hidden_width, depth), lambda e, s: (e, 0, 0)),
             ),
         ),
-        compiler_params=pltpu.CompilerParams(vmem_limit_bytes=48 * 2**20),
+        compiler_params=pltpu.CompilerParams(vmem_limit_bytes=58 * 2**20),
     )(lax.axis_index("section").astype(jnp.int32)[None], *parts[0], *parts[1], *dense)
 
 
@@ -1505,8 +1642,9 @@
     qw, kw = query_weight.shape[2], key_weight.shape[2]
     own = (query_weight[0], key_weight[0], value_weight[0], output_weight[0], gate_weight[0],
            up_weight[0], down_weight[0])
-    tables, masks, gains = prepare(lengths[:, 0], dealing[:, 0], slot_order[0], routes[0], attn_gain,
-                                   expert_gain, router_weight[0])
+    tables, masks, gains = prepare(lengths[:, 0], dealing[:, 0], slot_order[0],
+                                   jnp.swapaxes(routes[0], 1, 2), attn_gain, expert_gain,
+                                   router_weight[0].T)
     (out0, *state0), other = layer_forward(0, gains, own, None, tokens_in, tables, masks)
     (out1, *state1), _ = layer_forward(1, gains, own, other, out0, tables, masks)
     saved = (state0, state1)
@@ -1526,19 +1664,21 @@
             (ai, attended), tables, ending, Beside(jobs)
         )
 
-    (mid_grad, router1, gain1, pair, down, layer_outputs), _ = experts(1, out_cotangent, (out0, out1), [])
-    (grad1, attn_gain1, dense1), sums = attention(
-        1, mid_grad, (), [FirstStage(pair, 1), FirstStage(down, 2)]
+    def bring(layer, sums):
+        return [Bring(layer, kind, v) for kind, v in zip(("column", "row"), sums)]
+
+    (mid_grad, router1, gain1, pair, layer_outputs), down1, _ = experts(
+        1, out_cotangent, (out0, out1), []
     )
-    jobs = [Bring(1, kind, v) for stage in sums for kind, v in zip(("column", "row"), stage)]
-    (mid_grad, router0, gain0, pair, down), (*parts1, dense1) = experts(
-        0, grad1, (), jobs + [DenseSum(dense1, 1)]
+    (grad1, attn_gain1, dense1), (sums,) = attention(1, mid_grad, (), [FirstStage(pair, 1)])
+    (mid_grad, router0, gain0, pair), sums0, (*pair1, dense1) = experts(
+        0, grad1, (), bring(1, sums) + [DenseSum(dense1, 1)]
     )
-    (input_grads, small, dense0), parts0 = attention(
+    (input_grads, small, dense0), (pair0, *down0) = attention(
         0, mid_grad, (router0, gain0, router1, attn_gain1, gain1, grad1),
-        [FirstStage(pair, 1, 0), FirstStage(down, 2, 0)]
+        [FirstStage(pair, 1, 0), *bring(0, sums0)]
     )
-    parts0 = [v for stage in parts0 for v in stage]
+    parts0, parts1 = [*pair0, *down0], [*pair1, *down1]
     query, key, value, output, gate, up, down = assemble((parts0, parts1), (dense0, dense1), qw, kw)
     small = jnp.where(first, small[: small.shape[0] // 2], small[small.shape[0] // 2 :])
     router_grad, attn_gain_grad, expert_gain_grad = small[:E].T, small[E : E + 1], small[E + 1 : E + 2]

time: 511 us -> 463 us (0.906)
  Pallas kernels: 500 us -> 458 us
  local copies, waits for them, and re-layouts: 9.71 us -> 3.62 us
    pallas_call x2, Pallas kernels: 186 us -> 149 us  [attention_back(): pl.pallas_call(functools.partial(attention_back_kernel, layer, count, las...]
    unnamed x16 -> x8, local copies, waits for them, and re-layouts: 7.85 us -> 1.77 us
where the time goes in v5:
time: 463 us
  Pallas kernels  458 us (99%)
    pallas_call x2, Pallas kernels, layer_forward(): pl.pallas_call(functools.partial(forward_kernel, layer, count, swap), nam...  153 us
    pallas_call x2, Pallas kernels, attention_back(): pl.pallas_call(functools.partial(attention_back_kernel, layer, count, las...  149 us
    pallas_call x2, Pallas kernels, experts_back(): pl.pallas_call(functools.partial(experts_back_kernel, layer, count, trade...  142 us
    pallas_call x1, Pallas kernels, assemble(): pl.pallas_call(assemble_kernel, name='assemble', out_shape=(shape((depth,...  11.4 us

profile of v5, /device:TPU:0, one launch (start us, length us, event | category | flops | bytes accessed | tf_op | source)
XLA Modules:
  0.0 462.7 jit_solution(17108087543691294418)
XLA Ops:
  0.7 0.6 broadcast_in_dim_tile.3.freqs
  1.3 3.5 prepare.1
  4.8 78.1 %layer_forward_0.1 = (f32[64,1536]{1,0:T(8,128)}, f32[64,1536]{1,0:T(8,128)}, bf16[64,1536]{1,0:T(8,128)(2,1)}, bf16[1536,64]{1,0:T(8,128)(2,1)}, bf16[256,128]{...) custom-call(bf16[2,64,1536]{2,1,0:T(8,128)(2,1)} %refs_1_.1, ...), custom_call_target="tpu_custom_call" | custom-call | tf_op jit(solution)/shard_map/layer_forward_0/pallas_call | solution.py:940
  82.9 74.9 %layer_forward_1.1 = (f32[64,1536]{1,0:T(8,128)}, f32[64,1536]{1,0:T(8,128)}, bf16[64,1536]{1,0:T(8,128)(2,1)}, bf16[1536,64]{1,0:T(8,128)(2,1)}, bf16[256,128]{...) custom-call(f32[64,1536]{1,0:T(8,128)} %get-tuple-element.96.refs_0_, ...), custom_call_target="tpu_custom_call" | custom-call | tf_op jit(solution)/shard_map/layer_forward_1/pallas_call | solution.py:940
  157.8 74.2 %experts_back_1.1 = (f32[64,1536]{1,0:T(8,128)}, f32[16,1536]{1,0:T(8,128)}, f32[1,1536]{1,0:T(1,128)}, bf16[16,768,256]{2,1,0:T(8,128)(2,1)}, f32[2,64,1536]{2,...) custom-call(bf16[2,64,1536]{2,1,0:T(8,128)(2,1)} %refs_0_.3, ...), custom_call_target="tpu_custom_call" | custom-call | tf_op jit(solution)/shard_map/experts_back_1/pallas_call | solution.py:1196
  231.9 46.9 %attention_back_1.1 = (f32[64,1536]{1,0:T(8,128)}, f32[1,1536]{1,0:T(1,128)}, bf16[2,2,192,1024]{3,2,1,0:T(8,128)(2,1)}, bf16[2,4,384,256]{3,2,1,0:T(8,128)(2,1)}, bf16[2,4,384,256]{3,2,1,0:T(8,128)(2,1)}) custom-call(f32[64,1536]{1,0:T(8,128)} %get-tuple-element.112.refs_0_, f32[64,1536]{1,0:T(8,128)} %get-tuple-element.96.refs_0_.refs_16_.refs_1_, ...), custom_call_target="tpu_custom_call" | custom-call | tf_op jit(solution)/shard_map/attention_back_1/pallas_call | solution.py:1418
  278.9 67.7 %experts_back_0.1 = (f32[64,1536]{1,0:T(8,128)}, f32[16,1536]{1,0:T(8,128)}, f32[1,1536]{1,0:T(1,128)}, bf16[16,768,256]{2,1,0:T(8,128)(2,1)}, bf16[2,4,128,384]...) custom-call(f32[64,1536]{1,0:T(8,128)} %get-tuple-element.120.refs_0, ...), custom_call_target="tpu_custom_call" | custom-call | tf_op jit(solution)/shard_map/experts_back_0/pallas_call | solution.py:1196
  346.6 101.6 %attention_back_0.1 = (f32[2,64,1536]{2,1,0:T(8,128)}, f32[48,1536]{1,0:T(8,128)}, bf16[2,2,2,192,1024]{4,3,2,1,0:T(8,128)(2,1)}, bf16[2,2,4,384,256]{4,3,2,1,0:...) custom-call(f32[64,1536]{1,0:T(8,128)} %get-tuple-element.130.refs_0, ...), custom_call_target="tpu_custom_call" | custom-call | tf_op jit(solution)/shard_map/attention_back_0/pallas_call | solution.py:1418
  448.2 0.0 copy-start.2
  448.2 0.0 copy-start
  448.2 0.0 copy-start.1
  448.2 11.4 %assemble.1 = (f32[1536,384]{1,0:T(8,128)}, f32[1536,128]{1,0:T(8,128)}, f32[1536,128]{1,0:T(8,128)}, f32[384,1536]{1,0:T(8,128)}, f32[4,1536,128]{2,1,0:T(8,128...) custom-call(s32[1]{0:T(128)} %bitcast.18.section, bf16[2,2,4,384,256]{4,3,2,1,0:T(8,128)(2,1)} %get-tuple-element.147.refs_0_, ...), custom_call_target="tpu_custom_call" | custom-call | tf_op jit(solution)/shard_map/assemble/pallas_call | solution.py:1605
  459.6 0.0 copy-done.2
  459.7 0.6 slice_bitcast_fusion
  460.3 0.6 fusion
  460.9 0.0 copy-done
  460.9 0.9 copy.30
  461.8 0.0 copy-done.1
  461.8 0.9 copy.31
  (3 shorter events, 0.0 us)
Async XLA Ops:
  448.2 11.4 %copy-start.2 = (f32[48,1536]{1,0:T(8,128)S(1)}, f32[48,1536]{1,0:T(8,128)}, u32[]{:S(2)}) copy-start(f32[48,1536]{1,0:T(8,128)} %get-tuple-element.146) | copy-start | bytes 884740
  448.2 12.7 %copy-start = (f32[2,64,1536]{2,1,0:T(8,128)S(1)}, f32[2,64,1536]{2,1,0:T(8,128)}, u32[]{:S(2)}) copy-start(f32[2,64,1536]{2,1,0:T(8,128)} %get-tuple-element.111) | copy-start | bytes 2359300
  448.2 13.6 %copy-start.1 = (f32[2,64,1536]{2,1,0:T(8,128)S(1)}, f32[2,64,1536]{2,1,0:T(8,128)}, u32[]{:S(2)}) copy-start(f32[2,64,1536]{2,1,0:T(8,128)} %get-tuple-element.145) | copy-start | bytes 2359300

commit v6 on v5

--- a/solution.py
+++ b/solution.py
@@ -3,6 +3,7 @@
 
 import jax
 import jax.numpy as jnp
+import numpy as np
 from jax import lax
 from jax.experimental import pallas as pl
 from jax.experimental.pallas import tpu as pltpu
@@ -566,24 +567,6 @@
         return found
 
 
-def spread(count, buf, rows, sends, recvs, columns=slice(None)):
-    me = lax.axis_index("tensor")
-    own = buf.at[pl.ds(pl.multiple_of(me * rows, rows), rows), columns]
-    copies = []
-    for step in range(1, count):
-        copies.append(
-            pltpu.make_async_remote_copy(
-                src_ref=own,
-                dst_ref=own,
-                send_sem=sends.at[step - 1],
-                recv_sem=recvs.at[step - 1],
-                device_id={"tensor": lax.rem(me + step, count)},
-                device_id_type=MESH,
-            )
-        )
-    return copies
-
-
 def deal_out(count, part, rows, columns, landing, sends, recvs):
     me = lax.axis_index("tensor")
     copies = []
@@ -602,6 +585,116 @@
     for copy in copies:
         copy.start()
     return copies
+
+
+class Line:
+    def __init__(self, count, rows, passing=True):
+        self.count, self.rows = count, rows
+        self.passing = passing and count == 4
+        self.me = me = lax.axis_index("tensor")
+        half = me // 2
+        self.partner = me + 1 - 2 * lax.rem(me, 2)
+        self.far_inner, self.far_edge = 2 - half, 3 - 3 * half
+        self.inner = me == 1 + half
+
+    def cut(self, place):
+        return pl.ds(pl.multiple_of(place * self.rows, self.rows), self.rows)
+
+    def shard(self, buf, sems, place, target, index):
+        buf, columns = buf if isinstance(buf, tuple) else (buf, slice(None))
+        rows = buf.at[self.cut(place), columns]
+        return remote(rows, rows, sems[0].at[index], sems[1].at[place], {"tensor": target})
+
+    def gather_start(self, buf, sems):
+        if self.passing:
+            self.shard(buf, sems, self.me, self.far_inner, 1).start()
+            self.shard(buf, sems, self.me, self.partner, 0).start()
+        else:
+            for step in range(1, self.count):
+                self.shard(buf, sems, self.me, lax.rem(self.me + step, self.count), step - 1).start()
+
+    def gather_wait(self, buf, sems):
+        def arrived(place):
+            self.shard(buf, sems, place, self.partner, 0).wait_recv()
+
+        def left(number):
+            for index in range(number):
+                self.shard(buf, sems, self.me, self.partner, index).wait_send()
+
+        if not self.passing:
+            for step in range(1, self.count):
+                arrived(lax.rem(self.me + step, self.count))
+            left(self.count - 1)
+            return
+
+        @pl.when(self.inner)
+        def _():
+            arrived(self.far_inner)
+            self.shard(buf, sems, self.far_inner, self.partner, 2).start()
+            arrived(self.far_edge)
+            self.shard(buf, sems, self.far_edge, self.partner, 3).start()
+            arrived(self.partner)
+            left(4)
+
+        @pl.when(jnp.logical_not(self.inner))
+        def _():
+            for place in (self.partner, self.far_inner, self.far_edge):
+                arrived(place)
+            left(2)
+
+    def block(self, part, place, columns, landing, slot, sems, index, target):
+        return remote(part.at[self.cut(place), columns], landing.at[slot, :, columns],
+                      sems[0].at[index], sems[1].at[slot], {"tensor": target})
+
+    def scatter_start(self, part, columns, landing, sems):
+        if not self.passing:
+            for step in range(1, self.count):
+                peer = lax.rem(self.me + step, self.count)
+                self.block(part, peer, columns, landing, step - 1, sems, step - 1, peer).start()
+            return
+
+        @pl.when(self.inner)
+        def _():
+            self.block(part, self.partner, columns, landing, 2, sems, 0, self.partner).start()
+
+        @pl.when(jnp.logical_not(self.inner))
+        def _():
+            for slot, place in enumerate((self.far_edge, self.far_inner, self.partner)):
+                self.block(part, place, columns, landing, slot, sems, slot, self.partner).start()
+
+    def scatter_relay(self, part, columns, landing, sems):
+        if not self.passing:
+            return
+
+        @pl.when(self.inner)
+        def _():
+            for slot, place in enumerate((self.far_edge, self.far_inner)):
+                self.block(part, place, columns, landing, slot, sems, 0, self.partner).wait_recv()
+                landing[slot, :, columns] = (
+                    landing[slot, :, columns].astype(f32) + part[self.cut(place), columns].astype(f32)
+                ).astype(bf16)
+                remote(landing.at[slot, :, columns], landing.at[3, :, columns], sems[0].at[1 + slot],
+                       sems[1].at[3], {"tensor": place}).start()
+
+    def scatter_wait(self, part, columns, landing, sems):
+        slots = (2, 3) if self.passing else range(self.count - 1)
+        for slot in slots:
+            self.block(part, self.me, columns, landing, slot, sems, 0, self.partner).wait_recv()
+        for index in range(3 if self.passing else self.count - 1):
+            self.block(part, self.me, columns, landing, 0, sems, index, self.partner).wait_send()
+
+    def total(self, own, landing):
+        for slot in (2, 3) if self.passing else range(self.count - 1):
+            own = own + landing[slot].astype(f32)
+        return own
+
+    @staticmethod
+    def landing(count, rows, width):
+        return pltpu.VMEM((4 if count == 4 else count - 1, rows, width), bf16)
+
+    @staticmethod
+    def sems(count, number):
+        return [dma((number, count)), dma((number, count))]
 
 
 def core_peer():
@@ -734,6 +827,11 @@
     group = heads // key_heads
     me = lax.axis_index("tensor")
     own_rows = pl.ds(pl.multiple_of(me * rows, rows), rows)
+    ag1_line, rs1_line, ag2_line, rs2_line = [Line(count, rows, v) for v in (True, True, False, True)]
+
+    def sems(index):
+        return send_s.at[index], recv_s.at[index]
+
     use_own = lax.axis_index("section") == layer
 
     def start_attn(w):
@@ -765,16 +863,15 @@
     value = stream[...].astype(bf16).astype(f32)
     ag1[own_rows, :] = (value * norm_scale(value) * attn_gain[...]).astype(bf16)
     greet(tensor_peers(count) + ([core_peer()] if swap else []))
-    first = spread(count, ag1, rows, send_s.at[0], recv_s.at[0])
     if swap:
-        lead = min(2, experts)
+        lead = min(4, experts)
         for piece in range(4):
             swap_copies(own, other, swap_sems, piece).start()
         each_expert(lambda expert: [c.start() for c in swap_expert(expert)] and None)
 
         @pl.when(use_own)
         def _():
-            start_all(first)
+            ag1_line.gather_start(ag1, sems(0))
             start_attn(own)
             each_expert(lambda expert: start_expert(own, expert))
 
@@ -787,12 +884,12 @@
                 for copy in swap_expert(expert):
                     copy.wait_recv()
                 start_expert(other, expert)
-            start_all(first)
+            ag1_line.gather_start(ag1, sems(0))
     else:
-        start_all(first)
+        ag1_line.gather_start(ag1, sems(0))
         either(use_own, own, other, start_attn)
         either(use_own, own, other, lambda w: each_expert(lambda expert: start_expert(w, expert)))
-    wait_all(first)
+    ag1_line.gather_wait(ag1, sems(0))
     saved = [pltpu.make_async_copy(ag1, attn_in_out, save_sems.at[0])]
     saved[0].start()
     either(use_own, own, other, wait_attn)
@@ -826,40 +923,40 @@
     saved.append(pltpu.make_async_copy(attended_s, attended_out, save_sems.at[1]))
     saved[1].start()
     part[...] = dot(attended_s[...], output_s[...], NN).astype(bf16)
-    dealt = deal_out(count, part, rows, slice(None), landing1, send_s.at[1], recv_s.at[1])
-    wait_all(dealt)
-    mid = value + part[own_rows, :].astype(f32)
-    for step in range(count - 1):
-        mid = mid + landing1[step].astype(f32)
+    dealt = part, slice(None), landing1, sems(1)
+    rs1_line.scatter_start(*dealt)
+    rs1_line.scatter_relay(*dealt)
+    rs1_line.scatter_wait(*dealt)
+    mid = rs1_line.total(value + part[own_rows, :].astype(f32), landing1)
     mid_out[...] = mid
     expert_rows = (mid * norm_scale(mid) * expert_gain[...]).astype(bf16)
     expert_rows_out[...] = expert_rows
     ag2[own_rows, :] = expert_rows
     split = width // 2
     columns = pl.ds(0, split), pl.ds(split, split)
-    early, late = [
-        spread(count, ag2, rows, send_s.at[index], recv_s.at[index], lanes)
-        for index, lanes in zip((2, 7), columns)
-    ]
-    start_all(early)
-    start_all(late)
-    wait_all(early)
+    ag2_line.gather_start((ag2, columns[0]), sems(2))
+    ag2_line.gather_start((ag2, columns[1]), sems(8))
+    if swap:
+
+        @pl.when(jnp.logical_not(use_own))
+        def _():
+            def landed(expert, carry):
+                for copy in swap_expert(expert):
+                    copy.wait_recv()
+                start_expert(other, expert)
+                return carry
+
+            lax.fori_loop(lead, experts, landed, 0)
+
+    ag2_line.gather_wait((ag2, columns[0]), sems(2))
 
     def first_step(expert, carry):
-        if swap:
-
-            @pl.when(jnp.logical_not(use_own) & (expert + lead < experts))
-            def _():
-                for copy in swap_expert(expert + lead):
-                    copy.wait_recv()
-                start_expert(other, expert + lead)
-
         either(use_own, own, other, lambda w: wait_expert(w, expert))
         pre_s[expert] = dot(ag2[:, columns[0]], gu_s[expert, columns[0], :], NN)
         return carry
 
     lax.fori_loop(0, experts, first_step, 0)
-    wait_all(late)
+    ag2_line.gather_wait((ag2, columns[1]), sems(8))
     saved.append(pltpu.make_async_copy(ag2, expert_in_out, save_sems.at[2]))
     saved[2].start()
     logits = dot(ag2[...], router[...], NT)
@@ -883,16 +980,16 @@
     lax.fori_loop(0, experts, expert_step, 0)
     saved.append(pltpu.make_async_copy(gated_s, gated_out, save_sems.at[3]))
     saved[3].start()
-    copies = []
     tile = width // 4
-    for t in range(4):
-        columns = pl.ds(t * tile, tile)
-        part[:, columns] = dot(gated_s[...], down_s[:, columns], NN).astype(bf16)
-        copies += deal_out(count, part, rows, columns, landing2, send_s.at[3 + t], recv_s.at[3 + t])
-    wait_all(copies)
-    total = mid_out[...] + part[own_rows, :].astype(f32)
-    for step in range(count - 1):
-        total = total + landing2[step].astype(f32)
+    dealt = [(part, pl.ds(t * tile, tile), landing2, sems(3 + t)) for t in range(4)]
+    for each in dealt:
+        part[:, each[1]] = dot(gated_s[...], down_s[:, each[1]], NN).astype(bf16)
+        rs2_line.scatter_start(*each)
+    for each in dealt:
+        rs2_line.scatter_relay(*each)
+    for each in dealt:
+        rs2_line.scatter_wait(*each)
+    total = rs2_line.total(mid_out[...] + part[own_rows, :].astype(f32), landing2)
     out[...] = total
     wait_all(saved)
     if swap:
@@ -963,13 +1060,12 @@
             pltpu.VMEM((tokens, width), bf16),
             pltpu.VMEM((tokens, width), bf16),
             pltpu.VMEM((tokens, width), bf16),
-            pltpu.VMEM((count - 1, rows, width), bf16),
-            pltpu.VMEM((count - 1, rows, width), bf16),
+            Line.landing(count, rows, width),
+            Line.landing(count, rows, width),
             pltpu.VMEM((experts, tokens, 2 * hidden_width), f32),
             pltpu.VMEM((tokens, experts * hidden_width), bf16),
             pltpu.VMEM((tokens, qw), bf16),
-            dma((8, count - 1)),
-            dma((8, count - 1)),
+            *Line.sems(count, 9),
             dma((4,)),
             dma((3, experts)),
             dma((experts,)),
@@ -1023,6 +1119,9 @@
     hidden_width = gu_s.shape[2] // 2
     me = lax.axis_index("tensor")
     own_rows = pl.ds(pl.multiple_of(me * rows, rows), rows)
+    ag_line, rs_line = [Line(count, rows, v) for v in (False, False)]
+    gathering = ag1, (send_s.at[0], recv_s.at[0])
+    dealt = part, slice(None), landing1, (send_s.at[1], recv_s.at[1])
     use_own = lax.axis_index("section") == layer
 
     def start_expert(expert, carry):
@@ -1035,13 +1134,11 @@
     if layer:
         ag1[own_rows, :] = out_grad[lax.axis_index("section")]
         greet(tensor_peers(count) + [core_peer()] + everyone.peers())
-        first = spread(count, ag1, rows, send_s.at[0], recv_s.at[0])
-        start_all(first)
+        ag_line.gather_start(*gathering)
     else:
         ag1[own_rows, :] = out_grad[...].astype(bf16)
         greet(tensor_peers(count) + [core_peer()] + everyone.peers())
-        first = spread(count, ag1, rows, send_s.at[0], recv_s.at[0])
-        start_all(first)
+        ag_line.gather_start(*gathering)
     lax.fori_loop(0, experts, start_expert, 0)
     loads = hand_halves(x_in, x_s, [v.at[0] for v in (local_sems, hand_send, hand_recv)])
     loads += hand_rows(gated_in, gated_s, [v.at[1] for v in (local_sems, hand_send, hand_recv)])
@@ -1067,7 +1164,7 @@
         return carry
 
     lax.fori_loop(0, experts, ready_step, 0)
-    wait_all(first)
+    ag_line.gather_wait(*gathering)
     core = lax.axis_index("section")
     half = width // 2
     og_s[pl.ds(0, tokens), :] = ag1[:, pl.ds(pl.multiple_of(core * half, half), half)]
@@ -1126,8 +1223,9 @@
     handed.append(remote(gpu_s, gpu_peer, core_send.at[1], core_recv.at[1], core_peer()))
     handed[1].start()
     part[...] = acc[...].astype(bf16)
-    copies = deal_out(count, part, rows, slice(None), landing1, send_s.at[1], recv_s.at[1])
-    copies += deal_out(count, gate_part, rows, slice(None), gate_land, send_s.at[2], recv_s.at[2])
+    rs_line.scatter_start(*dealt)
+    copies = deal_out(count, gate_part, rows, slice(None), gate_land, send_s.at[2], recv_s.at[2])
+    rs_line.scatter_relay(*dealt)
     beside.middle(*beside_refs, step="middle2")
     turned_x[...] = x_s[...].T
     wait_all(handed[1:])
@@ -1146,13 +1244,12 @@
 
     lax.fori_loop(0, experts, grads_step, 0)
     beside.middle(*beside_refs, step="middle3")
-    if layer:
-        stage.middle(*stage_refs)
+    stage.middle(*stage_refs)
     wait_all(copies)
-    in_grad = acc[own_rows, :]
+    rs_line.scatter_wait(*dealt)
+    in_grad = rs_line.total(acc[own_rows, :], landing1)
     gate_grad = gate_part[own_rows, :]
     for step in range(count - 1):
-        in_grad = in_grad + landing1[step].astype(f32)
         gate_grad = gate_grad + gate_land[step]
     gate_grad = gate_grad[:, :experts]
     gate_rows = gate[own_rows, :]
@@ -1173,8 +1270,6 @@
     lax.fori_loop(0, experts, finish_save, 0)
     if trade:
         trade.wait(traded[0], traded_out[0], trade_sems)
-    if not layer:
-        stage.middle(*stage_refs)
     stage.wait(*stage_refs)
     beside.wait(*beside_refs)
 
@@ -1214,7 +1309,7 @@
             pltpu.VMEM((experts * hidden_width, depth), bf16),
             pltpu.VMEM((tokens, width), bf16),
             pltpu.VMEM((tokens, width), bf16),
-            pltpu.VMEM((count - 1, rows, width), bf16),
+            Line.landing(count, rows, width),
             pltpu.VMEM((experts, tokens, 2 * hidden_width), f32),
             pltpu.VMEM((experts, tokens, 2 * hidden_width), bf16),
             pltpu.VMEM((tokens, width), f32),
@@ -1228,8 +1323,7 @@
             pltpu.VMEM((experts, tokens, hidden_width), bf16),
             pltpu.VMEM((experts, width // 2, 2 * hidden_width), bf16),
             pltpu.VMEM(stage.blocks, bf16),
-            pltpu.SemaphoreType.DMA((3, count - 1)),
-            pltpu.SemaphoreType.DMA((3, count - 1)),
+            *Line.sems(count, 3),
             pltpu.SemaphoreType.DMA((3, experts)),
             pltpu.SemaphoreType.DMA((experts,)),
             *[pltpu.SemaphoreType.DMA((3,)) for _ in range(5)],
@@ -1286,12 +1380,13 @@
     group = heads // key_heads
     me = lax.axis_index("tensor")
     own_rows = pl.ds(pl.multiple_of(me * rows, rows), rows)
+    ag_line, rs_line = [Line(count, rows, v) for v in (True, False)]
+    gathering = ag2, (send_s.at[0], recv_s.at[0])
     use_own = lax.axis_index("section") == layer
     ag2[own_rows, :] = mid_grad[...].astype(bf16)
     everyone = Beside([*beside.jobs, dense_sum]) if last else beside
     greet(tensor_peers(count) + [core_peer()] + (whole_group() if last else everyone.peers()))
-    first = spread(count, ag2, rows, send_s.at[0], recv_s.at[0])
-    start_all(first)
+    ag_line.gather_start(*gathering)
     either(use_own, own, other, lambda w: [c.start() for c in attn_copies(w, scratch, attn_sems)])
     loads = hand_halves(ai_in, ai_s, [v.at[0] for v in (local_sems, hand_send, hand_recv)])
     loads += hand_rows(attended_in, attended_s, [v.at[1] for v in (local_sems, hand_send, hand_recv)])
@@ -1300,7 +1395,7 @@
     beside.start(*beside_refs)
     wait_all(loads)
     turned_ai[...] = ai_s[...].T
-    wait_all(first)
+    ag_line.gather_wait(*gathering)
     core = lax.axis_index("section")
     half = width // 2
     ao_s[pl.ds(0, tokens), :] = ag2[:, pl.ds(pl.multiple_of(core * half, half), half)]
@@ -1332,12 +1427,15 @@
         joint_rows[:, lanes] = (block * cosine[...] - turned(block) * sine[...]).astype(bf16)
     handed.append(remote(joint_rows, joint_peer, core_send.at[1], core_recv.at[1], core_peer()))
     handed[1].start()
-    copies = []
     tile = width // 2
-    for t in range(2):
-        columns = pl.ds(t * tile, tile)
-        part[:, columns] = dot(joint_rows[...], joint_s[columns, :], NT).astype(bf16)
-        copies += deal_out(count, part, rows, columns, landing2, send_s.at[1 + t], recv_s.at[1 + t])
+    dealt = [
+        (part, pl.ds(t * tile, tile), landing2, (send_s.at[1 + t], recv_s.at[1 + t])) for t in range(2)
+    ]
+    for each in dealt:
+        part[:, each[1]] = dot(joint_rows[...], joint_s[each[1], :], NT).astype(bf16)
+        rs_line.scatter_start(*each)
+    for each in dealt:
+        rs_line.scatter_relay(*each)
     wait_all(handed)
     wide = qw + 2 * kw
     joint_grads = (
@@ -1354,10 +1452,9 @@
     else:
         save = pltpu.make_async_copy(dense_s, dense_out, local_sems.at[0])
         save.start()
-    wait_all(copies)
-    in_grad = part[own_rows, :].astype(f32)
-    for step in range(count - 1):
-        in_grad = in_grad + landing2[step].astype(f32)
+    for each in dealt:
+        rs_line.scatter_wait(*each)
+    in_grad = rs_line.total(part[own_rows, :].astype(f32), landing2)
     stream_part, attn_gain_grad = norm_back(
         stream[...].astype(bf16).astype(f32), attn_gain[...], in_grad
     )
@@ -1426,7 +1523,7 @@
             pltpu.VMEM((qw, width), bf16),
             pltpu.VMEM((tokens, width), bf16),
             pltpu.VMEM((tokens, width), bf16),
-            pltpu.VMEM((count - 1, rows, width), bf16),
+            Line.landing(count, rows, width),
             pltpu.VMEM((heads * tokens, HD), bf16),
             pltpu.VMEM((tokens, qw + kw), f32),
             pltpu.VMEM((tokens, qw + 2 * kw), bf16),
@@ -1436,8 +1533,7 @@
             pltpu.VMEM((width // 2, 2 * tokens), bf16),
             pltpu.VMEM((2 * tokens, qw), bf16),
             pltpu.VMEM(dense.shape, bf16),
-            pltpu.SemaphoreType.DMA((3, count - 1)),
-            pltpu.SemaphoreType.DMA((3, count - 1)),
+            *Line.sems(count, 3),
             pltpu.SemaphoreType.DMA((4,)),
             *[pltpu.SemaphoreType.DMA((2,)) for _ in range(5)],
             *more,
@@ -1526,7 +1622,7 @@
     tokens = order.shape[2]
     width = attn_gain.shape[1]
     half = HD // 2
-    freqs = jnp.tile(rope_base ** (-2.0 * jnp.arange(half, dtype=f32) / HD), 128 // half)[None]
+    freqs = np.tile(rope_base ** (-2.0 * np.arange(half) / HD), 128 // half)[None].astype(np.float32)
     vmem = pl.BlockSpec(memory_space=pltpu.VMEM)
     smem = pl.BlockSpec(memory_space=pltpu.SMEM)
     shape = jax.ShapeDtypeStruct
@@ -1557,8 +1653,10 @@
 
 
 def assemble_kernel(section, *refs):
-    expert_refs, dense_refs, outs = (refs[:4], refs[4:8]), refs[8:10], refs[10:]
-    query, key, value, output, gate, up, down = outs
+    expert_refs, dense_refs, rows_in, outs = (refs[:4], refs[4:8]), refs[8:10], refs[10:12], refs[12:]
+    query, key, value, output, gate, up, down = outs[:7]
+    for source, target in zip(rows_in, outs[7:]):
+        target[...] = source[...]
     hidden_width = gate.shape[2]
     qw, kw = query.shape[1], key.shape[1]
 
@@ -1587,7 +1685,7 @@
     pl.when(section[0] == 1)(lambda: write(expert_refs[1], dense_refs[1]))
 
 
-def assemble(parts, denses, qw, kw):
+def assemble(parts, denses, rows_in, qw, kw):
     groups = parts[0][0].shape[2]
     hidden_width = parts[0][2].shape[3]
     dense = [v.reshape(-1, v.shape[-1]) for v in denses]
@@ -1601,6 +1699,8 @@
     def dense_spec(layer, width):
         return pl.BlockSpec((rows, width), lambda e, s: (jnp.where(s[0] == layer, e, 0), 0))
 
+    _, own_rows, width = rows_in[0].shape
+    row_spec = pl.BlockSpec((2, own_rows // groups, width), lambda e, s: (0, e, 0))
     shape = jax.ShapeDtypeStruct
     return pl.pallas_call(
         assemble_kernel,
@@ -1613,12 +1713,14 @@
             shape((groups, depth, hidden_width), f32),
             shape((groups, depth, hidden_width), f32),
             shape((groups, hidden_width, depth), f32),
+            *[shape(v.shape, f32) for v in rows_in],
         ),
         grid_spec=pltpu.PrefetchScalarGridSpec(
             num_scalar_prefetch=1,
             grid=(groups,),
             in_specs=[part_spec(layer, v.shape) for layer in range(2) for v in parts[layer]]
-            + [dense_spec(layer, dense[layer].shape[1]) for layer in range(2)],
+            + [dense_spec(layer, dense[layer].shape[1]) for layer in range(2)]
+            + [row_spec] * 2,
             out_specs=(
                 pl.BlockSpec((rows, qw), lambda e, s: (e, 0)),
                 pl.BlockSpec((rows, kw), lambda e, s: (e, 0)),
@@ -1627,10 +1729,12 @@
                 pl.BlockSpec((1, depth, hidden_width), lambda e, s: (e, 0, 0)),
                 pl.BlockSpec((1, depth, hidden_width), lambda e, s: (e, 0, 0)),
                 pl.BlockSpec((1, hidden_width, depth), lambda e, s: (e, 0, 0)),
+                row_spec,
+                row_spec,
             ),
         ),
         compiler_params=pltpu.CompilerParams(vmem_limit_bytes=58 * 2**20),
-    )(lax.axis_index("section").astype(jnp.int32)[None], *parts[0], *parts[1], *dense)
+    )(lax.axis_index("section").astype(jnp.int32)[None], *parts[0], *parts[1], *dense, *rows_in)
 
 
 def shards(
@@ -1679,7 +1783,9 @@
         [FirstStage(pair, 1, 0), *bring(0, sums0)]
     )
     parts0, parts1 = [*pair0, *down0], [*pair1, *down1]
-    query, key, value, output, gate, up, down = assemble((parts0, parts1), (dense0, dense1), qw, kw)
+    query, key, value, output, gate, up, down, layer_outputs, input_grads = assemble(
+        (parts0, parts1), (dense0, dense1), (layer_outputs, input_grads), qw, kw
+    )
     small = jnp.where(first, small[: small.shape[0] // 2], small[small.shape[0] // 2 :])
     router_grad, attn_gain_grad, expert_gain_grad = small[:E].T, small[E : E + 1], small[E + 1 : E + 2]
     return (

time: 463 us -> 444 us (0.959)
  Pallas kernels: 458 us -> 442 us
    pallas_call x2, Pallas kernels: 153 us -> 136 us  [layer_forward(): pl.pallas_call(functools.partial(forward_kernel, layer, count, swap), nam...]
where the time goes in v6:
time: 444 us
  Pallas kernels  442 us (100%)
    pallas_call x2, Pallas kernels, attention_back(): pl.pallas_call(functools.partial(attention_back_kernel, layer, count, las...  150 us
    pallas_call x2, Pallas kernels, experts_back(): pl.pallas_call(functools.partial(experts_back_kernel, layer, count, trade...  140 us
    pallas_call x2, Pallas kernels, layer_forward(): pl.pallas_call(functools.partial(forward_kernel, layer, count, swap), nam...  136 us
    pallas_call x1, Pallas kernels, assemble(): pl.pallas_call(assemble_kernel, name='assemble', out_shape=(shape((depth,...  12.1 us

profile of v6, /device:TPU:0, one launch (start us, length us, event | category | flops | bytes accessed | tf_op | source)
XLA Modules:
  0.0 443.9 jit_solution(11252334997590399729)
XLA Ops:
  0.6 3.5 prepare.1
  4.2 70.3 %layer_forward_0.1 = (f32[64,1536]{1,0:T(8,128)}, f32[64,1536]{1,0:T(8,128)}, bf16[64,1536]{1,0:T(8,128)(2,1)}, bf16[1536,64]{1,0:T(8,128)(2,1)}, bf16[256,128]{...) custom-call(bf16[2,64,1536]{2,1,0:T(8,128)(2,1)} %refs_1_.1, ...), custom_call_target="tpu_custom_call" | custom-call | tf_op jit(solution)/shard_map/layer_forward_0/pallas_call | solution.py:1037
  74.5 65.8 %layer_forward_1.1 = (f32[64,1536]{1,0:T(8,128)}, f32[64,1536]{1,0:T(8,128)}, bf16[64,1536]{1,0:T(8,128)(2,1)}, bf16[1536,64]{1,0:T(8,128)(2,1)}, bf16[256,128]{...) custom-call(f32[64,1536]{1,0:T(8,128)} %get-tuple-element.98.refs_0_, ...), custom_call_target="tpu_custom_call" | custom-call | tf_op jit(solution)/shard_map/layer_forward_1/pallas_call | solution.py:1037
  140.3 73.4 %experts_back_1.1 = (f32[64,1536]{1,0:T(8,128)}, f32[16,1536]{1,0:T(8,128)}, f32[1,1536]{1,0:T(1,128)}, bf16[16,768,256]{2,1,0:T(8,128)(2,1)}, f32[2,64,1536]{2,...) custom-call(bf16[2,64,1536]{2,1,0:T(8,128)(2,1)} %refs_0_.3, ...), custom_call_target="tpu_custom_call" | custom-call | tf_op jit(solution)/shard_map/experts_back_1/pallas_call | solution.py:1291
  213.7 46.3 %attention_back_1.1 = (f32[64,1536]{1,0:T(8,128)}, f32[1,1536]{1,0:T(1,128)}, bf16[2,2,192,1024]{3,2,1,0:T(8,128)(2,1)}, bf16[2,4,384,256]{3,2,1,0:T(8,128)(2,1)}, bf16[2,4,384,256]{3,2,1,0:T(8,128)(2,1)}) custom-call(f32[64,1536]{1,0:T(8,128)} %get-tuple-element.113.refs_0_, f32[64,1536]{1,0:T(8,128)} %get-tuple-element.98.refs_0_.refs_16_.refs_1_, ...), custom_call_target="tpu_custom_call" | custom-call | tf_op jit(solution)/shard_map/attention_back_1/pallas_call | solution.py:1515
  260.0 66.5 %experts_back_0.1 = (f32[64,1536]{1,0:T(8,128)}, f32[16,1536]{1,0:T(8,128)}, f32[1,1536]{1,0:T(1,128)}, bf16[16,768,256]{2,1,0:T(8,128)(2,1)}, bf16[2,4,128,384]...) custom-call(f32[64,1536]{1,0:T(8,128)} %get-tuple-element.121.refs_0, ...), custom_call_target="tpu_custom_call" | custom-call | tf_op jit(solution)/shard_map/experts_back_0/pallas_call | solution.py:1291
  326.5 104.0 %attention_back_0.1 = (f32[2,64,1536]{2,1,0:T(8,128)}, f32[48,1536]{1,0:T(8,128)}, bf16[2,2,2,192,1024]{4,3,2,1,0:T(8,128)(2,1)}, bf16[2,2,4,384,256]{4,3,2,1,0:...) custom-call(f32[64,1536]{1,0:T(8,128)} %get-tuple-element.131.refs_0, ...), custom_call_target="tpu_custom_call" | custom-call | tf_op jit(solution)/shard_map/attention_back_0/pallas_call | solution.py:1515
  430.5 0.0 copy-start
  430.5 12.1 %assemble.1 = (f32[1536,384]{1,0:T(8,128)}, f32[1536,128]{1,0:T(8,128)}, f32[1536,128]{1,0:T(8,128)}, f32[384,1536]{1,0:T(8,128)}, f32[4,1536,128]{2,1,0:T(8,128...) custom-call(s32[1]{0:T(128)} %bitcast.section, ...), custom_call_target="tpu_custom_call" | custom-call | tf_op jit(solution)/shard_map/assemble/pallas_call | solution.py:1705
  442.6 0.0 copy-done
  442.6 0.6 slice_bitcast_fusion
  443.3 0.6 fusion
  (1 shorter events, 0.0 us)
Async XLA Ops:
  430.5 12.1 %copy-start = (f32[48,1536]{1,0:T(8,128)S(1)}, f32[48,1536]{1,0:T(8,128)}, u32[]{:S(2)}) copy-start(f32[48,1536]{1,0:T(8,128)} %get-tuple-element.160) | copy-start | bytes 884740

commit v7 on v6

--- a/solution.py
+++ b/solution.py
@@ -1121,7 +1121,13 @@
     own_rows = pl.ds(pl.multiple_of(me * rows, rows), rows)
     ag_line, rs_line = [Line(count, rows, v) for v in (False, False)]
     gathering = ag1, (send_s.at[0], recv_s.at[0])
-    dealt = part, slice(None), landing1, (send_s.at[1], recv_s.at[1])
+    tile = width // 2
+    dealt = [
+        (part, pl.ds(t * tile, tile), landing1, (send_s.at[3 * t], recv_s.at[3 * t]))
+        if t
+        else (part, pl.ds(0, tile), landing1, (send_s.at[1], recv_s.at[1]))
+        for t in range(2)
+    ]
     use_own = lax.axis_index("section") == layer
 
     def start_expert(expert, carry):
@@ -1206,26 +1212,27 @@
             gate_part[...] += jnp.where(lane == expert, summed, 0.0)
             for cut in (pl.ds(0, hidden_width), pl.ds(hidden_width, hidden_width)):
                 gpu_s[expert, :, cut] = (value * pre_s[expert, :, cut]).astype(bf16)
-        back = dot(gpu_s[pair[0]], gu_s[pair[0]], NT) + dot(gpu_s[pair[1]], gu_s[pair[1]], NT)
-
-        @pl.when(index == 0)
-        def _():
-            acc[...] = back
-
-        @pl.when(index > 0)
-        def _():
-            acc[...] += back
-
         return carry
 
     lax.fori_loop(0, experts // 2, expert_step, 0)
     gate_part[:, :experts] = gate_part[:, :experts] * kept[...]
+    copies = deal_out(count, gate_part, rows, slice(None), gate_land, send_s.at[2], recv_s.at[2])
     handed.append(remote(gpu_s, gpu_peer, core_send.at[1], core_recv.at[1], core_peer()))
     handed[1].start()
-    part[...] = acc[...].astype(bf16)
-    rs_line.scatter_start(*dealt)
-    copies = deal_out(count, gate_part, rows, slice(None), gate_land, send_s.at[2], recv_s.at[2])
-    rs_line.scatter_relay(*dealt)
+    for each in dealt:
+        columns = each[1]
+        acc[...] = jnp.zeros_like(acc)
+
+        def back_step(index, carry, columns=columns):
+            pair = (2 * index, 2 * index + 1)
+            acc[...] += dot(gpu_s[pair[0]], gu_s[pair[0], columns, :], NT) + dot(
+                gpu_s[pair[1]], gu_s[pair[1], columns, :], NT
+            )
+            return carry
+
+        lax.fori_loop(0, experts // 2, back_step, 0)
+        part[:, columns] = acc[...].astype(bf16)
+        rs_line.scatter_start(*each)
     beside.middle(*beside_refs, step="middle2")
     turned_x[...] = x_s[...].T
     wait_all(handed[1:])
@@ -1246,8 +1253,9 @@
     beside.middle(*beside_refs, step="middle3")
     stage.middle(*stage_refs)
     wait_all(copies)
-    rs_line.scatter_wait(*dealt)
-    in_grad = rs_line.total(acc[own_rows, :], landing1)
+    for each in dealt:
+        rs_line.scatter_wait(*each)
+    in_grad = rs_line.total(part[own_rows, :].astype(f32), landing1)
     gate_grad = gate_part[own_rows, :]
     for step in range(count - 1):
         gate_grad = gate_grad + gate_land[step]
@@ -1283,7 +1291,7 @@
     trade = Trade((rows, width)) if traded else None
     experts, depth, hidden_width = own[0].shape
     stage = FirstStage(
-        jax.ShapeDtypeStruct((experts, hidden_width, width // 2), bf16), 2, layer if layer else None
+        jax.ShapeDtypeStruct((experts, hidden_width, width // 2), bf16), 2, layer
     )
     vmem = pl.BlockSpec(memory_space=pltpu.VMEM)
     hbm = pl.BlockSpec(memory_space=pl.ANY)
@@ -1312,7 +1320,7 @@
             Line.landing(count, rows, width),
             pltpu.VMEM((experts, tokens, 2 * hidden_width), f32),
             pltpu.VMEM((experts, tokens, 2 * hidden_width), bf16),
-            pltpu.VMEM((tokens, width), f32),
+            pltpu.VMEM((tokens, width // 2), f32),
             pltpu.VMEM((tokens, 128), f32),
             pltpu.VMEM((count - 1, rows, 128), f32),
             pltpu.VMEM((2 * tokens, width // 2), bf16),
@@ -1323,7 +1331,7 @@
             pltpu.VMEM((experts, tokens, hidden_width), bf16),
             pltpu.VMEM((experts, width // 2, 2 * hidden_width), bf16),
             pltpu.VMEM(stage.blocks, bf16),
-            *Line.sems(count, 3),
+            *Line.sems(count, 4),
             pltpu.SemaphoreType.DMA((3, experts)),
             pltpu.SemaphoreType.DMA((experts,)),
             *[pltpu.SemaphoreType.DMA((3,)) for _ in range(5)],
@@ -1452,6 +1460,7 @@
     else:
         save = pltpu.make_async_copy(dense_s, dense_out, local_sems.at[0])
         save.start()
+    beside.middle(*beside_refs)
     for each in dealt:
         rs_line.scatter_wait(*each)
     in_grad = rs_line.total(part[own_rows, :].astype(f32), landing2)
@@ -1463,7 +1472,6 @@
         attn_gain_out[...] = attn_gain_grad
         grad_out[...] = grad
         save.wait()
-        beside.middle(*beside_refs)
         beside.wait(*beside_refs)
         return
     small = small_sems[0]
@@ -1479,7 +1487,6 @@
     small_sum.first(small_sems)
     grad_s[...] = grad
     trade.start(grad_s, later_grad[0], trade_sems)
-    beside.middle(*beside_refs)
     dense_sum.middle1(*dense_refs)
     small_sum.second(small_sems)
     dense_sum.middle2(*dense_refs)
@@ -1775,12 +1782,12 @@
         1, out_cotangent, (out0, out1), []
     )
     (grad1, attn_gain1, dense1), (sums,) = attention(1, mid_grad, (), [FirstStage(pair, 1)])
-    (mid_grad, router0, gain0, pair), sums0, (*pair1, dense1) = experts(
+    (mid_grad, router0, gain0, pair), down0, (*pair1, dense1) = experts(
         0, grad1, (), bring(1, sums) + [DenseSum(dense1, 1)]
     )
-    (input_grads, small, dense0), (pair0, *down0) = attention(
+    (input_grads, small, dense0), (pair0,) = attention(
         0, mid_grad, (router0, gain0, router1, attn_gain1, gain1, grad1),
-        [FirstStage(pair, 1, 0), *bring(0, sums0)]
+        [FirstStage(pair, 1, 0)]
     )
     parts0, parts1 = [*pair0, *down0], [*pair1, *down1]
     query, key, value, output, gate, up, down, layer_outputs, input_grads = assemble(

time: 444 us -> 435 us (0.980)
  Pallas kernels: 442 us -> 433 us
    pallas_call x2, Pallas kernels: 150 us -> 138 us  [attention_back(): pl.pallas_call(functools.partial(attention_back_kernel, layer, count, las...]
where the time goes in v7:
time: 435 us
  Pallas kernels  433 us (100%)
    pallas_call x2, Pallas kernels, experts_back(): pl.pallas_call(functools.partial(experts_back_kernel, layer, count, trade...  143 us
    pallas_call x2, Pallas kernels, attention_back(): pl.pallas_call(functools.partial(attention_back_kernel, layer, count, las...  138 us
    pallas_call x2, Pallas kernels, layer_forward(): pl.pallas_call(functools.partial(forward_kernel, layer, count, swap), nam...  136 us
    pallas_call x1, Pallas kernels, assemble(): pl.pallas_call(assemble_kernel, name='assemble', out_shape=(shape((depth,...  12.1 us

profile of v7, /device:TPU:0, one launch (start us, length us, event | category | flops | bytes accessed | tf_op | source)
XLA Modules:
  0.0 435.1 jit_solution(981963292432871416)
XLA Ops:
  0.6 3.6 prepare.1
  4.2 70.3 %layer_forward_0.1 = (f32[64,1536]{1,0:T(8,128)}, f32[64,1536]{1,0:T(8,128)}, bf16[64,1536]{1,0:T(8,128)(2,1)}, bf16[1536,64]{1,0:T(8,128)(2,1)}, bf16[256,128]{...) custom-call(bf16[2,64,1536]{2,1,0:T(8,128)(2,1)} %refs_1_.1, ...), custom_call_target="tpu_custom_call" | custom-call | tf_op jit(solution)/shard_map/layer_forward_0/pallas_call | solution.py:1037
  74.6 65.8 %layer_forward_1.1 = (f32[64,1536]{1,0:T(8,128)}, f32[64,1536]{1,0:T(8,128)}, bf16[64,1536]{1,0:T(8,128)(2,1)}, bf16[1536,64]{1,0:T(8,128)(2,1)}, bf16[256,128]{...) custom-call(f32[64,1536]{1,0:T(8,128)} %get-tuple-element.96.refs_0_, ...), custom_call_target="tpu_custom_call" | custom-call | tf_op jit(solution)/shard_map/layer_forward_1/pallas_call | solution.py:1037
  140.4 65.4 %experts_back_1.1 = (f32[64,1536]{1,0:T(8,128)}, f32[16,1536]{1,0:T(8,128)}, f32[1,1536]{1,0:T(1,128)}, bf16[16,768,256]{2,1,0:T(8,128)(2,1)}, f32[2,64,1536]{2,...) custom-call(bf16[2,64,1536]{2,1,0:T(8,128)(2,1)} %refs_0_.3, ...), custom_call_target="tpu_custom_call" | custom-call | tf_op jit(solution)/shard_map/experts_back_1/pallas_call | solution.py:1299
  205.8 49.8 %attention_back_1.1 = (f32[64,1536]{1,0:T(8,128)}, f32[1,1536]{1,0:T(1,128)}, bf16[2,2,192,1024]{3,2,1,0:T(8,128)(2,1)}, bf16[2,4,384,256]{3,2,1,0:T(8,128)(2,1)}, bf16[2,4,384,256]{3,2,1,0:T(8,128)(2,1)}) custom-call(f32[64,1536]{1,0:T(8,128)} %get-tuple-element.111.refs_0_, f32[64,1536]{1,0:T(8,128)} %get-tuple-element.96.refs_0_.refs_16_.refs_1_, ...), custom_call_target="tpu_custom_call" | custom-call | tf_op jit(solution)/shard_map/attention_back_1/pallas_call | solution.py:1522
  255.6 77.9 %experts_back_0.1 = (f32[64,1536]{1,0:T(8,128)}, f32[16,1536]{1,0:T(8,128)}, f32[1,1536]{1,0:T(1,128)}, bf16[16,768,256]{2,1,0:T(8,128)(2,1)}, bf16[2,2,4,128,38...) custom-call(f32[64,1536]{1,0:T(8,128)} %get-tuple-element.119.refs_0, ...), custom_call_target="tpu_custom_call" | custom-call | tf_op jit(solution)/shard_map/experts_back_0/pallas_call | solution.py:1299
  333.5 88.2 %attention_back_0.1 = (f32[2,64,1536]{2,1,0:T(8,128)}, f32[48,1536]{1,0:T(8,128)}, bf16[2,2,2,192,1024]{4,3,2,1,0:T(8,128)(2,1)}, bf16[2,2,4,384,256]{4,3,2,1,0:T(8,128)(2,1)}, bf16[2,2,4,384,256]{4,3,2,1,0:T(8,128)(2,1)}) custom-call(f32[64,1536]{1,0:T(8,128)} %get-tuple-element.129.refs_0_, bf16[2,64,1536]{2,1,0:T(8,128)(2,1)} %refs_1_.1, ...), custom_call_target="tpu_custom_call" | custom-call | tf_op jit(solution)/shard_map/attention_back_0/pallas_call | solution.py:1522
  421.7 0.0 copy-start
  421.7 12.1 %assemble.1 = (f32[1536,384]{1,0:T(8,128)}, f32[1536,128]{1,0:T(8,128)}, f32[1536,128]{1,0:T(8,128)}, f32[384,1536]{1,0:T(8,128)}, f32[4,1536,128]{2,1,0:T(8,128...) custom-call(s32[1]{0:T(128)} %bitcast.section, ...), custom_call_target="tpu_custom_call" | custom-call | tf_op jit(solution)/shard_map/assemble/pallas_call | solution.py:1712
  433.8 0.0 copy-done
  433.8 0.6 slice_bitcast_fusion
  434.5 0.6 fusion
  (1 shorter events, 0.0 us)
Async XLA Ops:
  421.7 12.1 %copy-start = (f32[48,1536]{1,0:T(8,128)S(1)}, f32[48,1536]{1,0:T(8,128)}, u32[]{:S(2)}) copy-start(f32[48,1536]{1,0:T(8,128)} %get-tuple-element.156) | copy-start | bytes 884740

commit v8 on v7

--- a/solution.py
+++ b/solution.py
@@ -256,7 +256,8 @@
 
     def middle(self, inputs, outputs, sems):
         wait_all(self.copies(inputs, sems))
-        for total, landed in ((sems[4], sems[2]), (sems[5], sems[3])):
+        going = self.onward(outputs, sems) if self.brings else self.saves(outputs, sems)
+        for index, (total, landed) in enumerate(((sems[4], sems[2]), (sems[5], sems[3]))):
             depth = total.shape[1]
 
             def add(index, carry, total=total, landed=landed, depth=depth):
@@ -268,11 +269,11 @@
                 return carry
 
             lax.fori_loop(0, total.shape[0] * depth, add, 0)
-        if self.brings:
-            for bring, *refs in self.onward(outputs, sems):
+            if self.brings:
+                bring, *refs = going[index]
                 bring.start(*refs)
-        else:
-            start_all(self.saves(outputs, sems))
+            else:
+                going[index].start()
 
     def wait(self, inputs, outputs, sems):
         if self.brings:
@@ -833,6 +834,8 @@
         return send_s.at[index], recv_s.at[index]
 
     use_own = lax.axis_index("section") == layer
+    middle = width // 2
+    gathering = [((ag1, pl.ds(0, middle)), sems(0)), ((ag1, pl.ds(middle, middle)), sems(7))]
 
     def start_attn(w):
         for copy in attn_copies(w[:4], scratch[:2], attn_sems):
@@ -871,7 +874,7 @@
 
         @pl.when(use_own)
         def _():
-            ag1_line.gather_start(ag1, sems(0))
+            [ag1_line.gather_start(*each) for each in gathering]
             start_attn(own)
             each_expert(lambda expert: start_expert(own, expert))
 
@@ -884,12 +887,13 @@
                 for copy in swap_expert(expert):
                     copy.wait_recv()
                 start_expert(other, expert)
-            ag1_line.gather_start(ag1, sems(0))
+            [ag1_line.gather_start(*each) for each in gathering]
     else:
-        ag1_line.gather_start(ag1, sems(0))
+        [ag1_line.gather_start(*each) for each in gathering]
         either(use_own, own, other, start_attn)
         either(use_own, own, other, lambda w: each_expert(lambda expert: start_expert(w, expert)))
-    ag1_line.gather_wait(ag1, sems(0))
+    for each in gathering:
+        ag1_line.gather_wait(*each)
     saved = [pltpu.make_async_copy(ag1, attn_in_out, save_sems.at[0])]
     saved[0].start()
     either(use_own, own, other, wait_attn)
@@ -922,11 +926,15 @@
             attended_s[:, pl.ds((g * group + h) * HD, HD)] = attended[h * tokens : (h + 1) * tokens]
     saved.append(pltpu.make_async_copy(attended_s, attended_out, save_sems.at[1]))
     saved[1].start()
-    part[...] = dot(attended_s[...], output_s[...], NN).astype(bf16)
-    dealt = part, slice(None), landing1, sems(1)
-    rs1_line.scatter_start(*dealt)
-    rs1_line.scatter_relay(*dealt)
-    rs1_line.scatter_wait(*dealt)
+    half = width // 2
+    dealt = [(part, pl.ds(t * half, half), landing1, sems(1 + 8 * t)) for t in range(2)]
+    for each in dealt:
+        part[:, each[1]] = dot(attended_s[...], output_s[:, each[1]], NN).astype(bf16)
+        rs1_line.scatter_start(*each)
+    for each in dealt:
+        rs1_line.scatter_relay(*each)
+    for each in dealt:
+        rs1_line.scatter_wait(*each)
     mid = rs1_line.total(value + part[own_rows, :].astype(f32), landing1)
     mid_out[...] = mid
     expert_rows = (mid * norm_scale(mid) * expert_gain[...]).astype(bf16)
@@ -1065,7 +1073,7 @@
             pltpu.VMEM((experts, tokens, 2 * hidden_width), f32),
             pltpu.VMEM((tokens, experts * hidden_width), bf16),
             pltpu.VMEM((tokens, qw), bf16),
-            *Line.sems(count, 9),
+            *Line.sems(count, 10),
             dma((4,)),
             dma((3, experts)),
             dma((experts,)),

time: 435 us -> 434 us (level)
  no operation moved by 1% of the time
where the time goes in v8:
time: 434 us
  Pallas kernels  432 us (100%)
    pallas_call x2, Pallas kernels, experts_back(): pl.pallas_call(functools.partial(experts_back_kernel, layer, count, trade...  141 us
    pallas_call x2, Pallas kernels, layer_forward(): pl.pallas_call(functools.partial(forward_kernel, layer, count, swap), nam...  138 us
    pallas_call x2, Pallas kernels, attention_back(): pl.pallas_call(functools.partial(attention_back_kernel, layer, count, las...  137 us
    pallas_call x1, Pallas kernels, assemble(): pl.pallas_call(assemble_kernel, name='assemble', out_shape=(shape((depth,...  12.1 us

profile of v8, /device:TPU:0, one launch (start us, length us, event | category | flops | bytes accessed | tf_op | source)
XLA Modules:
  0.0 433.8 jit_solution(12996862076195684627)
XLA Ops:
  0.6 3.6 prepare.1
  4.2 70.7 %layer_forward_0.1 = (f32[64,1536]{1,0:T(8,128)}, f32[64,1536]{1,0:T(8,128)}, bf16[64,1536]{1,0:T(8,128)(2,1)}, bf16[1536,64]{1,0:T(8,128)(2,1)}, bf16[256,128]{...) custom-call(bf16[2,64,1536]{2,1,0:T(8,128)(2,1)} %refs_1_.1, ...), custom_call_target="tpu_custom_call" | custom-call | tf_op jit(solution)/shard_map/layer_forward_0/pallas_call | solution.py:1045
  74.9 67.6 %layer_forward_1.1 = (f32[64,1536]{1,0:T(8,128)}, f32[64,1536]{1,0:T(8,128)}, bf16[64,1536]{1,0:T(8,128)(2,1)}, bf16[1536,64]{1,0:T(8,128)(2,1)}, bf16[256,128]{...) custom-call(f32[64,1536]{1,0:T(8,128)} %get-tuple-element.96.refs_0_, ...), custom_call_target="tpu_custom_call" | custom-call | tf_op jit(solution)/shard_map/layer_forward_1/pallas_call | solution.py:1045
  142.5 62.3 %experts_back_1.1 = (f32[64,1536]{1,0:T(8,128)}, f32[16,1536]{1,0:T(8,128)}, f32[1,1536]{1,0:T(1,128)}, bf16[16,768,256]{2,1,0:T(8,128)(2,1)}, f32[2,64,1536]{2,...) custom-call(bf16[2,64,1536]{2,1,0:T(8,128)(2,1)} %refs_0_.3, ...), custom_call_target="tpu_custom_call" | custom-call | tf_op jit(solution)/shard_map/experts_back_1/pallas_call | solution.py:1307
  204.8 49.2 %attention_back_1.1 = (f32[64,1536]{1,0:T(8,128)}, f32[1,1536]{1,0:T(1,128)}, bf16[2,2,192,1024]{3,2,1,0:T(8,128)(2,1)}, bf16[2,4,384,256]{3,2,1,0:T(8,128)(2,1)}, bf16[2,4,384,256]{3,2,1,0:T(8,128)(2,1)}) custom-call(f32[64,1536]{1,0:T(8,128)} %get-tuple-element.111.refs_0_, f32[64,1536]{1,0:T(8,128)} %get-tuple-element.96.refs_0_.refs_16_.refs_1_, ...), custom_call_target="tpu_custom_call" | custom-call | tf_op jit(solution)/shard_map/attention_back_1/pallas_call | solution.py:1530
  254.0 78.2 %experts_back_0.1 = (f32[64,1536]{1,0:T(8,128)}, f32[16,1536]{1,0:T(8,128)}, f32[1,1536]{1,0:T(1,128)}, bf16[16,768,256]{2,1,0:T(8,128)(2,1)}, bf16[2,2,4,128,38...) custom-call(f32[64,1536]{1,0:T(8,128)} %get-tuple-element.119.refs_0, ...), custom_call_target="tpu_custom_call" | custom-call | tf_op jit(solution)/shard_map/experts_back_0/pallas_call | solution.py:1307
  332.2 88.2 %attention_back_0.1 = (f32[2,64,1536]{2,1,0:T(8,128)}, f32[48,1536]{1,0:T(8,128)}, bf16[2,2,2,192,1024]{4,3,2,1,0:T(8,128)(2,1)}, bf16[2,2,4,384,256]{4,3,2,1,0:T(8,128)(2,1)}, bf16[2,2,4,384,256]{4,3,2,1,0:T(8,128)(2,1)}) custom-call(f32[64,1536]{1,0:T(8,128)} %get-tuple-element.129.refs_0_, bf16[2,64,1536]{2,1,0:T(8,128)(2,1)} %refs_1_.1, ...), custom_call_target="tpu_custom_call" | custom-call | tf_op jit(solution)/shard_map/attention_back_0/pallas_call | solution.py:1530
  420.4 0.0 copy-start
  420.4 12.1 %assemble.1 = (f32[1536,384]{1,0:T(8,128)}, f32[1536,128]{1,0:T(8,128)}, f32[1536,128]{1,0:T(8,128)}, f32[384,1536]{1,0:T(8,128)}, f32[4,1536,128]{2,1,0:T(8,128...) custom-call(s32[1]{0:T(128)} %bitcast.section, ...), custom_call_target="tpu_custom_call" | custom-call | tf_op jit(solution)/shard_map/assemble/pallas_call | solution.py:1720
  432.5 0.0 copy-done
  432.5 0.6 slice_bitcast_fusion
  433.2 0.6 fusion
  (1 shorter events, 0.0 us)
Async XLA Ops:
  420.4 12.1 %copy-start = (f32[48,1536]{1,0:T(8,128)S(1)}, f32[48,1536]{1,0:T(8,128)}, u32[]{:S(2)}) copy-start(f32[48,1536]{1,0:T(8,128)} %get-tuple-element.156) | copy-start | bytes 884740

commit v9 on v8

--- a/solution.py
+++ b/solution.py
@@ -1178,6 +1178,8 @@
         return carry
 
     lax.fori_loop(0, experts, ready_step, 0)
+    wait_all(loads)
+    turned_x[...] = x_s[...].T
     ag_line.gather_wait(*gathering)
     core = lax.axis_index("section")
     half = width // 2
@@ -1187,7 +1189,6 @@
                og_s.at[pl.ds(tokens, tokens)], core_send.at[0], core_recv.at[0], core_peer())
     ]
     handed[0].start()
-    wait_all(loads)
     handed[0].wait()
     _, inner, per_group = stage.blocks[:3]
 
@@ -1242,7 +1243,6 @@
         part[:, columns] = acc[...].astype(bf16)
         rs_line.scatter_start(*each)
     beside.middle(*beside_refs, step="middle2")
-    turned_x[...] = x_s[...].T
     wait_all(handed[1:])
 
     def saves(expert):

time: 434 us -> 434 us (level)
  no operation moved by 1% of the time
where the time goes in v9:
time: 434 us; the launch traced here: 433 us
  Pallas kernels  431 us (99%)
    pallas_call x2, Pallas kernels, experts_back(): pl.pallas_call(functools.partial(experts_back_kernel, layer, count, trade...  140 us
    pallas_call x2, Pallas kernels, layer_forward(): pl.pallas_call(functools.partial(forward_kernel, layer, count, swap), nam...  138 us
    pallas_call x2, Pallas kernels, attention_back(): pl.pallas_call(functools.partial(attention_back_kernel, layer, count, las...  137 us
    pallas_call x1, Pallas kernels, assemble(): pl.pallas_call(assemble_kernel, name='assemble', out_shape=(shape((depth,...  12.1 us

profile of v9, /device:TPU:0, one launch (start us, length us, event | category | flops | bytes accessed | tf_op | source)
XLA Modules:
  0.0 433.5 jit_solution(12771447185502326947)
XLA Ops:
  0.6 3.6 prepare.1
  4.2 70.7 %layer_forward_0.1 = (f32[64,1536]{1,0:T(8,128)}, f32[64,1536]{1,0:T(8,128)}, bf16[64,1536]{1,0:T(8,128)(2,1)}, bf16[1536,64]{1,0:T(8,128)(2,1)}, bf16[256,128]{...) custom-call(bf16[2,64,1536]{2,1,0:T(8,128)(2,1)} %refs_1_.1, ...), custom_call_target="tpu_custom_call" | custom-call | tf_op jit(solution)/shard_map/layer_forward_0/pallas_call | solution.py:1045
  74.9 67.6 %layer_forward_1.1 = (f32[64,1536]{1,0:T(8,128)}, f32[64,1536]{1,0:T(8,128)}, bf16[64,1536]{1,0:T(8,128)(2,1)}, bf16[1536,64]{1,0:T(8,128)(2,1)}, bf16[256,128]{...) custom-call(f32[64,1536]{1,0:T(8,128)} %get-tuple-element.96.refs_0_, ...), custom_call_target="tpu_custom_call" | custom-call | tf_op jit(solution)/shard_map/layer_forward_1/pallas_call | solution.py:1045
  142.5 62.3 %experts_back_1.1 = (f32[64,1536]{1,0:T(8,128)}, f32[16,1536]{1,0:T(8,128)}, f32[1,1536]{1,0:T(1,128)}, bf16[16,768,256]{2,1,0:T(8,128)(2,1)}, f32[2,64,1536]{2,...) custom-call(bf16[2,64,1536]{2,1,0:T(8,128)(2,1)} %refs_0_.3, ...), custom_call_target="tpu_custom_call" | custom-call | tf_op jit(solution)/shard_map/experts_back_1/pallas_call | solution.py:1307
  204.8 49.2 %attention_back_1.1 = (f32[64,1536]{1,0:T(8,128)}, f32[1,1536]{1,0:T(1,128)}, bf16[2,2,192,1024]{3,2,1,0:T(8,128)(2,1)}, bf16[2,4,384,256]{3,2,1,0:T(8,128)(2,1)}, bf16[2,4,384,256]{3,2,1,0:T(8,128)(2,1)}) custom-call(f32[64,1536]{1,0:T(8,128)} %get-tuple-element.111.refs_0_, f32[64,1536]{1,0:T(8,128)} %get-tuple-element.96.refs_0_.refs_16_.refs_1_, ...), custom_call_target="tpu_custom_call" | custom-call | tf_op jit(solution)/shard_map/attention_back_1/pallas_call | solution.py:1530
  254.0 77.8 %experts_back_0.1 = (f32[64,1536]{1,0:T(8,128)}, f32[16,1536]{1,0:T(8,128)}, f32[1,1536]{1,0:T(1,128)}, bf16[16,768,256]{2,1,0:T(8,128)(2,1)}, bf16[2,2,4,128,38...) custom-call(f32[64,1536]{1,0:T(8,128)} %get-tuple-element.119.refs_0, ...), custom_call_target="tpu_custom_call" | custom-call | tf_op jit(solution)/shard_map/experts_back_0/pallas_call | solution.py:1307
  331.9 88.2 %attention_back_0.1 = (f32[2,64,1536]{2,1,0:T(8,128)}, f32[48,1536]{1,0:T(8,128)}, bf16[2,2,2,192,1024]{4,3,2,1,0:T(8,128)(2,1)}, bf16[2,2,4,384,256]{4,3,2,1,0:T(8,128)(2,1)}, bf16[2,2,4,384,256]{4,3,2,1,0:T(8,128)(2,1)}) custom-call(f32[64,1536]{1,0:T(8,128)} %get-tuple-element.129.refs_0_, bf16[2,64,1536]{2,1,0:T(8,128)(2,1)} %refs_1_.1, ...), custom_call_target="tpu_custom_call" | custom-call | tf_op jit(solution)/shard_map/attention_back_0/pallas_call | solution.py:1530
  420.1 0.0 copy-start
  420.1 12.1 %assemble.1 = (f32[1536,384]{1,0:T(8,128)}, f32[1536,128]{1,0:T(8,128)}, f32[1536,128]{1,0:T(8,128)}, f32[384,1536]{1,0:T(8,128)}, f32[4,1536,128]{2,1,0:T(8,128...) custom-call(s32[1]{0:T(128)} %bitcast.section, ...), custom_call_target="tpu_custom_call" | custom-call | tf_op jit(solution)/shard_map/assemble/pallas_call | solution.py:1720
  432.2 0.0 copy-done
  432.2 0.6 slice_bitcast_fusion
  432.9 0.6 fusion
  (1 shorter events, 0.0 us)
Async XLA Ops:
  420.1 12.1 %copy-start = (f32[48,1536]{1,0:T(8,128)S(1)}, f32[48,1536]{1,0:T(8,128)}, u32[]{:S(2)}) copy-start(f32[48,1536]{1,0:T(8,128)} %get-tuple-element.156) | copy-start | bytes 884740
